TPU v7x, 32 devices: a whole 2x2x4 slice. The times are simulated.
32 devices in a mesh: groups: 2 (over x), dp: 16 (over z, y, core).
Axes of the slice: x: 2, y: 2, z: 4, core: 2. Of those that a mesh axis runs over, the one named last changes fastest.
Arguments:
- train_hidden: bfloat16 [128, 40, 14336], P(('groups', 'dp')), parts along dimension 0, may hold values from -6 to 6
- train_cot: bfloat16 [128, 40, 4096], P(('groups', 'dp')), parts along dimension 0, may hold values from -6 to 6
- query_hidden: bfloat16 [192, 16, 14336], P(('groups', 'dp')), parts along dimension 0, may hold values from -6 to 6
- query_cot: bfloat16 [192, 16, 4096], P(('groups', 'dp')), parts along dimension 0, may hold values from -6 to 6
- proj_in: bfloat16 [64, 14336], replicated, may hold values from -0.046875 to 0.046875
- proj_out: bfloat16 [64, 4096], replicated, may hold values from -0.09375 to 0.09375
- hess_inv: float32 [8192, 4096], P(('groups', 'dp')), parts along dimension 0, as said below
Outputs:
- scores: float32 [128, 96], P(('groups', 'dp')), parts along dimension 0
There are 2 independent parts, one for each index of `groups`. A program takes and returns all parts, laid end to end along the dimension named above; an argument that names none is the same for every part. Nothing has to cross between parts.
Inputs may be any that keep to these rules, and one draw needn't show every extreme that they name: hess_inv is symmetric and positive definite.
All inputs are finite; a program needn't handle non-finite values.
Results may differ from a plain program's by a relative error of at most 0.0075.
Values may be sent and summed in bfloat16 or wider, within the bound.
No kernel may reach another device: no remote copies, remote signals or barrier semaphores. Data moves between devices by JAX's collectives and lax.ppermute only.
A program may use at most 64 MiB of HBM per device.

v0:
```python
import jax
import jax.numpy as jnp
from jax import lax
from jax.sharding import PartitionSpec as P


def example_grads(hidden, cotangent, proj_in, proj_out):
    number, length, inner = hidden.shape
    outer_width = cotangent.shape[2]
    rank = proj_in.shape[0]
    inputs = jnp.dot(
        hidden.reshape(number * length, inner), proj_in.T, preferred_element_type=jnp.float32
    ).astype(jnp.bfloat16)
    outputs = jnp.dot(
        cotangent.reshape(number * length, outer_width),
        proj_out.T,
        preferred_element_type=jnp.float32,
    ).astype(jnp.bfloat16)
    inputs = inputs.reshape(number, length, rank)
    outputs = outputs.reshape(number, length, rank)
    summed = jnp.einsum("sto,sti->soi", outputs, inputs, preferred_element_type=jnp.float32) * (
        1.0 / length
    )
    return summed.astype(jnp.bfloat16).reshape(number, rank * rank)


def on_device(train_hidden, train_cot, query_hidden, query_cot, proj_in, proj_out, hess_inv):
    train_grads = example_grads(train_hidden, train_cot, proj_in, proj_out)
    query_grads = example_grads(query_hidden, query_cot, proj_in, proj_out)
    block_width = hess_inv.shape[0]
    widened = lax.all_gather(query_grads, "dp", axis=0, tiled=True).astype(jnp.float32)
    product = jnp.dot(widened, hess_inv.T, precision=lax.Precision.HIGHEST)
    joined = jnp.concatenate([product, widened], axis=1)
    precond_bf = joined[:, :block_width].astype(jnp.bfloat16)
    full_query = joined[:, block_width:]
    full_precond = lax.all_gather(precond_bf, "dp", axis=1, tiled=True)
    self_inf = jnp.sum(full_query * full_precond.astype(jnp.float32), axis=1)
    raw = jnp.dot(train_grads, full_precond.T, preferred_element_type=jnp.float32)
    return raw / jnp.sqrt(self_inf)[None, :]


def solution(mesh):
    in_specs = (
        P(("groups", "dp"), None, None),
        P(("groups", "dp"), None, None),
        P(("groups", "dp"), None, None),
        P(("groups", "dp"), None, None),
        P(),
        P(),
        P(("groups", "dp"), None),
    )
    out_specs = P(("groups", "dp"), None)
    return jax.shard_map(
        on_device, mesh=mesh, in_specs=in_specs, out_specs=out_specs, check_vma=False
    )
```

profile of v0, /device:TPU:0, one launch (start us, length us, event | category | flops | bytes accessed | tf_op | source)
XLA Modules:
  0.0 72.2 jit_solution(13150244639720208165)
XLA Ops:
  0.0 0.0 copy-start
  0.0 1.8 %convolution_convert_fusion.3 = bf16[96,64]{0,1:T(8,128)(2,1)S(1)} fusion(bf16[96,4096]{1,0:T(8,128)(2,1)} %bitcast.27, bf16[64,4096]{1,0:T(8,128)(2,1)} %param.12), kind=kOutput, calls=%fused_computation.8 | convolution fusion | flops 50337792 | bytes 1323008 | tf_op jit(solution)/shard_map/dot_general | solution.py:14
  1.8 0.1 copy.18
  1.9 0.2 copy-done
  2.2 2.6 %convolution_convert_fusion.4 = bf16[96,64]{0,1:T(8,128)(2,1)S(1)} fusion(bf16[96,14336]{1,0:T(8,128)(2,1)S(1)} %bitcast.24, bf16[64,14336]{1,0:T(8,128)(2,1)} %param.11), kind=kOutput, calls=%fused_computation.9 | convolution fusion | flops 176166912 | bytes 4599808 | tf_op jit(solution)/shard_map/dot_general | solution.py:11
  4.8 0.1 copy.19
  4.9 0.2 fusion
  5.1 0.1 reshape.43
  5.3 27.5 %all-gather = bf16[16,6,4096]{2,1,0:T(8,128)(2,1)} all-gather(bf16[1,6,4096]{2,1,0:T(8,128)(2,1)S(1)} %reshape.43), channel_id=1, replica_groups=mesh['groups'=2,'dp'=16] {'dp'}, dimensions={0}, use_global_device_ids=true | all-gather | bytes 835584 | tf_op jit(solution)/shard_map/all_gather | solution.py:31
  32.7 1.4 %reshape.44 = bf16[96,4096]{1,0:T(8,128)(2,1)S(1)} reshape(bf16[16,6,4096]{2,1,0:T(8,128)(2,1)} %all-gather) | data formatting | bytes 1572864
  34.2 4.5 %convolution_convert_fusion = bf16[96,256]{1,0:T(8,128)(2,1)S(1)} fusion(bf16[96,4096]{1,0:T(8,128)(2,1)S(1)} %reshape.44, f32[256,4096]{1,0:T(8,128)} %param.13), kind=kOutput, calls=%fused_computation.5 | convolution fusion | flops 1207984128 | bytes 5029888 | tf_op jit(solution)/shard_map/dot_general | solution.py:32
  38.7 0.0 copy-start.3
  38.7 0.0 copy-start.4
  38.7 19.7 %all_gather.7 = bf16[96,4096]{1,0:T(8,128)(2,1)S(1)} all-gather(bf16[96,256]{1,0:T(8,128)(2,1)S(1)} %convolution_convert_fusion), channel_id=1, replica_groups=mesh['groups'=2,'dp'=16] {'dp'}, dimensions={1}, use_global_device_ids=true | all-gather | bytes 835584 | tf_op jit(solution)/shard_map/all_gather | solution.py:36
  58.4 0.0 copy-start.1
  58.4 0.3 multiply_reduce_fusion
  58.7 0.6 copy-done.1
  59.3 0.0 copy-done.3
  59.3 0.0 copy-done.4
  59.3 0.6 convolution_convert_fusion.1
  59.9 0.7 copy.16
  60.6 0.0 copy-start.2
  60.6 5.2 %convolution_convert_fusion.2 = bf16[160,64]{0,1:T(8,128)(2,1)} fusion(bf16[160,14336]{1,0:T(8,128)(2,1)} %bitcast.25, bf16[64,14336]{1,0:T(8,128)(2,1)} %param.11), kind=kOutput, calls=%fused_computation.7 | convolution fusion | flops 293611520 | bytes 6443008 | tf_op jit(solution)/shard_map/dot_general | solution.py:11
  65.8 1.5 %copy.17 = bf16[160,64]{1,0:T(8,128)(2,1)} copy(bf16[160,64]{0,1:T(8,128)(2,1)} %convolution_convert_fusion.2) | data formatting | bytes 40960 | tf_op jit(solution)/shard_map/convert_element_type | solution.py:13
  67.3 1.6 %fusion.1 = bf16[4,64,64]{2,1,0:T(8,128)(2,1)} fusion(bf16[4,40,64]{2,1,0:T(8,128)(2,1)} %bitcast.28, bf16[4,40,64]{2,1,0:T(8,128)(2,1)} %bitcast.29), kind=kOutput, calls=%fused_computation.4 | convolution fusion | flops 1343488 | bytes 73728 | tf_op jit(solution)/shard_map/sto,sti->soi/dot_general | solution.py:21
  68.9 1.6 %reshape.37 = bf16[4,4096]{1,0:T(4,128)(2,1)} reshape(bf16[4,64,64]{2,1,0:T(8,128)(2,1)} %fusion.1) | data formatting | bytes 65536 | tf_op jit(solution)/shard_map/reshape | solution.py:24
  70.5 0.0 copy-done.2
  70.5 1.7 %convolution_divide_fusion = f32[4,96]{1,0:T(4,128)} fusion(bf16[4,4096]{1,0:T(4,128)(2,1)} %reshape.37, bf16[96,4096]{1,0:T(8,128)(2,1)S(1)} %copy-done.2, f32[96]{0:T(128)S(1)} %sqrt.7), kind=kOutput, calls=%fused_computation.10 | convolution fusion | flops 3146112 | bytes 821120 | tf_op jit(solution)/shard_map/dot_general | solution.py:38
  (1 shorter events, 0.0 us)
Async XLA Ops:
  0.0 2.2 %copy-start = (bf16[6,16,14336]{2,1,0:T(8,128)(2,1)S(1)}, bf16[6,16,14336]{2,1,0:T(8,128)(2,1)}, u32[]{:S(2)}) copy-start(bf16[6,16,14336]{2,1,0:T(8,128)(2,1)} %param.9) | copy-start | bytes 8257540
  38.7 20.7 %copy-start.3 = (bf16[64,4096]{1,0:T(8,128)(2,1)S(1)}, bf16[64,4096]{1,0:T(8,128)(2,1)}, u32[]{:S(2)}) copy-start(bf16[64,4096]{1,0:T(8,128)(2,1)} %param.12) | copy-start | bytes 1572868
  38.7 20.7 %copy-start.4 = (bf16[4,40,4096]{2,1,0:T(8,128)(2,1)S(1)}, bf16[4,40,4096]{2,1,0:T(8,128)(2,1)}, u32[]{:S(2)}) copy-start(bf16[4,40,4096]{2,1,0:T(8,128)(2,1)} %param.8) | copy-start | bytes 3932164
  58.4 0.9 %copy-start.1 = (bf16[96,4096]{1,0:T(8,128)(2,1)}, bf16[96,4096]{1,0:T(8,128)(2,1)S(1)}, u32[]{:S(2)}) copy-start(bf16[96,4096]{1,0:T(8,128)(2,1)S(1)} %all_gather.7) | copy-start | bytes 2359300
  60.6 9.9 %copy-start.2 = (bf16[96,4096]{1,0:T(8,128)(2,1)S(1)}, bf16[96,4096]{1,0:T(8,128)(2,1)}, u32[]{:S(2)}) copy-start(bf16[96,4096]{1,0:T(8,128)(2,1)} %copy-done.1) | copy-start | bytes 2359300
where the time goes:
time: 72.6 us; the launch traced here: 72.2 us
  blocking collectives  47.2 us (65%)
  matrix products  18.2 us (25%)
  local copies, waits for them, and re-layouts  6.38 us (9%)
    all_gather x1, blocking collectives, on_device(): lax.all_gather(query_grads, 'dp', axis=0, tiled=True).astype(jnp.float32)  27.5 us
    all_gather x1, blocking collectives, on_device(): full_precond = lax.all_gather(precond_bf, 'dp', axis=1, tiled=True)  19.7 us
    dot_general x2, matrix products, example_grads(): jnp.dot(hidden.reshape(number * length, inner), proj_in.T, preferred_elem...  7.81 us
    dot_general x1, matrix products, on_device(): product = jnp.dot(widened, hess_inv.T, precision=lax.Precision.HIGHEST)  4.48 us
    unnamed x12, local copies, waits for them, and re-layouts  2.42 us
    dot_general x2, matrix products, example_grads(): jnp.dot(cotangent.reshape(number * length, outer_width), proj_out.T, pref...  2.39 us
    dot_general x2, matrix products, example_grads(): jnp.einsum('sto,sti->soi', outputs, inputs, preferred_element_type=jnp.fl...  1.88 us
    dot_general x1, matrix products, on_device(): jnp.dot(train_grads, full_precond.T, preferred_element_type=jnp.float32)  1.65 us

commit v1 on v0

v1 whole, which is shorter than its diff:
```python
import functools

import jax
import jax.numpy as jnp
from jax import lax
from jax.experimental import pallas as pl
from jax.experimental.pallas import tpu as pltpu
from jax.sharding import PartitionSpec as P

F32, BF16 = jnp.float32, jnp.bfloat16
NT = (((1,), (1,)), ((), ()))
VMEM = pl.BlockSpec(memory_space=pltpu.VMEM)
HBM = pl.BlockSpec(memory_space=pltpu.HBM)
INNER = 4
GROUP = 256


def dot(a, b):
    return jnp.dot(a, b, preferred_element_type=F32)


def dot_nt(a, b):
    return lax.dot_general(a, b, NT, preferred_element_type=F32)


def in_hbm(x):
    return pltpu.with_memory_space_constraint(x, pltpu.HBM)


def iota(shape, dim):
    return lax.broadcasted_iota(jnp.int32, shape, dim)


def example_grads(hidden, cotangent, proj_in, proj_out):
    number, length, inner = hidden.shape
    outer_width = cotangent.shape[2]
    rank = proj_in.shape[0]
    inputs = jnp.dot(
        hidden.reshape(number * length, inner), proj_in.T, preferred_element_type=jnp.float32
    ).astype(jnp.bfloat16)
    outputs = jnp.dot(
        cotangent.reshape(number * length, outer_width),
        proj_out.T,
        preferred_element_type=jnp.float32,
    ).astype(jnp.bfloat16)
    inputs = inputs.reshape(number, length, rank)
    outputs = outputs.reshape(number, length, rank)
    summed = jnp.einsum("sto,sti->soi", outputs, inputs, preferred_element_type=jnp.float32) * (
        1.0 / length
    )
    return summed.astype(jnp.bfloat16).reshape(number, rank * rank)


def general(train_hidden, train_cot, query_hidden, query_cot, proj_in, proj_out, hess_inv):
    train_grads = example_grads(train_hidden, train_cot, proj_in, proj_out)
    query_grads = example_grads(query_hidden, query_cot, proj_in, proj_out)
    full_query = lax.all_gather(query_grads, "dp", axis=0, tiled=True).astype(jnp.float32)
    product = jnp.dot(full_query, hess_inv.T, precision=lax.Precision.HIGHEST)
    full_precond = lax.all_gather(product.astype(jnp.bfloat16), "dp", axis=1, tiled=True)
    self_inf = jnp.sum(full_query * full_precond.astype(jnp.float32), axis=1)
    raw = jnp.dot(train_grads, full_precond.T, preferred_element_type=jnp.float32)
    return raw / jnp.sqrt(self_inf)[None, :]


def project_kernel(
    planes, number, length, chunks, me_ref, th_ref, tc_ref, qh_ref, qc_ref, pi_ref, po_ref, *rest
):
    outs, (th, tc, qh, qc, pi, po, grads, sems) = rest[:planes], rest[planes:]
    inner = th.shape[1]
    width = inner // chunks
    rank = pi.shape[0]
    tokens = th.shape[0]
    queries = qh.shape[0]

    copies = {}

    def load(name, src, dst, part=None):
        if part is not None:
            cols = pl.ds(part * width, width)
            src, dst = src.at[:, cols], dst.at[:, cols]
        copies[name, part] = pltpu.make_async_copy(src, dst, sems.at[len(copies)])
        copies[name, part].start()

    load("po", po_ref, po)
    load("tc", tc_ref, tc)
    load("qc", qc_ref, qc)
    for c in range(chunks):
        load("pi", pi_ref, pi, c)
        load("th", th_ref, th, c)
        load("qh", qh_ref, qh, c)

    rows = rank // 2 * number
    copies["po", None].wait()
    copies["tc", None].wait()
    t_out = dot_nt(po[...], tc[...]).astype(BF16)
    row, col = iota((rows, tokens), 0), iota((rows, tokens), 1)
    own = row % number == col // length
    lefts = []
    for half in range(2):
        pick = iota((rows, rank), 1) == 2 * (iota((rows, rank), 0) // number) + half
        lefts.append(jnp.where(own, dot(pick.astype(BF16), t_out), 0.0).astype(BF16))
    copies["qc", None].wait()
    q_out = dot_nt(qc[...], po[...])

    t_in = jnp.zeros((tokens, rank), F32)
    q_in = jnp.zeros((queries, rank), F32)
    for c in range(chunks):
        cols = slice(c * width, (c + 1) * width)
        copies["pi", c].wait()
        copies["th", c].wait()
        t_in += dot_nt(th[:, cols], pi[:, cols])
        copies["qh", c].wait()
        q_in += dot_nt(qh[:, cols], pi[:, cols])

    spread = jnp.concatenate([t_in, t_in], axis=1).astype(BF16)
    lane = iota((tokens, 2 * rank), 1)
    total = jnp.zeros((rows, 2 * rank), F32)
    for half in range(2):
        right = jnp.where(lane // rank == half, spread, jnp.zeros_like(spread))
        total += dot(lefts[half], right)
    grads[...] = (total * (1.0 / length)).astype(BF16)
    message = jnp.concatenate([q_in, q_out], axis=1).astype(BF16)

    plane = me_ref[0] // INNER
    share = rows // planes
    for k in range(planes):
        outs[k][:queries, :] = message
        start = pl.multiple_of((plane ^ k) * share, share)
        outs[k][queries:, :] = grads[pl.ds(start, share), :]


def project(me, planes, train_hidden, train_cot, query_hidden, query_cot, proj_in, proj_out):
    number, length, inner = train_hidden.shape
    width = train_cot.shape[2]
    rank = proj_in.shape[0]
    tokens, queries = number * length, query_hidden.shape[0] * query_hidden.shape[1]
    rows = rank // 2 * number
    chunks = 4
    out = pltpu.VMEM((queries + rows // planes, 2 * rank), BF16)
    return pl.pallas_call(
        functools.partial(project_kernel, planes, number, length, chunks),
        out_shape=[out] * planes,
        in_specs=[pl.BlockSpec(memory_space=pltpu.SMEM)] + [HBM] * 6,
        out_specs=[VMEM] * planes,
        scratch_shapes=[
            pltpu.VMEM((tokens, inner), BF16),
            pltpu.VMEM((tokens, width), BF16),
            pltpu.VMEM((queries, inner), BF16),
            pltpu.VMEM((queries, width), BF16),
            pltpu.VMEM((rank, inner), BF16),
            pltpu.VMEM((rank, width), BF16),
            pltpu.VMEM((rows, 2 * rank), BF16),
            pltpu.SemaphoreType.DMA((3 * chunks + 3,)),
        ],
        compiler_params=pltpu.CompilerParams(vmem_limit_bytes=20 * 2**20),
        name="project",
    )(
        me,
        in_hbm(train_hidden.reshape(tokens, inner)),
        in_hbm(train_cot.reshape(tokens, width)),
        in_hbm(query_hidden.reshape(queries, inner)),
        in_hbm(query_cot.reshape(queries, width)),
        in_hbm(proj_in),
        in_hbm(proj_out),
    )


def split_kernel(chunks, hess_ref, after_ref, high_ref, low_ref, hess, sems):
    width = hess.shape[1] // chunks
    copies = []
    for c in range(chunks):
        cols = pl.ds(c * width, width)
        copies.append(pltpu.make_async_copy(hess_ref.at[:, cols], hess.at[:, cols], sems.at[c]))
        copies[-1].start()
    for c in range(chunks):
        copies[c].wait()
        cols = slice(c * width, (c + 1) * width)
        h = hess[:, cols]
        high = h.astype(BF16)
        high_ref[:, cols] = high
        low_ref[:, cols] = (h - high.astype(F32)).astype(BF16)


def split(hess_inv, after):
    chunks = 4
    out = pltpu.VMEM(hess_inv.shape, BF16)
    return pl.pallas_call(
        functools.partial(split_kernel, chunks),
        out_shape=[out] * 2,
        in_specs=[HBM, VMEM],
        out_specs=[VMEM] * 2,
        scratch_shapes=[
            pltpu.VMEM(hess_inv.shape, F32),
            pltpu.SemaphoreType.DMA((chunks,)),
        ],
        compiler_params=pltpu.CompilerParams(vmem_limit_bytes=20 * 2**20),
        cost_estimate=pl.CostEstimate(
            flops=3 * hess_inv.size, bytes_accessed=8 * hess_inv.size, transcendentals=0
        ),
        name="split",
    )(in_hbm(hess_inv), after)


def score_kernel(n, number, qlen, slots, me_ref, *rest):
    pieces, (high_ref, low_ref, out_ref, tok, train, grads) = rest[:-6], rest[-6:]
    me = me_ref[0]
    block, coords = high_ref.shape
    lanes = tok.shape[1]
    rank = lanes // 2
    tokens = tok.shape[0] // n
    pairs = rank // 2
    local = block // lanes
    tile = local * number
    mine = me % INNER

    slots = iter(slots)
    for piece in pieces:
        for part in range(piece.shape[0]):
            source = me ^ next(slots)
            start = pl.multiple_of(source * tokens, tokens)
            tok[pl.ds(start, tokens), :] = piece[part, :tokens, :]
            share = piece[part, tokens:, :].astype(F32)
            picked = share[:tile]
            for j in range(1, INNER):
                picked = jnp.where(mine == j, share[j * tile : (j + 1) * tile], picked)
            train[source] = picked

    group = GROUP
    per = group // qlen
    pick = (iota((rank, lanes), 1) == iota((rank, lanes), 0) + rank).astype(BF16)
    shift = (iota((lanes, lanes), 1) == iota((lanes, lanes), 0) + rank).astype(BF16)
    own = (iota((per, group), 1) // qlen == iota((per, group), 0)).astype(BF16)
    low = iota((group, lanes), 1) < rank
    for g in range(n * tokens // group):
        x = tok[g * group : (g + 1) * group, :]
        outs = dot_nt(pick, x)
        right = jnp.concatenate(
            [jnp.where(low, x, jnp.zeros_like(x)), dot(x, shift).astype(BF16)], axis=0
        )
        left = []
        for pair in range(pairs):
            left.append(
                jnp.concatenate(
                    [
                        jnp.broadcast_to(outs[o : o + 1, :], (per, group)).astype(BF16) * own
                        for o in (2 * pair, 2 * pair + 1)
                    ],
                    axis=1,
                )
            )
        made = (dot(jnp.concatenate(left, axis=0), right) * (1.0 / qlen)).astype(BF16)
        for pair in range(pairs):
            grads[g * per : (g + 1) * per, pair * lanes : (pair + 1) * lanes] = made[
                pair * per : (pair + 1) * per, :
            ]

    queries = grads.shape[0]
    precond = dot_nt(high_ref[...], grads[...]) + dot_nt(low_ref[...], grads[...])
    precond = precond.astype(BF16)

    start = pl.multiple_of(me * block, block)
    square = dot(grads[:, pl.ds(start, block)], precond)
    eye = iota((queries, queries), 0) == iota((queries, queries), 1)
    self_inf = jnp.sum(jnp.where(eye, square, 0.0), axis=0, keepdims=True)

    rows = n * tile
    t = train[...].reshape(rows, lanes)
    where = iota((rows, lanes), 0) % tile // number
    wide = jnp.concatenate(
        [jnp.where(where == j, t, 0.0).astype(BF16) for j in range(local)], axis=1
    )
    parts = dot(wide, precond)
    raw = parts
    for j in range(1, local):
        raw = raw + pltpu.roll(parts, rows - j * number, 0)
    raw = jnp.where(iota((rows, queries), 0) % tile < number, raw, self_inf)
    out_ref[...] = jnp.zeros_like(out_ref)
    out_ref[:, :queries] = raw


def score(me, n, number, qlen, slots, pieces, high, low):
    block, coords = high.shape
    lanes = pieces[0].shape[2]
    local = block // lanes
    tokens = pieces[0].shape[1] - INNER * local * number
    queries = n * tokens // qlen
    padded = -(-queries // 128) * 128
    return pl.pallas_call(
        functools.partial(score_kernel, n, number, qlen, slots),
        out_shape=pltpu.VMEM((n * local * number, padded), F32),
        in_specs=[pl.BlockSpec(memory_space=pltpu.SMEM)] + [VMEM] * (len(pieces) + 2),
        out_specs=VMEM,
        scratch_shapes=[
            pltpu.VMEM((n * tokens, lanes), BF16),
            pltpu.VMEM((n, local * number, lanes), F32),
            pltpu.VMEM((queries, coords), BF16),
        ],
        compiler_params=pltpu.CompilerParams(vmem_limit_bytes=20 * 2**20),
        name="score",
    )(me, *pieces, high, low)


def finish_kernel(number, parts_ref, out_ref):
    total = jnp.sum(parts_ref[...], axis=0)
    queries = out_ref.shape[1]
    self_inf = total[number : number + 1, :queries]
    out_ref[...] = total[:number, :queries] / jnp.sqrt(self_inf)


def swap(x, k, n):
    return lax.ppermute(x, "dp", [(i, i ^ k) for i in range(n)])


def fast(n, train_hidden, train_cot, query_hidden, query_cot, proj_in, proj_out, hess_inv):
    number, qlen = train_hidden.shape[0], query_hidden.shape[1]
    queries = n * query_hidden.shape[0]
    planes = n // INNER
    me = lax.axis_index("dp").astype(jnp.int32).reshape(1)
    messages = project(
        me, planes, train_hidden, train_cot, query_hidden, query_cot, proj_in, proj_out
    )
    high, low = split(hess_inv, messages[0])
    got = [messages[0]] + [None] * (planes - 1)
    for k in range(planes - 1, 0, -1):
        got[k] = swap(messages[k], INNER * k, n)
    slots = [INNER * k for k in range(planes)]
    mine, high, low = lax.optimization_barrier((jnp.stack(got), high, low))
    for k in (2, 1):
        mine = jnp.concatenate([mine, swap(mine, k, n)], axis=0)
        slots += [slot ^ k for slot in slots]
    parts = score(me, n, number, qlen, slots, [mine], high, low)
    parts = parts.reshape(n, -1, parts.shape[1])
    parts = lax.all_to_all(parts, "dp", 0, 0, tiled=True)
    return pl.pallas_call(
        functools.partial(finish_kernel, number),
        out_shape=jax.ShapeDtypeStruct((number, queries), F32),
        in_specs=[VMEM],
        out_specs=VMEM,
        compiler_params=pltpu.CompilerParams(vmem_limit_bytes=4 * 2**20),
        name="finish",
    )(pltpu.with_memory_space_constraint(parts, pltpu.VMEM))


def suits(n, args):
    train_hidden, _, query_hidden, _, proj_in, _, hess_inv = args
    number, qlen = train_hidden.shape[0], query_hidden.shape[1]
    tokens = query_hidden.shape[0] * qlen
    lanes = 2 * proj_in.shape[0]
    block = hess_inv.shape[0]
    planes = n // INNER
    return (
        n % INNER == 0
        and planes > 1
        and planes & (planes - 1) == 0
        and lanes == 128
        and block % lanes == 0
        and block // lanes * number == 8
        and tokens % 16 == 0
        and GROUP % (16 * qlen) == 0
        and n * tokens % GROUP == 0
    )


def on_device(n, *args):
    return fast(n, *args) if suits(n, args) else general(*args)


def solution(mesh):
    n = mesh.shape["dp"]
    in_specs = (
        P(("groups", "dp"), None, None),
        P(("groups", "dp"), None, None),
        P(("groups", "dp"), None, None),
        P(("groups", "dp"), None, None),
        P(),
        P(),
        P(("groups", "dp"), None),
    )
    out_specs = P(("groups", "dp"), None)
    return jax.shard_map(
        functools.partial(on_device, n),
        mesh=mesh,
        in_specs=in_specs,
        out_specs=out_specs,
        check_vma=False,
    )
```

time: 72.6 us -> 40.2 us (0.55)
  blocking collectives: 47.2 us -> 9.61 us
  matrix products: 18.2 us -> 0 us
  Pallas kernels: 0 us -> 14.6 us
  waiting for transfers between devices: 0 us -> 8.3 us
  starting transfers between devices: 0 us -> 7.34 us
  local copies, waits for them, and re-layouts: 6.38 us -> 0 us
    all_gather x2 -> x0, blocking collectives: 47.2 us -> none  [the longest x1 27.5 us: on_device(): lax.all_gather(query_grads, 'dp', axis=0, tiled=True).astype(jnp.float32)]
    dot_general x8 -> x0, matrix products: 18.2 us -> none  [the longest x2 7.81 us: example_grads(): jnp.dot(hidden.reshape(number * length, inner), proj_in.T, preferred_elem...]
    pallas_call x0 -> x4, Pallas kernels: none -> 14.6 us  [the longest x1 7.19 us: project(): pl.pallas_call(functools.partial(project_kernel, planes, number, length,...]
    all_to_all x0 -> x1, blocking collectives: none -> 9.61 us  [fast(): parts = lax.all_to_all(parts, 'dp', 0, 0, tiled=True)]
    ppermute x0 -> x5, waiting for transfers between devices: none -> 8.3 us  [swap(): return lax.ppermute(x, 'dp', [(i, i ^ k) for i in range(n)])]
    ppermute x0 -> x5, starting transfers between devices: none -> 7.34 us  [swap(): return lax.ppermute(x, 'dp', [(i, i ^ k) for i in range(n)])]
    unnamed x12 -> x0, local copies, waits for them, and re-layouts: 2.42 us -> none
    convert_element_type x4 -> x0, local copies, waits for them, and re-layouts: 2.39 us -> none  [the longest x2 1.57 us: example_grads(): inputs = jnp.dot(hidden.reshape(number * length, inner), proj_in.T, prefe...]
  transfers between devices with their start and end apart: 0 -> 5, of which waited for: 0 -> 4; matrix products, arithmetic and copies ran while one was open for 0% -> 0% of each run, Pallas kernels for 0% -> 6%
where the time goes in v1:
time: 40.2 us; the launch traced here: 40 us
  Pallas kernels  14.6 us (36%)
  blocking collectives  9.61 us (24%)
  waiting for transfers between devices  8.3 us (21%)
  starting transfers between devices  7.34 us (18%)
    all_to_all x1, blocking collectives, fast(): parts = lax.all_to_all(parts, 'dp', 0, 0, tiled=True)  9.61 us
    ppermute x5, waiting for transfers between devices, swap(): return lax.ppermute(x, 'dp', [(i, i ^ k) for i in range(n)])  8.3 us
    ppermute x5, starting transfers between devices, swap(): return lax.ppermute(x, 'dp', [(i, i ^ k) for i in range(n)])  7.34 us
    pallas_call x1, Pallas kernels, project(): pl.pallas_call(functools.partial(project_kernel, planes, number, length,...  7.19 us
    pallas_call x1, Pallas kernels, score(): pl.pallas_call(functools.partial(score_kernel, n, number, qlen, slots), o...  4.47 us
    pallas_call x1, Pallas kernels, split(): pl.pallas_call(functools.partial(split_kernel, chunks), out_shape=[out] *...  2.35 us
  transfers between devices with their start and end apart: 5, of which 4 were waited for; matrix products, arithmetic and copies ran while one was open for 0% of the time, Pallas kernels for 6%

profile of v1, /device:TPU:0, one launch (start us, length us, event | category | flops | bytes accessed | tf_op | source)
XLA Modules:
  0.0 40.0 jit_solution(10204337730727177293)
XLA Ops:
  0.0 7.2 %project.1 = (bf16[128,128]{1,0:T(8,128)(2,1)S(1)}, bf16[128,128]{1,0:T(8,128)(2,1)S(1)}, bf16[128,128]{1,0:T(8,128)(2,1)S(1)}, bf16[128,128]{1,0:T(8,128)(2,1)S(1)}) custom-call(s32[1]{0:T(128)} %bitcast.me_ref, bf16[160,14336]{1,0:T(8,128)(2,1)} %bitcast.12, bf16[160,4096]{1,0:T(8,128)(2,1)} %bitcast.14, bf16[96,14336]{1,0:T(8,128)(2,1)} %bitcast.13, ...), custom_call_target="tpu_custom_call" | custom-call | tf_op jit(solution)/shard_map/project/pallas_call | solution.py:140
  7.2 3.1 %collective-permute-start = (bf16[128,128]{1,0:T(8,128)(2,1)S(1)}, bf16[128,128]{1,0:T(8,128)(2,1)S(1)}, u32[]{:S(2)}, u32[]{:S(2)}) collective-permute-start(bf16[128,128]{1,0:T(8,128)(2,1)S(1)} %get-tuple-element.15), channel_id=1, source_target_pairs={{0,4},{1,5},{2,6},{3,7},{4,0},{5,1},{6,2},{7,3},{8,12},{9,13},{10,... | collective-permute-start | bytes 98312 | tf_op jit(solution)/shard_map/ppermute | solution.py:311
  10.3 2.6 %collective-permute-start.1 = (bf16[128,128]{1,0:T(8,128)(2,1)S(1)}, bf16[128,128]{1,0:T(8,128)(2,1)S(1)}, u32[]{:S(2)}, u32[]{:S(2)}) collective-permute-start(bf16[128,128]{1,0:T(8,128)(2,1)S(1)} %get-tuple-element.16), channel_id=1, source_target_pairs={{0,8},{1,9},{2,10},{3,11},{4,12},{5,13},{6,14},{7,15},{8,0},{9,1},... | collective-permute-start | bytes 98312 | tf_op jit(solution)/shard_map/ppermute | solution.py:311
  12.9 0.0 collective-permute-start.2
  12.9 2.4 %split.1 = (bf16[256,4096]{1,0:T(8,128)(2,1)S(1)}, bf16[256,4096]{1,0:T(8,128)(2,1)S(1)}) custom-call(f32[256,4096]{1,0:T(8,128)} %hess_ref.1, bf16[128,128]{1,0:T(8,128)(2,1)S(1)} %get-tuple-element.14.after_ref), custom_call_target="tpu_custom_call" | custom-call | flops 3145728 | bytes 8388608 | tf_op jit(solution)/shard_map/split/pallas_call | solution.py:187
  15.2 0.0 collective-permute-done
  15.2 0.4 %collective-permute-done.1 = bf16[128,128]{1,0:T(8,128)(2,1)S(1)} collective-permute-done((bf16[128,128]{1,0:T(8,128)(2,1)S(1)}, bf16[128,128]{1,0:T(8,128)(2,1)S(1)}, u32[]{:S(2)}, u32[]{:S(2)}) %collective-permute-start.1) | collective-permute-done | bytes 32800 | tf_op jit(solution)/shard_map/ppermute | solution.py:311
  15.7 2.9 %collective-permute-done.2 = bf16[128,128]{1,0:T(8,128)(2,1)S(1)} collective-permute-done((bf16[128,128]{1,0:T(8,128)(2,1)S(1)}, bf16[128,128]{1,0:T(8,128)(2,1)S(1)}, u32[]{:S(2)}, u32[]{:S(2)}) %collective-permute-start.2) | collective-permute-done | bytes 32800 | tf_op jit(solution)/shard_map/ppermute | solution.py:311
  18.6 1.6 %collective-permute-start.3 = (bf16[4,128,128]{2,1,0:T(8,128)(2,1)S(1)}, bf16[4,128,128]{2,1,0:T(8,128)(2,1)S(1)}, u32[]{:S(2)}, u32[]{:S(2)}) collective-permute-start(bf16[4,128,128]{2,1,0:T(8,128)(2,1)S(1)} %pad_maximum_fusion.2), channel_id=1, source_target_pairs={{0,2},{1,3},{2,0},{3,1},{4,6},{5,7},{6,4},{7,5},{8,10},{9,11},{10,... | collective-permute-start | bytes 393224 | tf_op jit(solution)/shard_map/ppermute | solution.py:311
  20.2 3.4 %collective-permute-done.3 = bf16[4,128,128]{2,1,0:T(8,128)(2,1)S(1)} collective-permute-done((bf16[4,128,128]{2,1,0:T(8,128)(2,1)S(1)}, bf16[4,128,128]{2,1,0:T(8,128)(2,1)S(1)}, u32[]{:S(2)}, u32[]{:S(2)}) %collective-permute-start.3) | collective-permute-done | bytes 131104 | tf_op jit(solution)/shard_map/ppermute | solution.py:311
  23.7 0.1 collective-permute-start.4
  23.7 1.5 %collective-permute-done.4 = bf16[8,128,128]{2,1,0:T(8,128)(2,1)S(1)} collective-permute-done((bf16[8,128,128]{2,1,0:T(8,128)(2,1)S(1)}, bf16[8,128,128]{2,1,0:T(8,128)(2,1)S(1)}, u32[]{:S(2)}, u32[]{:S(2)}) %collective-permute-start.4) | collective-permute-done | bytes 262176 | tf_op jit(solution)/shard_map/ppermute | solution.py:311
  25.3 0.1 pad_maximum_fusion.rest_0_
  25.3 4.5 %score.1 = f32[128,128]{1,0:T(8,128)S(1)} custom-call(s32[1]{0:T(128)} %bitcast.me_ref, bf16[16,128,128]{2,1,0:T(8,128)(2,1)S(1)} %pad_maximum_fusion.rest_0_, bf16[256,4096]{1,0:T(8,128)(2,1)S(1)} %get-tuple-element.21.rest_1_, bf16[256,4096]{1,0:T(8,128)(2,1)S(1)} %get-tuple-element.22.rest_2_), custom_call_target="tpu_custom_call" | custom-call | tf_op jit(solution)/shard_map/score/pallas_call | solution.py:288
  29.8 9.6 %all_to_all.5.parts_ref = f32[16,8,128]{2,1,0:T(8,128)S(1)} all-to-all(f32[16,8,128]{2,1,0:T(8,128)S(1)} %bitcast.10), channel_id=1, replica_groups=mesh['groups'=2,'dp'=16] {'dp'}, dimensions={0} | all-to-all | bytes 131072 | tf_op jit(solution)/shard_map/all_to_all | solution.py:333
  39.4 0.6 %finish.1 = f32[4,96]{1,0:T(4,128)} custom-call(f32[16,8,128]{2,1,0:T(8,128)S(1)} %all_to_all.5.parts_ref), custom_call_target="tpu_custom_call" | custom-call | tf_op jit(solution)/shard_map/finish/pallas_call | solution.py:334
  (2 shorter events, 0.0 us)
Async XLA Ops:
  7.2 8.0 %collective-permute-start = (bf16[128,128]{1,0:T(8,128)(2,1)S(1)}, bf16[128,128]{1,0:T(8,128)(2,1)S(1)}, u32[]{:S(2)}, u32[]{:S(2)}) collective-permute-start(bf16[128,128]{1,0:T(8,128)(2,1)S(1)} %get-tuple-element.15), channel_id=1, source_target_pairs={{0,4},{1,5},{2,6},{3,7},{4,0},{5,1},{6,2},{7,3},{8,12},{9,13},{10,... | collective-permute-start | bytes 98312 | tf_op jit(solution)/shard_map/ppermute | solution.py:311
  10.3 5.4 %collective-permute-start.1 = (bf16[128,128]{1,0:T(8,128)(2,1)S(1)}, bf16[128,128]{1,0:T(8,128)(2,1)S(1)}, u32[]{:S(2)}, u32[]{:S(2)}) collective-permute-start(bf16[128,128]{1,0:T(8,128)(2,1)S(1)} %get-tuple-element.16), channel_id=1, source_target_pairs={{0,8},{1,9},{2,10},{3,11},{4,12},{5,13},{6,14},{7,15},{8,0},{9,1},... | collective-permute-start | bytes 98312 | tf_op jit(solution)/shard_map/ppermute | solution.py:311
  12.9 5.7 %collective-permute-start.2 = (bf16[128,128]{1,0:T(8,128)(2,1)S(1)}, bf16[128,128]{1,0:T(8,128)(2,1)S(1)}, u32[]{:S(2)}, u32[]{:S(2)}) collective-permute-start(bf16[128,128]{1,0:T(8,128)(2,1)S(1)} %get-tuple-element.17), channel_id=1, source_target_pairs={{0,12},{1,13},{2,14},{3,15},{4,8},{5,9},{6,10},{7,11},{8,4},{9,5},... | collective-permute-start | bytes 98312 | tf_op jit(solution)/shard_map/ppermute | solution.py:311
  18.6 5.0 %collective-permute-start.3 = (bf16[4,128,128]{2,1,0:T(8,128)(2,1)S(1)}, bf16[4,128,128]{2,1,0:T(8,128)(2,1)S(1)}, u32[]{:S(2)}, u32[]{:S(2)}) collective-permute-start(bf16[4,128,128]{2,1,0:T(8,128)(2,1)S(1)} %pad_maximum_fusion.2), channel_id=1, source_target_pairs={{0,2},{1,3},{2,0},{3,1},{4,6},{5,7},{6,4},{7,5},{8,10},{9,11},{10,... | collective-permute-start | bytes 393224 | tf_op jit(solution)/shard_map/ppermute | solution.py:311
  23.7 1.6 %collective-permute-start.4 = (bf16[8,128,128]{2,1,0:T(8,128)(2,1)S(1)}, bf16[8,128,128]{2,1,0:T(8,128)(2,1)S(1)}, u32[]{:S(2)}, u32[]{:S(2)}) collective-permute-start(bf16[8,128,128]{2,1,0:T(8,128)(2,1)S(1)} %pad_maximum_fusion.1), channel_id=1, source_target_pairs={{0,1},{1,0},{2,3},{3,2},{4,5},{5,4},{6,7},{7,6},{8,9},{9,8},{10,11... | collective-permute-start | bytes 786440 | tf_op jit(solution)/shard_map/ppermute | solution.py:311

commit v2 on v1

v2 whole, which is shorter than its diff:
```python
import functools

import jax
import jax.numpy as jnp
from jax import lax
from jax.experimental import pallas as pl
from jax.experimental.pallas import tpu as pltpu
from jax.sharding import PartitionSpec as P

F32, BF16 = jnp.float32, jnp.bfloat16
NT = (((1,), (1,)), ((), ()))
VMEM = pl.BlockSpec(memory_space=pltpu.VMEM)
HBM = pl.BlockSpec(memory_space=pltpu.HBM)
CORES = 2
GROUP = 256


def dot(a, b):
    return jnp.dot(a, b, preferred_element_type=F32)


def dot_nt(a, b):
    return lax.dot_general(a, b, NT, preferred_element_type=F32)


def in_hbm(x):
    return pltpu.with_memory_space_constraint(x, pltpu.HBM)


def iota(shape, dim):
    return lax.broadcasted_iota(jnp.int32, shape, dim)


def example_grads(hidden, cotangent, proj_in, proj_out):
    number, length, inner = hidden.shape
    outer_width = cotangent.shape[2]
    rank = proj_in.shape[0]
    inputs = jnp.dot(
        hidden.reshape(number * length, inner), proj_in.T, preferred_element_type=jnp.float32
    ).astype(jnp.bfloat16)
    outputs = jnp.dot(
        cotangent.reshape(number * length, outer_width),
        proj_out.T,
        preferred_element_type=jnp.float32,
    ).astype(jnp.bfloat16)
    inputs = inputs.reshape(number, length, rank)
    outputs = outputs.reshape(number, length, rank)
    summed = jnp.einsum("sto,sti->soi", outputs, inputs, preferred_element_type=jnp.float32) * (
        1.0 / length
    )
    return summed.astype(jnp.bfloat16).reshape(number, rank * rank)


def general(train_hidden, train_cot, query_hidden, query_cot, proj_in, proj_out, hess_inv):
    train_grads = example_grads(train_hidden, train_cot, proj_in, proj_out)
    query_grads = example_grads(query_hidden, query_cot, proj_in, proj_out)
    full_query = lax.all_gather(query_grads, "dp", axis=0, tiled=True).astype(jnp.float32)
    product = jnp.dot(full_query, hess_inv.T, precision=lax.Precision.HIGHEST)
    full_precond = lax.all_gather(product.astype(jnp.bfloat16), "dp", axis=1, tiled=True)
    self_inf = jnp.sum(full_query * full_precond.astype(jnp.float32), axis=1)
    raw = jnp.dot(train_grads, full_precond.T, preferred_element_type=jnp.float32)
    return raw / jnp.sqrt(self_inf)[None, :]


def project_kernel(
    number, length, widths, th_ref, tc_ref, qh_ref, qc_ref, pi_ref, po_ref, out_ref, *scratch
):
    th, tc, qh, qc, pi, po, sems = scratch
    inner = th.shape[1]
    rank = pi.shape[0]
    tokens = th.shape[0]
    queries = qh.shape[0]

    copies = []

    def load(*pairs):
        group = []
        for src, dst in pairs:
            group.append(pltpu.make_async_copy(src, dst, sems.at[sum(map(len, copies)) + len(group)]))
            group[-1].start()
        copies.append(group)

    def arrived():
        for copy in copies.pop(0):
            copy.wait()

    parts = [slice(sum(widths[:c]), sum(widths[: c + 1])) for c in range(len(widths))]
    for c, cols in enumerate(parts):
        load(
            (pi_ref.at[:, cols], pi.at[:, cols]),
            (th_ref.at[:, cols], th.at[:, cols]),
            (qh_ref.at[:, cols], qh.at[:, cols]),
        )
        if c == 0:
            load((po_ref, po), (tc_ref, tc), (qc_ref, qc))

    rows = rank // 2 * number
    t_in = jnp.zeros((tokens, rank), F32)
    q_in = jnp.zeros((queries, rank), F32)
    for c, cols in enumerate(parts):
        arrived()
        t_in += dot_nt(th[:, cols], pi[:, cols])
        q_in += dot_nt(qh[:, cols], pi[:, cols])
        if c == 0:
            arrived()
            q_out = dot_nt(qc[...], po[...])
            t_out = dot_nt(po[...], tc[...]).astype(BF16)

    row, col = iota((rows, tokens), 0), iota((rows, tokens), 1)
    own = row % number == col // length
    lefts = []
    for half in range(2):
        pick = iota((rows, rank), 1) == 2 * (iota((rows, rank), 0) // number) + half
        lefts.append(jnp.where(own, dot(pick.astype(BF16), t_out), 0.0).astype(BF16))

    spread = jnp.concatenate([t_in, t_in], axis=1).astype(BF16)
    lane = iota((tokens, 2 * rank), 1)
    total = jnp.zeros((rows, 2 * rank), F32)
    for half in range(2):
        right = jnp.where(lane // rank == half, spread, jnp.zeros_like(spread))
        total += dot(lefts[half], right)
    grads = (total * (1.0 / length)).astype(BF16)
    message = jnp.concatenate([q_in, q_out], axis=1).astype(BF16)

    share = rows // out_ref.shape[0]
    for chip in range(out_ref.shape[0]):
        out_ref[chip, :queries, :] = message
        out_ref[chip, queries:, :] = grads[chip * share : (chip + 1) * share, :]


def project(chips, train_hidden, train_cot, query_hidden, query_cot, proj_in, proj_out):
    number, length, inner = train_hidden.shape
    width = train_cot.shape[2]
    rank = proj_in.shape[0]
    tokens, queries = number * length, query_hidden.shape[0] * query_hidden.shape[1]
    rows = rank // 2 * number
    widths = [2048, 4096, 4096, 4096]
    return pl.pallas_call(
        functools.partial(project_kernel, number, length, widths),
        out_shape=pltpu.VMEM((chips, queries + rows // chips, 2 * rank), BF16),
        in_specs=[HBM] * 6,
        out_specs=VMEM,
        scratch_shapes=[
            pltpu.VMEM((tokens, inner), BF16),
            pltpu.VMEM((tokens, width), BF16),
            pltpu.VMEM((queries, inner), BF16),
            pltpu.VMEM((queries, width), BF16),
            pltpu.VMEM((rank, inner), BF16),
            pltpu.VMEM((rank, width), BF16),
            pltpu.SemaphoreType.DMA((3 * len(widths) + 3,)),
        ],
        compiler_params=pltpu.CompilerParams(vmem_limit_bytes=20 * 2**20),
        name="project",
    )(
        in_hbm(train_hidden.reshape(tokens, inner)),
        in_hbm(train_cot.reshape(tokens, width)),
        in_hbm(query_hidden.reshape(queries, inner)),
        in_hbm(query_cot.reshape(queries, width)),
        in_hbm(proj_in),
        in_hbm(proj_out),
    )


def build(tok, qlen, grads):
    lanes = tok.shape[1]
    rank = lanes // 2
    pairs = rank // 2
    per = GROUP // qlen
    pick = (iota((rank, lanes), 1) == iota((rank, lanes), 0) + rank).astype(BF16)
    shift = (iota((lanes, lanes), 1) == iota((lanes, lanes), 0) + rank).astype(BF16)
    own = (iota((per, GROUP), 1) // qlen == iota((per, GROUP), 0)).astype(BF16)
    low = iota((GROUP, lanes), 1) < rank
    for g in range(tok.shape[0] // GROUP):
        x = tok[g * GROUP : (g + 1) * GROUP, :]
        outs = dot_nt(pick, x)
        right = jnp.concatenate(
            [jnp.where(low, x, jnp.zeros_like(x)), dot(x, shift).astype(BF16)], axis=0
        )
        left = []
        for pair in range(pairs):
            left.append(
                jnp.concatenate(
                    [
                        jnp.broadcast_to(outs[o : o + 1, :], (per, GROUP)).astype(BF16) * own
                        for o in (2 * pair, 2 * pair + 1)
                    ],
                    axis=1,
                )
            )
        made = (dot(jnp.concatenate(left, axis=0), right) * (1.0 / qlen)).astype(BF16)
        for pair in range(pairs):
            grads[g * per : (g + 1) * per, pair * lanes : (pair + 1) * lanes] = made[
                pair * per : (pair + 1) * per, :
            ]


def prepare_kernel(qlen, chunks, mine_ref, hess_ref, grads_ref, high_ref, low_ref, tok, hess, sems):
    width = hess.shape[1] // chunks
    copies = []
    for c in range(chunks):
        cols = pl.ds(c * width, width)
        copies.append(pltpu.make_async_copy(hess_ref.at[:, cols], hess.at[:, cols], sems.at[c]))
        copies[-1].start()
    tokens = tok.shape[0] // mine_ref.shape[0]
    for chip in range(mine_ref.shape[0]):
        tok[chip * tokens : (chip + 1) * tokens, :] = mine_ref[chip, :tokens, :]
    build(tok, qlen, grads_ref)
    for c in range(chunks):
        copies[c].wait()
        cols = slice(c * width, (c + 1) * width)
        h = hess[:, cols]
        high = h.astype(BF16)
        high_ref[:, cols] = high
        low_ref[:, cols] = (h - high.astype(F32)).astype(BF16)


def prepare(tokens, qlen, mine, hess_inv):
    chips, _, lanes = mine.shape
    coords = hess_inv.shape[1]
    chunks = 4
    return pl.pallas_call(
        functools.partial(prepare_kernel, qlen, chunks),
        out_shape=[
            pltpu.VMEM((chips * tokens // qlen, coords), BF16),
            pltpu.VMEM(hess_inv.shape, BF16),
            pltpu.VMEM(hess_inv.shape, BF16),
        ],
        in_specs=[VMEM, HBM],
        out_specs=[VMEM] * 3,
        scratch_shapes=[
            pltpu.VMEM((chips * tokens, lanes), BF16),
            pltpu.VMEM(hess_inv.shape, F32),
            pltpu.SemaphoreType.DMA((chunks,)),
        ],
        compiler_params=pltpu.CompilerParams(vmem_limit_bytes=20 * 2**20),
        name="prepare",
    )(mine, in_hbm(hess_inv))


def score_kernel(number, qlen, me_ref, mine_ref, theirs_ref, made_ref, high_ref, low_ref, *rest):
    out_ref, tok, train, grads = rest
    me = me_ref[0]
    core = me % CORES
    block = high_ref.shape[0]
    chips, _, lanes = mine_ref.shape
    tokens = tok.shape[0] // chips
    each = tokens // qlen
    local = block // lanes
    tile = local * number

    for chip in range(chips):
        tok[chip * tokens : (chip + 1) * tokens, :] = theirs_ref[chip, :tokens, :]
        for ref, which in ((mine_ref, core), (theirs_ref, 1 - core)):
            both = ref[chip, tokens:, :].astype(F32)
            train[CORES * chip + which] = jnp.where(core == 0, both[:tile], both[tile:])
    half = chips * each
    grads[:half, :] = made_ref[...]
    build(tok, qlen, grads.at[half:, :])

    queries = grads.shape[0]
    precond = dot_nt(high_ref[...], grads[...]) + dot_nt(low_ref[...], grads[...])
    row, col = iota((queries, queries), 0), iota((queries, queries), 1)
    from_core = jnp.where(row < half, core, 1 - core)
    place = (row % half // each * CORES + from_core) * each + row % each
    order = place == col
    precond = dot(precond.astype(BF16), order.astype(BF16)).astype(BF16)

    start = pl.multiple_of(me * block, block)
    square = dot(grads[:, pl.ds(start, block)], precond)
    self_inf = jnp.sum(jnp.where(order, square, 0.0), axis=0, keepdims=True)

    rows = CORES * chips * tile
    t = train[...].reshape(rows, lanes)
    where = iota((rows, lanes), 0) % tile // number
    wide = jnp.concatenate(
        [jnp.where(where == j, t, 0.0).astype(BF16) for j in range(local)], axis=1
    )
    parts = dot(wide, precond)
    raw = parts
    for j in range(1, local):
        raw = raw + pltpu.roll(parts, rows - j * number, 0)
    raw = jnp.where(iota((rows, queries), 0) % tile < number, raw, self_inf)
    out_ref[...] = jnp.zeros_like(out_ref)
    out_ref[:, :queries] = raw


def score(me, number, qlen, tokens, mine, theirs, made, high, low):
    block, coords = high.shape
    chips, _, lanes = mine.shape
    tile = block // lanes * number
    n = CORES * chips
    queries = n * tokens // qlen
    padded = -(-queries // 128) * 128
    return pl.pallas_call(
        functools.partial(score_kernel, number, qlen),
        out_shape=pltpu.VMEM((n * tile, padded), F32),
        in_specs=[pl.BlockSpec(memory_space=pltpu.SMEM)] + [VMEM] * 5,
        out_specs=VMEM,
        scratch_shapes=[
            pltpu.VMEM((chips * tokens, lanes), BF16),
            pltpu.VMEM((n, tile, lanes), F32),
            pltpu.VMEM((queries, coords), BF16),
        ],
        compiler_params=pltpu.CompilerParams(vmem_limit_bytes=20 * 2**20),
        name="score",
    )(me, mine, theirs, made, high, low)


def finish_kernel(number, parts_ref, out_ref):
    total = jnp.sum(parts_ref[...], axis=0)
    queries = out_ref.shape[1]
    self_inf = total[number : number + 1, :queries]
    out_ref[...] = total[:number, :queries] / jnp.sqrt(self_inf)


def fast(n, train_hidden, train_cot, query_hidden, query_cot, proj_in, proj_out, hess_inv):
    number, qlen = train_hidden.shape[0], query_hidden.shape[1]
    tokens = query_hidden.shape[0] * qlen
    queries = n * query_hidden.shape[0]
    chips = n // CORES
    me = lax.axis_index("dp").astype(jnp.int32).reshape(1)
    messages = project(
        chips, train_hidden, train_cot, query_hidden, query_cot, proj_in, proj_out
    )
    same_core = [[CORES * chip + core for chip in range(chips)] for core in range(CORES)]
    mine = lax.all_to_all(messages, "dp", 0, 0, tiled=True, axis_index_groups=same_core)
    theirs = lax.ppermute(mine, "dp", [(i, i ^ 1) for i in range(n)])
    made, high, low = prepare(tokens, qlen, mine, hess_inv)
    parts = score(me, number, qlen, tokens, mine, theirs, made, high, low)
    parts = parts.reshape(n, -1, parts.shape[1])
    parts = lax.all_to_all(parts, "dp", 0, 0, tiled=True)
    return pl.pallas_call(
        functools.partial(finish_kernel, number),
        out_shape=jax.ShapeDtypeStruct((number, queries), F32),
        in_specs=[VMEM],
        out_specs=VMEM,
        compiler_params=pltpu.CompilerParams(vmem_limit_bytes=4 * 2**20),
        name="finish",
    )(pltpu.with_memory_space_constraint(parts, pltpu.VMEM))


def suits(n, args):
    train_hidden, _, query_hidden, _, proj_in, _, hess_inv = args
    number, qlen = train_hidden.shape[0], query_hidden.shape[1]
    tokens = query_hidden.shape[0] * qlen
    lanes = 2 * proj_in.shape[0]
    block = hess_inv.shape[0]
    return (
        n % CORES == 0
        and n > CORES
        and lanes == 128
        and block % lanes == 0
        and block // lanes * number == 8
        and tokens % 16 == 0
        and GROUP % (16 * qlen) == 0
        and n // CORES * tokens % GROUP == 0
    )


def on_device(n, *args):
    return fast(n, *args) if suits(n, args) else general(*args)


def solution(mesh):
    n = mesh.shape["dp"]
    in_specs = (
        P(("groups", "dp"), None, None),
        P(("groups", "dp"), None, None),
        P(("groups", "dp"), None, None),
        P(("groups", "dp"), None, None),
        P(),
        P(),
        P(("groups", "dp"), None),
    )
    out_specs = P(("groups", "dp"), None)
    return jax.shard_map(
        functools.partial(on_device, n),
        mesh=mesh,
        in_specs=in_specs,
        out_specs=out_specs,
        check_vma=False,
    )
```

time: 40.2 us -> 38 us (0.945)
  blocking collectives: 9.61 us -> 25.8 us
  waiting for transfers between devices: 8.3 us -> 0.01 us
  starting transfers between devices: 7.34 us -> 0.01 us
  Pallas kernels: 14.6 us -> 12 us
    all_to_all x0 -> x1, blocking collectives: none -> 15.5 us  [fast(): lax.all_to_all(messages, 'dp', 0, 0, tiled=True, axis_index_groups=same_c...]
    ppermute x5 -> x1, waiting for transfers between devices: 8.3 us -> 0.01 us  [fast(): theirs = lax.ppermute(mine, 'dp', [(i, i ^ 1) for i in range(n)])]
    ppermute x5 -> x1, starting transfers between devices: 7.34 us -> 0.01 us  [fast(): theirs = lax.ppermute(mine, 'dp', [(i, i ^ 1) for i in range(n)])]
    pallas_call x3, Pallas kernels: 14 us -> 11.4 us  [the longest x1 5.75 us: project(): pl.pallas_call(functools.partial(project_kernel, number, length, widths),...]
    all_to_all x1, blocking collectives: 9.61 us -> 10.3 us  [fast(): parts = lax.all_to_all(parts, 'dp', 0, 0, tiled=True)]
  transfers between devices with their start and end apart: 5 -> 1, of which waited for: 4 -> 0; matrix products, arithmetic and copies ran while one was open for 0% -> 0% of each run, Pallas kernels for 6% -> 6%
where the time goes in v2:
time: 38 us; the launch traced here: 37.8 us
  blocking collectives  25.8 us (68%)
  Pallas kernels  12 us (32%)
    all_to_all x1, blocking collectives, fast(): lax.all_to_all(messages, 'dp', 0, 0, tiled=True, axis_index_groups=same_c...  15.5 us
    all_to_all x1, blocking collectives, fast(): parts = lax.all_to_all(parts, 'dp', 0, 0, tiled=True)  10.3 us
    pallas_call x1, Pallas kernels, project(): pl.pallas_call(functools.partial(project_kernel, number, length, widths),...  5.75 us
    pallas_call x1, Pallas kernels, score(): pl.pallas_call(functools.partial(score_kernel, number, qlen), out_shape=p...  3.27 us
    pallas_call x1, Pallas kernels, prepare(): pl.pallas_call(functools.partial(prepare_kernel, qlen, chunks), out_shape...  2.37 us
  transfers between devices with their start and end apart: 1, of which 0 were waited for; matrix products, arithmetic and copies ran while one was open for 0% of the time, Pallas kernels for 6%

profile of v2, /device:TPU:0, one launch (start us, length us, event | category | flops | bytes accessed | tf_op | source)
XLA Modules:
  0.0 37.8 jit_solution(9605491278067081447)
XLA Ops:
  0.0 5.7 %project.1 = bf16[8,112,128]{2,1,0:T(8,128)(2,1)S(1)} custom-call(bf16[160,14336]{1,0:T(8,128)(2,1)} %bitcast.7, bf16[160,4096]{1,0:T(8,128)(2,1)} %bitcast.9, bf16[96,14336]{1,0:T(8,128)(2,1)} %bitcast.8, bf16[96,4096]{1,0:T(8,128)(2,1)} %bitcast.10, bf16[64,14336]{1,0:T(8,128)(2,1)} %pi_ref.1, bf16[64,4096]{1,0:T(8,128)(2,1)} %po_ref.1), custom_call_target="tpu_custom_call" | custom-call | tf_op jit(solution)/shard_map/project/pallas_call | solution.py:138
  5.8 15.5 %all_to_all.10.mine_ref = bf16[8,112,128]{2,1,0:T(8,128)(2,1)S(1)} all-to-all(bf16[8,112,128]{2,1,0:T(8,128)(2,1)S(1)} %project.1), channel_id=1, replica_groups={{0,2,4,6,8,10,12,14},{1,3,5,7,9,11,13,15},{16,18,20,22,24,26,28,30},{17..., dimensions={0} | all-to-all | bytes 458752 | tf_op jit(solution)/shard_map/all_to_all | solution.py:326
  21.3 0.0 collective-permute-start
  21.3 2.4 %prepare.1 = (bf16[48,4096]{1,0:T(8,128)(2,1)S(1)}, bf16[256,4096]{1,0:T(8,128)(2,1)S(1)}, bf16[256,4096]{1,0:T(8,128)(2,1)S(1)}) custom-call(bf16[8,112,128]{2,1,0:T(8,128)(2,1)S(1)} %all_to_all.10.mine_ref, f32[256,4096]{1,0:T(8,128)} %hess_ref.1), custom_call_target="tpu_custom_call" | custom-call | tf_op jit(solution)/shard_map/prepare/pallas_call | solution.py:221
  23.7 0.0 collective-permute-done.theirs_ref
  23.7 3.3 %score.1 = f32[128,128]{1,0:T(8,128)S(1)} custom-call(s32[1]{0:T(128)} %bitcast.me_ref, bf16[8,112,128]{2,1,0:T(8,128)(2,1)S(1)} %all_to_all.10.mine_ref, bf16[8,112,128]{2,1,0:T(8,128)(2,1)S(1)} %collective-permute-done.theirs_ref, bf16[48,4096]{1,0:T(8,128)(2,1)S(1)} %get-tuple-element.8.made_ref, bf16[256,4096]{1,0:T(8,128)(2,1)S(1)} %get-tuple-element.9.high_ref, ...), custom_call_target="tpu_custom_call" | custom-call | tf_op jit(solution)/shard_map/score/pallas_call | solution.py:294
  27.0 10.3 %all_to_all.11.parts_ref = f32[16,8,128]{2,1,0:T(8,128)S(1)} all-to-all(f32[16,8,128]{2,1,0:T(8,128)S(1)} %bitcast.6), channel_id=1, replica_groups=mesh['groups'=2,'dp'=16] {'dp'}, dimensions={0} | all-to-all | bytes 131072 | tf_op jit(solution)/shard_map/all_to_all | solution.py:331
  37.2 0.6 %finish.1 = f32[4,96]{1,0:T(4,128)} custom-call(f32[16,8,128]{2,1,0:T(8,128)S(1)} %all_to_all.11.parts_ref), custom_call_target="tpu_custom_call" | custom-call | tf_op jit(solution)/shard_map/finish/pallas_call | solution.py:332
Async XLA Ops:
  21.3 2.4 %collective-permute-start = (bf16[8,112,128]{2,1,0:T(8,128)(2,1)S(1)}, bf16[8,112,128]{2,1,0:T(8,128)(2,1)S(1)}, u32[]{:S(2)}, u32[]{:S(2)}) collective-permute-start(bf16[8,112,128]{2,1,0:T(8,128)(2,1)S(1)} %all_to_all.10.mine_ref), channel_id=1, source_target_pairs={{0,1},{1,0},{2,3},{3,2},{4,5},{5,4},{6,7},{7,6},{8,9},{9,8},{10,11... | collective-permute-start | bytes 688136 | tf_op jit(solution)/shard_map/ppermute | solution.py:327

commit v3 on v2

--- a/solution.py
+++ b/solution.py
@@ -11,7 +11,7 @@
 NT = (((1,), (1,)), ((), ()))
 VMEM = pl.BlockSpec(memory_space=pltpu.VMEM)
 HBM = pl.BlockSpec(memory_space=pltpu.HBM)
-CORES = 2
+INNER = 4
 GROUP = 256
 
 
@@ -63,9 +63,9 @@
 
 
 def project_kernel(
-    number, length, widths, th_ref, tc_ref, qh_ref, qc_ref, pi_ref, po_ref, out_ref, *scratch
+    planes, number, length, widths, me_ref, th_ref, tc_ref, qh_ref, qc_ref, pi_ref, po_ref, *rest
 ):
-    th, tc, qh, qc, pi, po, sems = scratch
+    outs, (th, tc, qh, qc, pi, po, grads, sems) = rest[:planes], rest[planes:]
     inner = th.shape[1]
     rank = pi.shape[0]
     tokens = th.shape[0]
@@ -119,16 +119,18 @@
     for half in range(2):
         right = jnp.where(lane // rank == half, spread, jnp.zeros_like(spread))
         total += dot(lefts[half], right)
-    grads = (total * (1.0 / length)).astype(BF16)
+    grads[...] = (total * (1.0 / length)).astype(BF16)
     message = jnp.concatenate([q_in, q_out], axis=1).astype(BF16)
 
-    share = rows // out_ref.shape[0]
-    for chip in range(out_ref.shape[0]):
-        out_ref[chip, :queries, :] = message
-        out_ref[chip, queries:, :] = grads[chip * share : (chip + 1) * share, :]
-
-
-def project(chips, train_hidden, train_cot, query_hidden, query_cot, proj_in, proj_out):
+    plane = me_ref[0] // INNER
+    share = rows // planes
+    for k in range(planes):
+        outs[k][:queries, :] = message
+        first = pl.multiple_of((plane ^ k) * share, share)
+        outs[k][queries:, :] = grads[pl.ds(first, share), :]
+
+
+def project(me, planes, train_hidden, train_cot, query_hidden, query_cot, proj_in, proj_out):
     number, length, inner = train_hidden.shape
     width = train_cot.shape[2]
     rank = proj_in.shape[0]
@@ -136,10 +138,10 @@
     rows = rank // 2 * number
     widths = [2048, 4096, 4096, 4096]
     return pl.pallas_call(
-        functools.partial(project_kernel, number, length, widths),
-        out_shape=pltpu.VMEM((chips, queries + rows // chips, 2 * rank), BF16),
-        in_specs=[HBM] * 6,
-        out_specs=VMEM,
+        functools.partial(project_kernel, planes, number, length, widths),
+        out_shape=[pltpu.VMEM((queries + rows // planes, 2 * rank), BF16)] * planes,
+        in_specs=[pl.BlockSpec(memory_space=pltpu.SMEM)] + [HBM] * 6,
+        out_specs=[VMEM] * planes,
         scratch_shapes=[
             pltpu.VMEM((tokens, inner), BF16),
             pltpu.VMEM((tokens, width), BF16),
@@ -147,11 +149,13 @@
             pltpu.VMEM((queries, width), BF16),
             pltpu.VMEM((rank, inner), BF16),
             pltpu.VMEM((rank, width), BF16),
+            pltpu.VMEM((rows, 2 * rank), BF16),
             pltpu.SemaphoreType.DMA((3 * len(widths) + 3,)),
         ],
         compiler_params=pltpu.CompilerParams(vmem_limit_bytes=20 * 2**20),
         name="project",
     )(
+        me,
         in_hbm(train_hidden.reshape(tokens, inner)),
         in_hbm(train_cot.reshape(tokens, width)),
         in_hbm(query_hidden.reshape(queries, inner)),
@@ -169,24 +173,24 @@
     pick = (iota((rank, lanes), 1) == iota((rank, lanes), 0) + rank).astype(BF16)
     shift = (iota((lanes, lanes), 1) == iota((lanes, lanes), 0) + rank).astype(BF16)
     own = (iota((per, GROUP), 1) // qlen == iota((per, GROUP), 0)).astype(BF16)
-    low = iota((GROUP, lanes), 1) < rank
+    every = tok[...]
+    outs = dot_nt(pick, every)
+    moved = dot(every, shift).astype(BF16)
+    still = jnp.where(iota(every.shape, 1) < rank, every, jnp.zeros_like(every))
     for g in range(tok.shape[0] // GROUP):
-        x = tok[g * GROUP : (g + 1) * GROUP, :]
-        outs = dot_nt(pick, x)
-        right = jnp.concatenate(
-            [jnp.where(low, x, jnp.zeros_like(x)), dot(x, shift).astype(BF16)], axis=0
-        )
+        cols = slice(g * GROUP, (g + 1) * GROUP)
         left = []
         for pair in range(pairs):
             left.append(
                 jnp.concatenate(
                     [
-                        jnp.broadcast_to(outs[o : o + 1, :], (per, GROUP)).astype(BF16) * own
+                        jnp.broadcast_to(outs[o : o + 1, cols], (per, GROUP)).astype(BF16) * own
                         for o in (2 * pair, 2 * pair + 1)
                     ],
                     axis=1,
                 )
             )
+        right = jnp.concatenate([still[cols], moved[cols]], axis=0)
         made = (dot(jnp.concatenate(left, axis=0), right) * (1.0 / qlen)).astype(BF16)
         for pair in range(pairs):
             grads[g * per : (g + 1) * per, pair * lanes : (pair + 1) * lanes] = made[
@@ -194,17 +198,13 @@
             ]
 
 
-def prepare_kernel(qlen, chunks, mine_ref, hess_ref, grads_ref, high_ref, low_ref, tok, hess, sems):
+def split_kernel(chunks, hess_ref, after_ref, high_ref, low_ref, hess, sems):
     width = hess.shape[1] // chunks
     copies = []
     for c in range(chunks):
         cols = pl.ds(c * width, width)
         copies.append(pltpu.make_async_copy(hess_ref.at[:, cols], hess.at[:, cols], sems.at[c]))
         copies[-1].start()
-    tokens = tok.shape[0] // mine_ref.shape[0]
-    for chip in range(mine_ref.shape[0]):
-        tok[chip * tokens : (chip + 1) * tokens, :] = mine_ref[chip, :tokens, :]
-    build(tok, qlen, grads_ref)
     for c in range(chunks):
         copies[c].wait()
         cols = slice(c * width, (c + 1) * width)
@@ -214,62 +214,76 @@
         low_ref[:, cols] = (h - high.astype(F32)).astype(BF16)
 
 
-def prepare(tokens, qlen, mine, hess_inv):
-    chips, _, lanes = mine.shape
-    coords = hess_inv.shape[1]
+def split(hess_inv, after):
     chunks = 4
     return pl.pallas_call(
-        functools.partial(prepare_kernel, qlen, chunks),
-        out_shape=[
-            pltpu.VMEM((chips * tokens // qlen, coords), BF16),
-            pltpu.VMEM(hess_inv.shape, BF16),
-            pltpu.VMEM(hess_inv.shape, BF16),
-        ],
-        in_specs=[VMEM, HBM],
-        out_specs=[VMEM] * 3,
+        functools.partial(split_kernel, chunks),
+        out_shape=[pltpu.VMEM(hess_inv.shape, BF16)] * 2,
+        in_specs=[HBM, VMEM],
+        out_specs=[VMEM] * 2,
         scratch_shapes=[
-            pltpu.VMEM((chips * tokens, lanes), BF16),
             pltpu.VMEM(hess_inv.shape, F32),
             pltpu.SemaphoreType.DMA((chunks,)),
         ],
         compiler_params=pltpu.CompilerParams(vmem_limit_bytes=20 * 2**20),
+        name="split",
+    )(in_hbm(hess_inv), after)
+
+
+def prepare_kernel(qlen, mine_ref, grads_ref, tok):
+    tokens = tok.shape[0] // mine_ref.shape[0]
+    for slot in range(mine_ref.shape[0]):
+        tok[slot * tokens : (slot + 1) * tokens, :] = mine_ref[slot, :tokens, :]
+    build(tok, qlen, grads_ref)
+
+
+def prepare(tokens, qlen, coords, mine):
+    count, _, lanes = mine.shape
+    return pl.pallas_call(
+        functools.partial(prepare_kernel, qlen),
+        out_shape=pltpu.VMEM((count * tokens // qlen, coords), BF16),
+        in_specs=[VMEM],
+        out_specs=VMEM,
+        scratch_shapes=[pltpu.VMEM((count * tokens, lanes), BF16)],
+        compiler_params=pltpu.CompilerParams(vmem_limit_bytes=20 * 2**20),
         name="prepare",
-    )(mine, in_hbm(hess_inv))
-
-
-def score_kernel(number, qlen, me_ref, mine_ref, theirs_ref, made_ref, high_ref, low_ref, *rest):
-    out_ref, tok, train, grads = rest
+    )(mine)
+
+
+def score_kernel(number, tokens, qlen, me_ref, mine_ref, theirs_ref, *rest):
+    made_refs, (high_ref, low_ref, out_ref, train) = rest[:2], rest[2:]
     me = me_ref[0]
-    core = me % CORES
     block = high_ref.shape[0]
-    chips, _, lanes = mine_ref.shape
-    tokens = tok.shape[0] // chips
+    count, _, lanes = mine_ref.shape
+    planes = count // (INNER // 2)
     each = tokens // qlen
     local = block // lanes
     tile = local * number
-
-    for chip in range(chips):
-        tok[chip * tokens : (chip + 1) * tokens, :] = theirs_ref[chip, :tokens, :]
-        for ref, which in ((mine_ref, core), (theirs_ref, 1 - core)):
-            both = ref[chip, tokens:, :].astype(F32)
-            train[CORES * chip + which] = jnp.where(core == 0, both[:tile], both[tile:])
-    half = chips * each
-    grads[:half, :] = made_ref[...]
-    build(tok, qlen, grads.at[half:, :])
-
+    inner = me % INNER
+
+    def source(slot):
+        by_two, plane = slot // planes % 2, (planes - slot % planes) % planes
+        return me ^ (plane * INNER + by_two * 2 + slot // count)
+
+    for slot in range(count):
+        for ref, first in ((mine_ref, 0), (theirs_ref, count)):
+            share = ref[slot, tokens:, :].astype(F32)
+            picked = share[:tile]
+            for j in range(1, INNER):
+                picked = jnp.where(inner == j, share[j * tile : (j + 1) * tile], picked)
+            train[source(first + slot)] = picked
+    grads = jnp.concatenate([ref[...] for ref in made_refs], axis=0)
     queries = grads.shape[0]
-    precond = dot_nt(high_ref[...], grads[...]) + dot_nt(low_ref[...], grads[...])
+    precond = dot_nt(high_ref[...], grads) + dot_nt(low_ref[...], grads)
     row, col = iota((queries, queries), 0), iota((queries, queries), 1)
-    from_core = jnp.where(row < half, core, 1 - core)
-    place = (row % half // each * CORES + from_core) * each + row % each
-    order = place == col
+    order = source(row // each) * each + row % each == col
     precond = dot(precond.astype(BF16), order.astype(BF16)).astype(BF16)
 
-    start = pl.multiple_of(me * block, block)
-    square = dot(grads[:, pl.ds(start, block)], precond)
+    cols = pl.ds(pl.multiple_of(me * block, block), block)
+    square = dot(jnp.concatenate([ref[:, cols] for ref in made_refs], axis=0), precond)
     self_inf = jnp.sum(jnp.where(order, square, 0.0), axis=0, keepdims=True)
 
-    rows = CORES * chips * tile
+    rows = 2 * count * tile
     t = train[...].reshape(rows, lanes)
     where = iota((rows, lanes), 0) % tile // number
     wide = jnp.concatenate(
@@ -284,26 +298,22 @@
     out_ref[:, :queries] = raw
 
 
-def score(me, number, qlen, tokens, mine, theirs, made, high, low):
-    block, coords = high.shape
-    chips, _, lanes = mine.shape
+def score(me, number, tokens, qlen, mine, theirs, made, high, low):
+    block = high.shape[0]
+    count, _, lanes = mine.shape
     tile = block // lanes * number
-    n = CORES * chips
+    n = 2 * count
     queries = n * tokens // qlen
     padded = -(-queries // 128) * 128
     return pl.pallas_call(
-        functools.partial(score_kernel, number, qlen),
+        functools.partial(score_kernel, number, tokens, qlen),
         out_shape=pltpu.VMEM((n * tile, padded), F32),
-        in_specs=[pl.BlockSpec(memory_space=pltpu.SMEM)] + [VMEM] * 5,
+        in_specs=[pl.BlockSpec(memory_space=pltpu.SMEM)] + [VMEM] * 6,
         out_specs=VMEM,
-        scratch_shapes=[
-            pltpu.VMEM((chips * tokens, lanes), BF16),
-            pltpu.VMEM((n, tile, lanes), F32),
-            pltpu.VMEM((queries, coords), BF16),
-        ],
+        scratch_shapes=[pltpu.VMEM((n, tile, lanes), F32)],
         compiler_params=pltpu.CompilerParams(vmem_limit_bytes=20 * 2**20),
         name="score",
-    )(me, mine, theirs, made, high, low)
+    )(me, mine, theirs, *made, high, low)
 
 
 def finish_kernel(number, parts_ref, out_ref):
@@ -313,20 +323,26 @@
     out_ref[...] = total[:number, :queries] / jnp.sqrt(self_inf)
 
 
+def swap(x, k, n):
+    return lax.ppermute(x, "dp", [(i, i ^ k) for i in range(n)])
+
+
 def fast(n, train_hidden, train_cot, query_hidden, query_cot, proj_in, proj_out, hess_inv):
     number, qlen = train_hidden.shape[0], query_hidden.shape[1]
     tokens = query_hidden.shape[0] * qlen
     queries = n * query_hidden.shape[0]
-    chips = n // CORES
+    planes = n // INNER
     me = lax.axis_index("dp").astype(jnp.int32).reshape(1)
     messages = project(
-        chips, train_hidden, train_cot, query_hidden, query_cot, proj_in, proj_out
-    )
-    same_core = [[CORES * chip + core for chip in range(chips)] for core in range(CORES)]
-    mine = lax.all_to_all(messages, "dp", 0, 0, tiled=True, axis_index_groups=same_core)
-    theirs = lax.ppermute(mine, "dp", [(i, i ^ 1) for i in range(n)])
-    made, high, low = prepare(tokens, qlen, mine, hess_inv)
-    parts = score(me, number, qlen, tokens, mine, theirs, made, high, low)
+        me, planes, train_hidden, train_cot, query_hidden, query_cot, proj_in, proj_out
+    )
+    high, low = split(hess_inv, messages[0])
+    got = [messages[0]] + [swap(messages[k], INNER * k, n) for k in range(planes - 1, 0, -1)]
+    got, high, low = lax.optimization_barrier((jnp.stack(got), high, low))
+    mine = jnp.concatenate([got, swap(got, 2, n)], axis=0)
+    theirs = swap(mine, 1, n)
+    made = [prepare(tokens, qlen, hess_inv.shape[1], part) for part in (mine, theirs)]
+    parts = score(me, number, tokens, qlen, mine, theirs, made, high, low)
     parts = parts.reshape(n, -1, parts.shape[1])
     parts = lax.all_to_all(parts, "dp", 0, 0, tiled=True)
     return pl.pallas_call(
@@ -345,15 +361,17 @@
     tokens = query_hidden.shape[0] * qlen
     lanes = 2 * proj_in.shape[0]
     block = hess_inv.shape[0]
+    planes = n // INNER
     return (
-        n % CORES == 0
-        and n > CORES
+        n % INNER == 0
+        and planes > 1
+        and planes & (planes - 1) == 0
         and lanes == 128
         and block % lanes == 0
         and block // lanes * number == 8
         and tokens % 16 == 0
         and GROUP % (16 * qlen) == 0
-        and n // CORES * tokens % GROUP == 0
+        and n // 2 * tokens % GROUP == 0
     )
 
 

time: 38 us -> 36.5 us (0.961)
  blocking collectives: 25.8 us -> 11.1 us
  starting transfers between devices: 0.01 us -> 7.43 us
  waiting for transfers between devices: 0.01 us -> 6.03 us
    all_to_all x1 -> x0, blocking collectives: 15.5 us -> none  [fast(): lax.all_to_all(messages, 'dp', 0, 0, tiled=True, axis_index_groups=same_c...]
    ppermute x1 -> x5, starting transfers between devices: 0.01 us -> 7.43 us  [swap(): return lax.ppermute(x, 'dp', [(i, i ^ k) for i in range(n)])]
    ppermute x1 -> x5, waiting for transfers between devices: 0.01 us -> 6.03 us  [swap(): return lax.ppermute(x, 'dp', [(i, i ^ k) for i in range(n)])]
    all_to_all x1, blocking collectives: 10.3 us -> 11.1 us  [fast(): parts = lax.all_to_all(parts, 'dp', 0, 0, tiled=True)]
    pallas_call x3 -> x5, Pallas kernels: 11.4 us -> 11.1 us  [the longest x1 5.76 us: project(): pl.pallas_call(functools.partial(project_kernel, planes, number, length,...]
  transfers between devices with their start and end apart: 1 -> 5, of which waited for: 0 -> 3; matrix products, arithmetic and copies ran while one was open for 0% -> 0% of each run, Pallas kernels for 6% -> 8%
where the time goes in v3:
time: 36.5 us; the launch traced here: 36.4 us
  Pallas kernels  11.8 us (32%)
  blocking collectives  11.1 us (30%)
  starting transfers between devices  7.43 us (20%)
  waiting for transfers between devices  6.03 us (17%)
    all_to_all x1, blocking collectives, fast(): parts = lax.all_to_all(parts, 'dp', 0, 0, tiled=True)  11.1 us
    ppermute x5, starting transfers between devices, swap(): return lax.ppermute(x, 'dp', [(i, i ^ k) for i in range(n)])  7.43 us
    ppermute x5, waiting for transfers between devices, swap(): return lax.ppermute(x, 'dp', [(i, i ^ k) for i in range(n)])  6.03 us
    pallas_call x1, Pallas kernels, project(): pl.pallas_call(functools.partial(project_kernel, planes, number, length,...  5.76 us
    pallas_call x1, Pallas kernels, split(): pl.pallas_call(functools.partial(split_kernel, chunks), out_shape=[pltpu....  2.35 us
    pallas_call x1, Pallas kernels, score(): pl.pallas_call(functools.partial(score_kernel, number, tokens, qlen), out...  1.59 us
    pallas_call x2, Pallas kernels, prepare(): pl.pallas_call(functools.partial(prepare_kernel, qlen), out_shape=pltpu.V...  1.45 us
  transfers between devices with their start and end apart: 5, of which 3 were waited for; matrix products, arithmetic and copies ran while one was open for 0% of the time, Pallas kernels for 8%

profile of v3, /device:TPU:0, one launch (start us, length us, event | category | flops | bytes accessed | tf_op | source)
XLA Modules:
  0.0 36.4 jit_solution(14177242787849610181)
XLA Ops:
  0.0 5.8 %project.1 = (bf16[128,128]{1,0:T(8,128)(2,1)S(1)}, bf16[128,128]{1,0:T(8,128)(2,1)S(1)}, bf16[128,128]{1,0:T(8,128)(2,1)S(1)}, bf16[128,128]{1,0:T(8,128)(2,1)S(1)}) custom-call(s32[1]{0:T(128)} %bitcast.me_ref, bf16[160,14336]{1,0:T(8,128)(2,1)} %bitcast.12, bf16[160,4096]{1,0:T(8,128)(2,1)} %bitcast.14, bf16[96,14336]{1,0:T(8,128)(2,1)} %bitcast.13, ...), custom_call_target="tpu_custom_call" | custom-call | tf_op jit(solution)/shard_map/project/pallas_call | solution.py:140
  5.8 5.1 %collective-permute-start = (bf16[128,128]{1,0:T(8,128)(2,1)S(1)}, bf16[128,128]{1,0:T(8,128)(2,1)S(1)}, u32[]{:S(2)}, u32[]{:S(2)}) collective-permute-start(bf16[128,128]{1,0:T(8,128)(2,1)S(1)} %get-tuple-element.15), channel_id=1, source_target_pairs={{0,12},{1,13},{2,14},{3,15},{4,8},{5,9},{6,10},{7,11},{8,4},{9,5},... | collective-permute-start | bytes 98312 | tf_op jit(solution)/shard_map/ppermute | solution.py:327
  10.9 0.0 collective-permute-start.1
  10.9 0.6 %collective-permute-start.2 = (bf16[128,128]{1,0:T(8,128)(2,1)S(1)}, bf16[128,128]{1,0:T(8,128)(2,1)S(1)}, u32[]{:S(2)}, u32[]{:S(2)}) collective-permute-start(bf16[128,128]{1,0:T(8,128)(2,1)S(1)} %get-tuple-element.17), channel_id=1, source_target_pairs={{0,4},{1,5},{2,6},{3,7},{4,0},{5,1},{6,2},{7,3},{8,12},{9,13},{10,... | collective-permute-start | bytes 98312 | tf_op jit(solution)/shard_map/ppermute | solution.py:327
  11.5 2.4 %split.1 = (bf16[256,4096]{1,0:T(8,128)(2,1)S(1)}, bf16[256,4096]{1,0:T(8,128)(2,1)S(1)}) custom-call(f32[256,4096]{1,0:T(8,128)} %hess_ref.1, bf16[128,128]{1,0:T(8,128)(2,1)S(1)} %get-tuple-element.14.after_ref), custom_call_target="tpu_custom_call" | custom-call | tf_op jit(solution)/shard_map/split/pallas_call | solution.py:219
  13.9 0.0 collective-permute-done
  13.9 1.8 %collective-permute-done.1 = bf16[128,128]{1,0:T(8,128)(2,1)S(1)} collective-permute-done((bf16[128,128]{1,0:T(8,128)(2,1)S(1)}, bf16[128,128]{1,0:T(8,128)(2,1)S(1)}, u32[]{:S(2)}, u32[]{:S(2)}) %collective-permute-start.1) | collective-permute-done | bytes 32800 | tf_op jit(solution)/shard_map/ppermute | solution.py:327
  15.7 0.0 collective-permute-done.2
  15.7 1.6 %collective-permute-start.3 = (bf16[4,128,128]{2,1,0:T(8,128)(2,1)S(1)}, bf16[4,128,128]{2,1,0:T(8,128)(2,1)S(1)}, u32[]{:S(2)}, u32[]{:S(2)}) collective-permute-start(bf16[4,128,128]{2,1,0:T(8,128)(2,1)S(1)} %pad_maximum_fusion), channel_id=1, source_target_pairs={{0,2},{1,3},{2,0},{3,1},{4,6},{5,7},{6,4},{7,5},{8,10},{9,11},{10,... | collective-permute-start | bytes 393224 | tf_op jit(solution)/shard_map/ppermute | solution.py:327
  17.3 3.4 %collective-permute-done.3 = bf16[4,128,128]{2,1,0:T(8,128)(2,1)S(1)} collective-permute-done((bf16[4,128,128]{2,1,0:T(8,128)(2,1)S(1)}, bf16[4,128,128]{2,1,0:T(8,128)(2,1)S(1)}, u32[]{:S(2)}, u32[]{:S(2)}) %collective-permute-start.3) | collective-permute-done | bytes 131104 | tf_op jit(solution)/shard_map/ppermute | solution.py:327
  20.8 0.1 collective-permute-start.4
  20.9 0.7 %prepare.2.rest_0_ = bf16[48,4096]{1,0:T(8,128)(2,1)S(1)} custom-call(bf16[8,128,128]{2,1,0:T(8,128)(2,1)S(1)} %constant_dynamic-update-slice_fusion.mine_ref), custom_call_target="tpu_custom_call" | custom-call | tf_op jit(solution)/shard_map/prepare/pallas_call | solution.py:242
  21.6 0.8 %collective-permute-done.4.mine_ref.theirs_ref = bf16[8,128,128]{2,1,0:T(8,128)(2,1)S(1)} collective-permute-done((bf16[8,128,128]{2,1,0:T(8,128)(2,1)S(1)}, bf16[8,128,128]{2,1,0:T(8,128)(2,1)S(1)}, u32[]{:S(2)}, u32[]{:S(2)}) %collective-permute-start.4) | collective-permute-done | bytes 262176 | tf_op jit(solution)/shard_map/ppermute | solution.py:327
  22.4 0.7 %prepare.3.rest_1_ = bf16[48,4096]{1,0:T(8,128)(2,1)S(1)} custom-call(bf16[8,128,128]{2,1,0:T(8,128)(2,1)S(1)} %collective-permute-done.4.mine_ref.theirs_ref), custom_call_target="tpu_custom_call" | custom-call | tf_op jit(solution)/shard_map/prepare/pallas_call | solution.py:242
  23.1 1.6 %score.1 = f32[128,128]{1,0:T(8,128)S(1)} custom-call(s32[1]{0:T(128)} %bitcast.me_ref, bf16[8,128,128]{2,1,0:T(8,128)(2,1)S(1)} %constant_dynamic-update-slice_fusion.mine_ref, bf16[8,128,128]{2,1,0:T(8,128)(2,1)S(1)} %collective-permute-done.4.mine_ref.theirs_ref, bf16[48,4096]{1,0:T(8,128)(2,1)S(1)} %prepare.2.rest_0_, ...), custom_call_target="tpu_custom_call" | custom-call | tf_op jit(solution)/shard_map/score/pallas_call | solution.py:308
  24.7 11.1 %all_to_all.5.parts_ref = f32[16,8,128]{2,1,0:T(8,128)S(1)} all-to-all(f32[16,8,128]{2,1,0:T(8,128)S(1)} %bitcast.10), channel_id=1, replica_groups=mesh['groups'=2,'dp'=16] {'dp'}, dimensions={0} | all-to-all | bytes 131072 | tf_op jit(solution)/shard_map/all_to_all | solution.py:347
  35.8 0.6 %finish.1 = f32[4,96]{1,0:T(4,128)} custom-call(f32[16,8,128]{2,1,0:T(8,128)S(1)} %all_to_all.5.parts_ref), custom_call_target="tpu_custom_call" | custom-call | tf_op jit(solution)/shard_map/finish/pallas_call | solution.py:348
  (3 shorter events, 0.0 us)
Async XLA Ops:
  5.8 8.1 %collective-permute-start = (bf16[128,128]{1,0:T(8,128)(2,1)S(1)}, bf16[128,128]{1,0:T(8,128)(2,1)S(1)}, u32[]{:S(2)}, u32[]{:S(2)}) collective-permute-start(bf16[128,128]{1,0:T(8,128)(2,1)S(1)} %get-tuple-element.15), channel_id=1, source_target_pairs={{0,12},{1,13},{2,14},{3,15},{4,8},{5,9},{6,10},{7,11},{8,4},{9,5},... | collective-permute-start | bytes 98312 | tf_op jit(solution)/shard_map/ppermute | solution.py:327
  10.9 4.8 %collective-permute-start.1 = (bf16[128,128]{1,0:T(8,128)(2,1)S(1)}, bf16[128,128]{1,0:T(8,128)(2,1)S(1)}, u32[]{:S(2)}, u32[]{:S(2)}) collective-permute-start(bf16[128,128]{1,0:T(8,128)(2,1)S(1)} %get-tuple-element.16), channel_id=1, source_target_pairs={{0,8},{1,9},{2,10},{3,11},{4,12},{5,13},{6,14},{7,15},{8,0},{9,1},... | collective-permute-start | bytes 98312 | tf_op jit(solution)/shard_map/ppermute | solution.py:327
  10.9 4.8 %collective-permute-start.2 = (bf16[128,128]{1,0:T(8,128)(2,1)S(1)}, bf16[128,128]{1,0:T(8,128)(2,1)S(1)}, u32[]{:S(2)}, u32[]{:S(2)}) collective-permute-start(bf16[128,128]{1,0:T(8,128)(2,1)S(1)} %get-tuple-element.17), channel_id=1, source_target_pairs={{0,4},{1,5},{2,6},{3,7},{4,0},{5,1},{6,2},{7,3},{8,12},{9,13},{10,... | collective-permute-start | bytes 98312 | tf_op jit(solution)/shard_map/ppermute | solution.py:327
  15.7 5.0 %collective-permute-start.3 = (bf16[4,128,128]{2,1,0:T(8,128)(2,1)S(1)}, bf16[4,128,128]{2,1,0:T(8,128)(2,1)S(1)}, u32[]{:S(2)}, u32[]{:S(2)}) collective-permute-start(bf16[4,128,128]{2,1,0:T(8,128)(2,1)S(1)} %pad_maximum_fusion), channel_id=1, source_target_pairs={{0,2},{1,3},{2,0},{3,1},{4,6},{5,7},{6,4},{7,5},{8,10},{9,11},{10,... | collective-permute-start | bytes 393224 | tf_op jit(solution)/shard_map/ppermute | solution.py:327
  20.8 1.6 %collective-permute-start.4 = (bf16[8,128,128]{2,1,0:T(8,128)(2,1)S(1)}, bf16[8,128,128]{2,1,0:T(8,128)(2,1)S(1)}, u32[]{:S(2)}, u32[]{:S(2)}) collective-permute-start(bf16[8,128,128]{2,1,0:T(8,128)(2,1)S(1)} %constant_dynamic-update-slice_fusion.mine_ref), channel_id=1, source_target_pairs={{0,1},{1,0},{2,3},{3,2},{4,5},{5,4},{6,7},{7,6},{8,9},{9,8},{10,11... | collective-permute-start | bytes 786440 | tf_op jit(solution)/shard_map/ppermute | solution.py:327

commit v4 on v3

--- a/solution.py
+++ b/solution.py
@@ -12,7 +12,7 @@
 VMEM = pl.BlockSpec(memory_space=pltpu.VMEM)
 HBM = pl.BlockSpec(memory_space=pltpu.HBM)
 INNER = 4
-GROUP = 256
+GROUP = 128
 
 
 def dot(a, b):
@@ -170,32 +170,36 @@
     rank = lanes // 2
     pairs = rank // 2
     per = GROUP // qlen
+    groups = tok.shape[0] // GROUP
     pick = (iota((rank, lanes), 1) == iota((rank, lanes), 0) + rank).astype(BF16)
     shift = (iota((lanes, lanes), 1) == iota((lanes, lanes), 0) + rank).astype(BF16)
-    own = (iota((per, GROUP), 1) // qlen == iota((per, GROUP), 0)).astype(BF16)
+    own = iota((per, GROUP), 1) // qlen == iota((per, GROUP), 0)
     every = tok[...]
     outs = dot_nt(pick, every)
     moved = dot(every, shift).astype(BF16)
     still = jnp.where(iota(every.shape, 1) < rank, every, jnp.zeros_like(every))
-    for g in range(tok.shape[0] // GROUP):
+    made = []
+    for g in range(groups):
         cols = slice(g * GROUP, (g + 1) * GROUP)
-        left = []
+        left = [
+            jnp.concatenate(
+                [
+                    jnp.where(own, jnp.broadcast_to(outs[o : o + 1, cols], own.shape), 0.0)
+                    for o in range(half, rank, 2)
+                ],
+                axis=0,
+            ).astype(BF16)
+            for half in range(2)
+        ]
+        right = jnp.concatenate([still[cols], moved[cols]], axis=0)
+        made.append(dot(jnp.concatenate(left, axis=1), right) * (1.0 / qlen))
+    made += [jnp.zeros_like(made[0])] * (groups % 2)
+    for g in range(0, groups, 2):
         for pair in range(pairs):
-            left.append(
-                jnp.concatenate(
-                    [
-                        jnp.broadcast_to(outs[o : o + 1, cols], (per, GROUP)).astype(BF16) * own
-                        for o in (2 * pair, 2 * pair + 1)
-                    ],
-                    axis=1,
-                )
-            )
-        right = jnp.concatenate([still[cols], moved[cols]], axis=0)
-        made = (dot(jnp.concatenate(left, axis=0), right) * (1.0 / qlen)).astype(BF16)
-        for pair in range(pairs):
-            grads[g * per : (g + 1) * per, pair * lanes : (pair + 1) * lanes] = made[
-                pair * per : (pair + 1) * per, :
-            ]
+            rows = slice(pair * per, (pair + 1) * per)
+            grads[g * per : (g + 2) * per, pair * lanes : (pair + 1) * lanes] = jnp.concatenate(
+                [made[g][rows], made[g + 1][rows]], axis=0
+            ).astype(BF16)
 
 
 def split_kernel(chunks, hess_ref, after_ref, high_ref, low_ref, hess, sems):
@@ -230,60 +234,66 @@
     )(in_hbm(hess_inv), after)
 
 
-def prepare_kernel(qlen, mine_ref, grads_ref, tok):
-    tokens = tok.shape[0] // mine_ref.shape[0]
-    for slot in range(mine_ref.shape[0]):
-        tok[slot * tokens : (slot + 1) * tokens, :] = mine_ref[slot, :tokens, :]
+def prepare_kernel(tokens, qlen, *refs):
+    pieces, (grads_ref, tok) = refs[:-2], refs[-2:]
+    first = 0
+    for piece in pieces:
+        for part in range(piece.shape[0]):
+            tok[first : first + tokens, :] = piece[part, :tokens, :]
+            first += tokens
     build(tok, qlen, grads_ref)
 
 
-def prepare(tokens, qlen, coords, mine):
-    count, _, lanes = mine.shape
+def prepare(tokens, qlen, coords, *pieces):
+    total = sum(piece.shape[0] for piece in pieces) * tokens
+    rows = -(-total // (2 * GROUP)) * (2 * GROUP) // qlen
     return pl.pallas_call(
-        functools.partial(prepare_kernel, qlen),
-        out_shape=pltpu.VMEM((count * tokens // qlen, coords), BF16),
-        in_specs=[VMEM],
+        functools.partial(prepare_kernel, tokens, qlen),
+        out_shape=pltpu.VMEM((rows, coords), BF16),
+        in_specs=[VMEM] * len(pieces),
         out_specs=VMEM,
-        scratch_shapes=[pltpu.VMEM((count * tokens, lanes), BF16)],
+        scratch_shapes=[pltpu.VMEM((total, pieces[0].shape[2]), BF16)],
         compiler_params=pltpu.CompilerParams(vmem_limit_bytes=20 * 2**20),
         name="prepare",
-    )(mine)
-
-
-def score_kernel(number, tokens, qlen, me_ref, mine_ref, theirs_ref, *rest):
-    made_refs, (high_ref, low_ref, out_ref, train) = rest[:2], rest[2:]
+    )(*pieces)
+
+
+def score_kernel(number, tokens, qlen, slots, rows_of, me_ref, *refs):
+    pieces, refs = refs[: len(slots)], refs[len(slots) :]
+    made_refs, (high_ref, low_ref, out_ref, train) = refs[: len(rows_of)], refs[len(rows_of) :]
     me = me_ref[0]
     block = high_ref.shape[0]
-    count, _, lanes = mine_ref.shape
-    planes = count // (INNER // 2)
+    n, tile, lanes = train.shape
     each = tokens // qlen
+    queries = n * each
     local = block // lanes
-    tile = local * number
     inner = me % INNER
 
-    def source(slot):
-        by_two, plane = slot // planes % 2, (planes - slot % planes) % planes
-        return me ^ (plane * INNER + by_two * 2 + slot // count)
-
-    for slot in range(count):
-        for ref, first in ((mine_ref, 0), (theirs_ref, count)):
-            share = ref[slot, tokens:, :].astype(F32)
+    for piece, froms in zip(pieces, slots):
+        for part, slot in enumerate(froms):
+            share = piece[part, tokens:, :].astype(F32)
             picked = share[:tile]
             for j in range(1, INNER):
                 picked = jnp.where(inner == j, share[j * tile : (j + 1) * tile], picked)
-            train[source(first + slot)] = picked
+            train[me ^ slot] = picked
     grads = jnp.concatenate([ref[...] for ref in made_refs], axis=0)
-    queries = grads.shape[0]
     precond = dot_nt(high_ref[...], grads) + dot_nt(low_ref[...], grads)
-    row, col = iota((queries, queries), 0), iota((queries, queries), 1)
-    order = source(row // each) * each + row % each == col
+    row, col = iota((grads.shape[0], queries), 0), iota((grads.shape[0], queries), 1)
+    place = jnp.full(row.shape, -1, jnp.int32)
+    first = 0
+    for ref, froms in zip(made_refs, rows_of):
+        for i, slot in enumerate(froms):
+            at = row - (first + i * each)
+            place = jnp.where((at >= 0) & (at < each), (me ^ slot) * each + at, place)
+        first += ref.shape[0]
+    order = place == col
     precond = dot(precond.astype(BF16), order.astype(BF16)).astype(BF16)
 
     cols = pl.ds(pl.multiple_of(me * block, block), block)
     square = dot(jnp.concatenate([ref[:, cols] for ref in made_refs], axis=0), precond)
     self_inf = jnp.sum(jnp.where(order, square, 0.0), axis=0, keepdims=True)
 
-    rows = 2 * count * tile
+    rows = n * tile
     t = train[...].reshape(rows, lanes)
     where = iota((rows, lanes), 0) % tile // number
     wide = jnp.concatenate(
@@ -298,22 +308,22 @@
     out_ref[:, :queries] = raw
 
 
-def score(me, number, tokens, qlen, mine, theirs, made, high, low):
+def score(me, number, tokens, qlen, pieces, slots, made, rows_of, high, low):
     block = high.shape[0]
-    count, _, lanes = mine.shape
+    lanes = pieces[0].shape[2]
     tile = block // lanes * number
-    n = 2 * count
+    n = sum(map(len, slots))
     queries = n * tokens // qlen
     padded = -(-queries // 128) * 128
     return pl.pallas_call(
-        functools.partial(score_kernel, number, tokens, qlen),
+        functools.partial(score_kernel, number, tokens, qlen, slots, rows_of),
         out_shape=pltpu.VMEM((n * tile, padded), F32),
-        in_specs=[pl.BlockSpec(memory_space=pltpu.SMEM)] + [VMEM] * 6,
+        in_specs=[pl.BlockSpec(memory_space=pltpu.SMEM)] + [VMEM] * (len(pieces) + len(made) + 2),
         out_specs=VMEM,
         scratch_shapes=[pltpu.VMEM((n, tile, lanes), F32)],
         compiler_params=pltpu.CompilerParams(vmem_limit_bytes=20 * 2**20),
         name="score",
-    )(me, mine, theirs, *made, high, low)
+    )(me, *pieces, *made, high, low)
 
 
 def finish_kernel(number, parts_ref, out_ref):
@@ -336,13 +346,22 @@
     messages = project(
         me, planes, train_hidden, train_cot, query_hidden, query_cot, proj_in, proj_out
     )
-    high, low = split(hess_inv, messages[0])
-    got = [messages[0]] + [swap(messages[k], INNER * k, n) for k in range(planes - 1, 0, -1)]
-    got, high, low = lax.optimization_barrier((jnp.stack(got), high, low))
-    mine = jnp.concatenate([got, swap(got, 2, n)], axis=0)
-    theirs = swap(mine, 1, n)
-    made = [prepare(tokens, qlen, hess_inv.shape[1], part) for part in (mine, theirs)]
-    parts = score(me, number, tokens, qlen, mine, theirs, made, high, low)
+    coords = hess_inv.shape[1]
+    others = [INNER * k for k in range(planes - 1, 0, -1)]
+    far = [swap(messages[slot // INNER], slot, n) for slot in others]
+    own_two = swap(messages[0], 2, n)
+    by_plane = jnp.stack([messages[0]] + far)
+    by_plane_one = swap(by_plane, 1, n)
+    by_two = jnp.concatenate([own_two[None], swap(by_plane[1:], 2, n)], axis=0)
+    high, low = split(hess_inv, by_plane)
+    made = [prepare(tokens, qlen, coords, by_plane, by_plane_one)]
+    by_two, high, low = lax.optimization_barrier((by_two, high, low))
+    by_two_one = swap(by_two, 1, n)
+    made += [prepare(tokens, qlen, coords, by_two), prepare(tokens, qlen, coords, by_two_one)]
+    slots = [[first ^ slot for slot in [0] + others] for first in (0, 1, 2, 3)]
+    rows_of = [slots[0] + slots[1], slots[2], slots[3]]
+    pieces = [by_plane, by_plane_one, by_two, by_two_one]
+    parts = score(me, number, tokens, qlen, pieces, slots, made, rows_of, high, low)
     parts = parts.reshape(n, -1, parts.shape[1])
     parts = lax.all_to_all(parts, "dp", 0, 0, tiled=True)
     return pl.pallas_call(
@@ -370,8 +389,9 @@
         and block % lanes == 0
         and block // lanes * number == 8
         and tokens % 16 == 0
-        and GROUP % (16 * qlen) == 0
-        and n // 2 * tokens % GROUP == 0
+        and GROUP == 8 * qlen
+        and planes * tokens % GROUP == 0
+        and 2 * planes * tokens % (2 * GROUP) == 0
     )
 
 

time: 36.5 us -> 35.7 us (0.978)
  waiting for transfers between devices: 6.03 us -> 3.39 us
  starting transfers between devices: 7.43 us -> 9.15 us
    ppermute x5 -> x7, waiting for transfers between devices: 6.03 us -> 3.39 us  [swap(): return lax.ppermute(x, 'dp', [(i, i ^ k) for i in range(n)])]
    ppermute x5 -> x7, starting transfers between devices: 7.43 us -> 9.15 us  [swap(): return lax.ppermute(x, 'dp', [(i, i ^ k) for i in range(n)])]
    pallas_call x3 -> x4, Pallas kernels: 3.04 us -> 3.11 us  [the longest x1 1.6 us: score(): pl.pallas_call(functools.partial(score_kernel, number, tokens, qlen, slot...]
  transfers between devices with their start and end apart: 5 -> 7, of which waited for: 3 -> 3; matrix products, arithmetic and copies ran while one was open for 0% -> 0% of each run, Pallas kernels for 8% -> 10%
where the time goes in v4:
time: 35.7 us; the launch traced here: 35.6 us
  Pallas kernels  11.8 us (33%)
  blocking collectives  11.1 us (31%)
  starting transfers between devices  9.15 us (26%)
  waiting for transfers between devices  3.39 us (9%)
    all_to_all x1, blocking collectives, fast(): parts = lax.all_to_all(parts, 'dp', 0, 0, tiled=True)  11.1 us
    ppermute x7, starting transfers between devices, swap(): return lax.ppermute(x, 'dp', [(i, i ^ k) for i in range(n)])  9.15 us
    pallas_call x1, Pallas kernels, project(): pl.pallas_call(functools.partial(project_kernel, planes, number, length,...  5.76 us
    ppermute x7, waiting for transfers between devices, swap(): return lax.ppermute(x, 'dp', [(i, i ^ k) for i in range(n)])  3.39 us
    pallas_call x1, Pallas kernels, split(): pl.pallas_call(functools.partial(split_kernel, chunks), out_shape=[pltpu....  2.36 us
    pallas_call x1, Pallas kernels, score(): pl.pallas_call(functools.partial(score_kernel, number, tokens, qlen, slot...  1.6 us
    pallas_call x3, Pallas kernels, prepare(): pl.pallas_call(functools.partial(prepare_kernel, tokens, qlen), out_shape...  1.51 us
  transfers between devices with their start and end apart: 7, of which 3 were waited for; matrix products, arithmetic and copies ran while one was open for 0% of the time, Pallas kernels for 10%

profile of v4, /device:TPU:0, one launch (start us, length us, event | category | flops | bytes accessed | tf_op | source)
XLA Modules:
  0.0 35.6 jit_solution(623933521792033335)
XLA Ops:
  0.0 5.8 %project.1 = (bf16[128,128]{1,0:T(8,128)(2,1)S(1)}, bf16[128,128]{1,0:T(8,128)(2,1)S(1)}, bf16[128,128]{1,0:T(8,128)(2,1)S(1)}, bf16[128,128]{1,0:T(8,128)(2,1)S(1)}) custom-call(s32[1]{0:T(128)} %bitcast.me_ref, bf16[160,14336]{1,0:T(8,128)(2,1)} %bitcast.13, bf16[160,4096]{1,0:T(8,128)(2,1)} %bitcast.15, bf16[96,14336]{1,0:T(8,128)(2,1)} %bitcast.14, ...), custom_call_target="tpu_custom_call" | custom-call | tf_op jit(solution)/shard_map/project/pallas_call | solution.py:140
  5.8 5.1 %collective-permute-start = (bf16[128,128]{1,0:T(8,128)(2,1)S(1)}, bf16[128,128]{1,0:T(8,128)(2,1)S(1)}, u32[]{:S(2)}, u32[]{:S(2)}) collective-permute-start(bf16[128,128]{1,0:T(8,128)(2,1)S(1)} %get-tuple-element.15), channel_id=1, source_target_pairs={{0,12},{1,13},{2,14},{3,15},{4,8},{5,9},{6,10},{7,11},{8,4},{9,5},... | collective-permute-start | bytes 98312 | tf_op jit(solution)/shard_map/ppermute | solution.py:337
  10.9 0.0 collective-permute-start.1
  10.9 0.6 %collective-permute-start.2 = (bf16[128,128]{1,0:T(8,128)(2,1)S(1)}, bf16[128,128]{1,0:T(8,128)(2,1)S(1)}, u32[]{:S(2)}, u32[]{:S(2)}) collective-permute-start(bf16[128,128]{1,0:T(8,128)(2,1)S(1)} %get-tuple-element.17), channel_id=1, source_target_pairs={{0,4},{1,5},{2,6},{3,7},{4,0},{5,1},{6,2},{7,3},{8,12},{9,13},{10,... | collective-permute-start | bytes 98312 | tf_op jit(solution)/shard_map/ppermute | solution.py:337
  11.5 1.6 %collective-permute-start.4 = (bf16[128,128]{1,0:T(8,128)(2,1)S(1)}, bf16[128,128]{1,0:T(8,128)(2,1)S(1)}, u32[]{:S(2)}, u32[]{:S(2)}) collective-permute-start(bf16[128,128]{1,0:T(8,128)(2,1)S(1)} %get-tuple-element.14), channel_id=1, source_target_pairs={{0,2},{1,3},{2,0},{3,1},{4,6},{5,7},{6,4},{7,5},{8,10},{9,11},{10,... | collective-permute-start | bytes 98312 | tf_op jit(solution)/shard_map/ppermute | solution.py:337
  13.2 0.0 collective-permute-done
  13.2 2.5 %collective-permute-done.1 = bf16[128,128]{1,0:T(8,128)(2,1)S(1)} collective-permute-done((bf16[128,128]{1,0:T(8,128)(2,1)S(1)}, bf16[128,128]{1,0:T(8,128)(2,1)S(1)}, u32[]{:S(2)}, u32[]{:S(2)}) %collective-permute-start.1) | collective-permute-done | bytes 32800 | tf_op jit(solution)/shard_map/ppermute | solution.py:337
  15.7 0.0 collective-permute-done.2
  15.7 1.6 %collective-permute-start.5 = (bf16[3,128,128]{2,1,0:T(8,128)(2,1)S(1)}, bf16[3,128,128]{2,1,0:T(8,128)(2,1)S(1)}, u32[]{:S(2)}, u32[]{:S(2)}) collective-permute-start(bf16[3,128,128]{2,1,0:T(8,128)(2,1)S(1)} %pad_maximum_fusion.2), channel_id=1, source_target_pairs={{0,2},{1,3},{2,0},{3,1},{4,6},{5,7},{6,4},{7,5},{8,10},{9,11},{10,... | collective-permute-start | bytes 294920 | tf_op jit(solution)/shard_map/ppermute | solution.py:337
  17.3 0.1 collective-permute-start.3
  17.4 2.4 %split.1 = (bf16[256,4096]{1,0:T(8,128)(2,1)S(1)}, bf16[256,4096]{1,0:T(8,128)(2,1)S(1)}) custom-call(f32[256,4096]{1,0:T(8,128)} %hess_ref.1, bf16[4,128,128]{2,1,0:T(8,128)(2,1)S(1)} %pad_maximum_fusion.after_ref.refs_0_), custom_call_target="tpu_custom_call" | custom-call | tf_op jit(solution)/shard_map/split/pallas_call | solution.py:223
  19.8 0.0 collective-permute-done.4
  19.8 0.6 %collective-permute-done.5 = bf16[3,128,128]{2,1,0:T(8,128)(2,1)S(1)} collective-permute-done((bf16[3,128,128]{2,1,0:T(8,128)(2,1)S(1)}, bf16[3,128,128]{2,1,0:T(8,128)(2,1)S(1)}, u32[]{:S(2)}, u32[]{:S(2)}) %collective-permute-start.5) | collective-permute-done | bytes 98336 | tf_op jit(solution)/shard_map/ppermute | solution.py:337
  20.4 0.1 collective-permute-start.6
  20.5 0.4 %prepare.4.refs_5_ = bf16[32,4096]{1,0:T(8,128)(2,1)S(1)} custom-call(bf16[4,128,128]{2,1,0:T(8,128)(2,1)S(1)} %pad_maximum_fusion.1.refs_0_.refs_2_), custom_call_target="tpu_custom_call" | custom-call | tf_op jit(solution)/shard_map/prepare/pallas_call | solution.py:250
  21.0 0.0 collective-permute-done.3.refs_1_
  21.0 0.6 %prepare.3.refs_4_ = bf16[48,4096]{1,0:T(8,128)(2,1)S(1)} custom-call(bf16[4,128,128]{2,1,0:T(8,128)(2,1)S(1)} %pad_maximum_fusion.after_ref.refs_0_, bf16[4,128,128]{2,1,0:T(8,128)(2,1)S(1)} %collective-permute-done.3.refs_1_), custom_call_target="tpu_custom_call" | custom-call | tf_op jit(solution)/shard_map/prepare/pallas_call | solution.py:250
  21.6 0.2 collective-permute-done.6.refs_0_.refs_3_
  21.8 0.4 %prepare.5.refs_6_ = bf16[32,4096]{1,0:T(8,128)(2,1)S(1)} custom-call(bf16[4,128,128]{2,1,0:T(8,128)(2,1)S(1)} %collective-permute-done.6.refs_0_.refs_3_), custom_call_target="tpu_custom_call" | custom-call | tf_op jit(solution)/shard_map/prepare/pallas_call | solution.py:250
  22.3 1.6 %score.1 = f32[128,128]{1,0:T(8,128)S(1)} custom-call(s32[1]{0:T(128)} %bitcast.me_ref, bf16[4,128,128]{2,1,0:T(8,128)(2,1)S(1)} %pad_maximum_fusion.after_ref.refs_0_, bf16[4,128,128]{2,1,0:T(8,128)(2,1)S(1)} %collective-permute-done.3.refs_1_, bf16[4,128,128]{2,1,0:T(8,128)(2,1)S(1)} %pad_maximum_fusion.1.refs_0_.refs_2_, ...), custom_call_target="tpu_custom_call" | custom-call | tf_op jit(solution)/shard_map/score/pallas_call | solution.py:318
  23.9 11.1 %all_to_all.5.parts_ref = f32[16,8,128]{2,1,0:T(8,128)S(1)} all-to-all(f32[16,8,128]{2,1,0:T(8,128)S(1)} %bitcast.11), channel_id=1, replica_groups=mesh['groups'=2,'dp'=16] {'dp'}, dimensions={0} | all-to-all | bytes 131072 | tf_op jit(solution)/shard_map/all_to_all | solution.py:366
  35.0 0.6 %finish.1 = f32[4,96]{1,0:T(4,128)} custom-call(f32[16,8,128]{2,1,0:T(8,128)S(1)} %all_to_all.5.parts_ref), custom_call_target="tpu_custom_call" | custom-call | tf_op jit(solution)/shard_map/finish/pallas_call | solution.py:367
  (3 shorter events, 0.0 us)
Async XLA Ops:
  5.8 7.4 %collective-permute-start = (bf16[128,128]{1,0:T(8,128)(2,1)S(1)}, bf16[128,128]{1,0:T(8,128)(2,1)S(1)}, u32[]{:S(2)}, u32[]{:S(2)}) collective-permute-start(bf16[128,128]{1,0:T(8,128)(2,1)S(1)} %get-tuple-element.15), channel_id=1, source_target_pairs={{0,12},{1,13},{2,14},{3,15},{4,8},{5,9},{6,10},{7,11},{8,4},{9,5},... | collective-permute-start | bytes 98312 | tf_op jit(solution)/shard_map/ppermute | solution.py:337
  10.9 4.8 %collective-permute-start.1 = (bf16[128,128]{1,0:T(8,128)(2,1)S(1)}, bf16[128,128]{1,0:T(8,128)(2,1)S(1)}, u32[]{:S(2)}, u32[]{:S(2)}) collective-permute-start(bf16[128,128]{1,0:T(8,128)(2,1)S(1)} %get-tuple-element.16), channel_id=1, source_target_pairs={{0,8},{1,9},{2,10},{3,11},{4,12},{5,13},{6,14},{7,15},{8,0},{9,1},... | collective-permute-start | bytes 98312 | tf_op jit(solution)/shard_map/ppermute | solution.py:337
  10.9 4.8 %collective-permute-start.2 = (bf16[128,128]{1,0:T(8,128)(2,1)S(1)}, bf16[128,128]{1,0:T(8,128)(2,1)S(1)}, u32[]{:S(2)}, u32[]{:S(2)}) collective-permute-start(bf16[128,128]{1,0:T(8,128)(2,1)S(1)} %get-tuple-element.17), channel_id=1, source_target_pairs={{0,4},{1,5},{2,6},{3,7},{4,0},{5,1},{6,2},{7,3},{8,12},{9,13},{10,... | collective-permute-start | bytes 98312 | tf_op jit(solution)/shard_map/ppermute | solution.py:337
  11.5 8.2 %collective-permute-start.4 = (bf16[128,128]{1,0:T(8,128)(2,1)S(1)}, bf16[128,128]{1,0:T(8,128)(2,1)S(1)}, u32[]{:S(2)}, u32[]{:S(2)}) collective-permute-start(bf16[128,128]{1,0:T(8,128)(2,1)S(1)} %get-tuple-element.14), channel_id=1, source_target_pairs={{0,2},{1,3},{2,0},{3,1},{4,6},{5,7},{6,4},{7,5},{8,10},{9,11},{10,... | collective-permute-start | bytes 98312 | tf_op jit(solution)/shard_map/ppermute | solution.py:337
  15.7 4.7 %collective-permute-start.5 = (bf16[3,128,128]{2,1,0:T(8,128)(2,1)S(1)}, bf16[3,128,128]{2,1,0:T(8,128)(2,1)S(1)}, u32[]{:S(2)}, u32[]{:S(2)}) collective-permute-start(bf16[3,128,128]{2,1,0:T(8,128)(2,1)S(1)} %pad_maximum_fusion.2), channel_id=1, source_target_pairs={{0,2},{1,3},{2,0},{3,1},{4,6},{5,7},{6,4},{7,5},{8,10},{9,11},{10,... | collective-permute-start | bytes 294920 | tf_op jit(solution)/shard_map/ppermute | solution.py:337
  17.3 3.6 %collective-permute-start.3 = (bf16[4,128,128]{2,1,0:T(8,128)(2,1)S(1)}, bf16[4,128,128]{2,1,0:T(8,128)(2,1)S(1)}, u32[]{:S(2)}, u32[]{:S(2)}) collective-permute-start(bf16[4,128,128]{2,1,0:T(8,128)(2,1)S(1)} %pad_maximum_fusion.after_ref.refs_0_), channel_id=1, source_target_pairs={{0,1},{1,0},{2,3},{3,2},{4,5},{5,4},{6,7},{7,6},{8,9},{9,8},{10,11... | collective-permute-start | bytes 393224 | tf_op jit(solution)/shard_map/ppermute | solution.py:337
  20.4 1.4 %collective-permute-start.6 = (bf16[4,128,128]{2,1,0:T(8,128)(2,1)S(1)}, bf16[4,128,128]{2,1,0:T(8,128)(2,1)S(1)}, u32[]{:S(2)}, u32[]{:S(2)}) collective-permute-start(bf16[4,128,128]{2,1,0:T(8,128)(2,1)S(1)} %pad_maximum_fusion.1.refs_0_.refs_2_), channel_id=1, source_target_pairs={{0,1},{1,0},{2,3},{3,2},{4,5},{5,4},{6,7},{7,6},{8,9},{9,8},{10,11... | collective-permute-start | bytes 393224 | tf_op jit(solution)/shard_map/ppermute | solution.py:337

commit v5 on v4

--- a/solution.py
+++ b/solution.py
@@ -119,15 +119,20 @@
     for half in range(2):
         right = jnp.where(lane // rank == half, spread, jnp.zeros_like(spread))
         total += dot(lefts[half], right)
-    grads[...] = (total * (1.0 / length)).astype(BF16)
+    grads[...] = total * (1.0 / length)
     message = jnp.concatenate([q_in, q_out], axis=1).astype(BF16)
 
-    plane = me_ref[0] // INNER
-    share = rows // planes
+    plane, inner = me_ref[0] // INNER, me_ref[0] % INNER
+    tile = rows // planes // INNER
+    edge = 2 * tile
     for k in range(planes):
-        outs[k][:queries, :] = message
-        first = pl.multiple_of((plane ^ k) * share, share)
-        outs[k][queries:, :] = grads[pl.ds(first, share), :]
+        shares = [
+            grads[pl.ds(pl.multiple_of(((plane ^ k) * INNER + (inner ^ j)) * tile, tile), tile), :]
+            for j in (0, 1, 3, 2)
+        ]
+        outs[k][:edge, :] = jnp.concatenate(shares[:2], axis=0).astype(BF16)
+        outs[k][edge : edge + queries, :] = message
+        outs[k][edge + queries :, :] = jnp.concatenate(shares[2:], axis=0).astype(BF16)
 
 
 def project(me, planes, train_hidden, train_cot, query_hidden, query_cot, proj_in, proj_out):
@@ -149,7 +154,7 @@
             pltpu.VMEM((queries, width), BF16),
             pltpu.VMEM((rank, inner), BF16),
             pltpu.VMEM((rank, width), BF16),
-            pltpu.VMEM((rows, 2 * rank), BF16),
+            pltpu.VMEM((rows, 2 * rank), F32),
             pltpu.SemaphoreType.DMA((3 * len(widths) + 3,)),
         ],
         compiler_params=pltpu.CompilerParams(vmem_limit_bytes=20 * 2**20),
@@ -234,21 +239,21 @@
     )(in_hbm(hess_inv), after)
 
 
-def prepare_kernel(tokens, qlen, *refs):
+def prepare_kernel(tokens, qlen, starts, *refs):
     pieces, (grads_ref, tok) = refs[:-2], refs[-2:]
     first = 0
-    for piece in pieces:
+    for piece, start in zip(pieces, starts):
         for part in range(piece.shape[0]):
-            tok[first : first + tokens, :] = piece[part, :tokens, :]
+            tok[first : first + tokens, :] = piece[part, start : start + tokens, :]
             first += tokens
     build(tok, qlen, grads_ref)
 
 
-def prepare(tokens, qlen, coords, *pieces):
+def prepare(tokens, qlen, coords, starts, *pieces):
     total = sum(piece.shape[0] for piece in pieces) * tokens
     rows = -(-total // (2 * GROUP)) * (2 * GROUP) // qlen
     return pl.pallas_call(
-        functools.partial(prepare_kernel, tokens, qlen),
+        functools.partial(prepare_kernel, tokens, qlen, starts),
         out_shape=pltpu.VMEM((rows, coords), BF16),
         in_specs=[VMEM] * len(pieces),
         out_specs=VMEM,
@@ -258,24 +263,19 @@
     )(*pieces)
 
 
-def score_kernel(number, tokens, qlen, slots, rows_of, me_ref, *refs):
+def score_kernel(number, each, slots, shares, rows_of, me_ref, *refs):
     pieces, refs = refs[: len(slots)], refs[len(slots) :]
     made_refs, (high_ref, low_ref, out_ref, train) = refs[: len(rows_of)], refs[len(rows_of) :]
     me = me_ref[0]
     block = high_ref.shape[0]
     n, tile, lanes = train.shape
-    each = tokens // qlen
     queries = n * each
     local = block // lanes
-    inner = me % INNER
-
-    for piece, froms in zip(pieces, slots):
+
+    for piece, froms, (first, second) in zip(pieces, slots, shares):
         for part, slot in enumerate(froms):
-            share = piece[part, tokens:, :].astype(F32)
-            picked = share[:tile]
-            for j in range(1, INNER):
-                picked = jnp.where(inner == j, share[j * tile : (j + 1) * tile], picked)
-            train[me ^ slot] = picked
+            both = piece[part, first : first + 2 * tile, :].astype(F32)
+            train[me ^ slot] = both[tile:] if second else both[:tile]
     grads = jnp.concatenate([ref[...] for ref in made_refs], axis=0)
     precond = dot_nt(high_ref[...], grads) + dot_nt(low_ref[...], grads)
     row, col = iota((grads.shape[0], queries), 0), iota((grads.shape[0], queries), 1)
@@ -308,15 +308,15 @@
     out_ref[:, :queries] = raw
 
 
-def score(me, number, tokens, qlen, pieces, slots, made, rows_of, high, low):
+def score(me, number, each, pieces, slots, shares, made, rows_of, high, low):
     block = high.shape[0]
     lanes = pieces[0].shape[2]
     tile = block // lanes * number
     n = sum(map(len, slots))
-    queries = n * tokens // qlen
+    queries = n * each
     padded = -(-queries // 128) * 128
     return pl.pallas_call(
-        functools.partial(score_kernel, number, tokens, qlen, slots, rows_of),
+        functools.partial(score_kernel, number, each, slots, shares, rows_of),
         out_shape=pltpu.VMEM((n * tile, padded), F32),
         in_specs=[pl.BlockSpec(memory_space=pltpu.SMEM)] + [VMEM] * (len(pieces) + len(made) + 2),
         out_specs=VMEM,
@@ -349,19 +349,22 @@
     coords = hess_inv.shape[1]
     others = [INNER * k for k in range(planes - 1, 0, -1)]
     far = [swap(messages[slot // INNER], slot, n) for slot in others]
-    own_two = swap(messages[0], 2, n)
+    edge = (messages[0].shape[0] - tokens) // 2
+    own_two = swap(messages[0][edge:], 2, n)
     by_plane = jnp.stack([messages[0]] + far)
-    by_plane_one = swap(by_plane, 1, n)
-    by_two = jnp.concatenate([own_two[None], swap(by_plane[1:], 2, n)], axis=0)
+    by_plane_one = swap(by_plane[:, :-edge], 1, n)
+    by_two = jnp.concatenate([own_two[None], swap(jnp.stack(far)[:, edge:], 2, n)], axis=0)
     high, low = split(hess_inv, by_plane)
-    made = [prepare(tokens, qlen, coords, by_plane, by_plane_one)]
+    made = [prepare(tokens, qlen, coords, [edge, edge], by_plane, by_plane_one)]
     by_two, high, low = lax.optimization_barrier((by_two, high, low))
     by_two_one = swap(by_two, 1, n)
-    made += [prepare(tokens, qlen, coords, by_two), prepare(tokens, qlen, coords, by_two_one)]
+    made += [prepare(tokens, qlen, coords, [0], piece) for piece in (by_two, by_two_one)]
     slots = [[first ^ slot for slot in [0] + others] for first in (0, 1, 2, 3)]
     rows_of = [slots[0] + slots[1], slots[2], slots[3]]
     pieces = [by_plane, by_plane_one, by_two, by_two_one]
-    parts = score(me, number, tokens, qlen, pieces, slots, made, rows_of, high, low)
+    shares = [(0, False), (0, True), (tokens, True), (tokens, False)]
+    each = tokens // qlen
+    parts = score(me, number, each, pieces, slots, shares, made, rows_of, high, low)
     parts = parts.reshape(n, -1, parts.shape[1])
     parts = lax.all_to_all(parts, "dp", 0, 0, tiled=True)
     return pl.pallas_call(

time: 35.7 us -> 35.6 us (level)
  no operation moved by 1% of the time
where the time goes in v5:
time: 35.6 us; the launch traced here: 35.4 us
  Pallas kernels  11.8 us (33%)
  blocking collectives  11.1 us (31%)
  starting transfers between devices  9.17 us (26%)
  waiting for transfers between devices  3.18 us (9%)
    all_to_all x1, blocking collectives, fast(): parts = lax.all_to_all(parts, 'dp', 0, 0, tiled=True)  11.1 us
    ppermute x7, starting transfers between devices, swap(): return lax.ppermute(x, 'dp', [(i, i ^ k) for i in range(n)])  9.17 us
    pallas_call x1, Pallas kernels, project(): pl.pallas_call(functools.partial(project_kernel, planes, number, length,...  5.76 us
    ppermute x7, waiting for transfers between devices, swap(): return lax.ppermute(x, 'dp', [(i, i ^ k) for i in range(n)])  3.18 us
    pallas_call x1, Pallas kernels, split(): pl.pallas_call(functools.partial(split_kernel, chunks), out_shape=[pltpu....  2.36 us
    pallas_call x1, Pallas kernels, score(): pl.pallas_call(functools.partial(score_kernel, number, each, slots, share...  1.59 us
    pallas_call x3, Pallas kernels, prepare(): pl.pallas_call(functools.partial(prepare_kernel, tokens, qlen, starts), o...  1.52 us
  transfers between devices with their start and end apart: 7, of which 3 were waited for; matrix products, arithmetic and copies ran while one was open for 0% of the time, Pallas kernels for 10%

profile of v5, /device:TPU:0, one launch (start us, length us, event | category | flops | bytes accessed | tf_op | source)
XLA Modules:
  0.0 35.4 jit_solution(1831013887920227059)
XLA Ops:
  0.0 5.8 %project.1 = (bf16[128,128]{1,0:T(8,128)(2,1)S(1)}, bf16[128,128]{1,0:T(8,128)(2,1)S(1)}, bf16[128,128]{1,0:T(8,128)(2,1)S(1)}, bf16[128,128]{1,0:T(8,128)(2,1)S(1)}) custom-call(s32[1]{0:T(128)} %bitcast.me_ref, bf16[160,14336]{1,0:T(8,128)(2,1)} %bitcast.13, bf16[160,4096]{1,0:T(8,128)(2,1)} %bitcast.15, bf16[96,14336]{1,0:T(8,128)(2,1)} %bitcast.14, ...), custom_call_target="tpu_custom_call" | custom-call | tf_op jit(solution)/shard_map/project/pallas_call | solution.py:145
  5.8 5.1 %collective-permute-start = (bf16[128,128]{1,0:T(8,128)(2,1)S(1)}, bf16[128,128]{1,0:T(8,128)(2,1)S(1)}, u32[]{:S(2)}, u32[]{:S(2)}) collective-permute-start(bf16[128,128]{1,0:T(8,128)(2,1)S(1)} %get-tuple-element.15), channel_id=1, source_target_pairs={{0,12},{1,13},{2,14},{3,15},{4,8},{5,9},{6,10},{7,11},{8,4},{9,5},... | collective-permute-start | bytes 98312 | tf_op jit(solution)/shard_map/ppermute | solution.py:337
  10.9 0.0 collective-permute-start.1
  10.9 0.6 %collective-permute-start.2 = (bf16[128,128]{1,0:T(8,128)(2,1)S(1)}, bf16[128,128]{1,0:T(8,128)(2,1)S(1)}, u32[]{:S(2)}, u32[]{:S(2)}) collective-permute-start(bf16[128,128]{1,0:T(8,128)(2,1)S(1)} %get-tuple-element.17), channel_id=1, source_target_pairs={{0,4},{1,5},{2,6},{3,7},{4,0},{5,1},{6,2},{7,3},{8,12},{9,13},{10,... | collective-permute-start | bytes 98312 | tf_op jit(solution)/shard_map/ppermute | solution.py:337
  11.5 1.6 %collective-permute-start.4 = (bf16[112,128]{1,0:T(8,128)(2,1)S(1)}, bf16[112,128]{1,0:T(8,128)(2,1)S(1)}, u32[]{:S(2)}, u32[]{:S(2)}) collective-permute-start(bf16[112,128]{1,0:T(8,128)(2,1)S(1)} %slice.10), channel_id=1, source_target_pairs={{0,2},{1,3},{2,0},{3,1},{4,6},{5,7},{6,4},{7,5},{8,10},{9,11},{10,... | collective-permute-start | bytes 86024 | tf_op jit(solution)/shard_map/ppermute | solution.py:337
  13.2 0.0 collective-permute-done
  13.2 2.5 %collective-permute-done.1 = bf16[128,128]{1,0:T(8,128)(2,1)S(1)} collective-permute-done((bf16[128,128]{1,0:T(8,128)(2,1)S(1)}, bf16[128,128]{1,0:T(8,128)(2,1)S(1)}, u32[]{:S(2)}, u32[]{:S(2)}) %collective-permute-start.1) | collective-permute-done | bytes 32800 | tf_op jit(solution)/shard_map/ppermute | solution.py:337
  15.7 0.0 collective-permute-done.2
  15.7 1.6 %collective-permute-start.5 = (bf16[3,112,128]{2,1,0:T(8,128)(2,1)S(1)}, bf16[3,112,128]{2,1,0:T(8,128)(2,1)S(1)}, u32[]{:S(2)}, u32[]{:S(2)}) collective-permute-start(bf16[3,112,128]{2,1,0:T(8,128)(2,1)S(1)} %pad_maximum_fusion.2), channel_id=1, source_target_pairs={{0,2},{1,3},{2,0},{3,1},{4,6},{5,7},{6,4},{7,5},{8,10},{9,11},{10,... | collective-permute-start | bytes 258056 | tf_op jit(solution)/shard_map/ppermute | solution.py:337
  17.4 0.1 collective-permute-start.3
  17.4 2.4 %split.1 = (bf16[256,4096]{1,0:T(8,128)(2,1)S(1)}, bf16[256,4096]{1,0:T(8,128)(2,1)S(1)}) custom-call(f32[256,4096]{1,0:T(8,128)} %hess_ref.1, bf16[4,128,128]{2,1,0:T(8,128)(2,1)S(1)} %pad_maximum_fusion.after_ref.refs_0_), custom_call_target="tpu_custom_call" | custom-call | tf_op jit(solution)/shard_map/split/pallas_call | solution.py:228
  19.8 0.0 collective-permute-done.4
  19.8 0.5 %collective-permute-done.5 = bf16[3,112,128]{2,1,0:T(8,128)(2,1)S(1)} collective-permute-done((bf16[3,112,128]{2,1,0:T(8,128)(2,1)S(1)}, bf16[3,112,128]{2,1,0:T(8,128)(2,1)S(1)}, u32[]{:S(2)}, u32[]{:S(2)}) %collective-permute-start.5) | collective-permute-done | bytes 86048 | tf_op jit(solution)/shard_map/ppermute | solution.py:337
  20.3 0.1 collective-permute-start.6
  20.4 0.4 %prepare.4.refs_5_ = bf16[32,4096]{1,0:T(8,128)(2,1)S(1)} custom-call(bf16[4,112,128]{2,1,0:T(8,128)(2,1)S(1)} %pad_maximum_fusion.1.refs_0_.refs_2_), custom_call_target="tpu_custom_call" | custom-call | tf_op jit(solution)/shard_map/prepare/pallas_call | solution.py:255
  20.8 0.0 collective-permute-done.3.refs_1_
  20.8 0.6 %prepare.3.refs_4_ = bf16[48,4096]{1,0:T(8,128)(2,1)S(1)} custom-call(bf16[4,128,128]{2,1,0:T(8,128)(2,1)S(1)} %pad_maximum_fusion.after_ref.refs_0_, bf16[4,112,128]{2,1,0:T(8,128)(2,1)S(1)} %collective-permute-done.3.refs_1_), custom_call_target="tpu_custom_call" | custom-call | tf_op jit(solution)/shard_map/prepare/pallas_call | solution.py:255
  21.5 0.2 collective-permute-done.6.refs_0_.refs_3_
  21.7 0.4 %prepare.5.refs_6_ = bf16[32,4096]{1,0:T(8,128)(2,1)S(1)} custom-call(bf16[4,112,128]{2,1,0:T(8,128)(2,1)S(1)} %collective-permute-done.6.refs_0_.refs_3_), custom_call_target="tpu_custom_call" | custom-call | tf_op jit(solution)/shard_map/prepare/pallas_call | solution.py:255
  22.1 1.6 %score.1 = f32[128,128]{1,0:T(8,128)S(1)} custom-call(s32[1]{0:T(128)} %bitcast.me_ref, bf16[4,128,128]{2,1,0:T(8,128)(2,1)S(1)} %pad_maximum_fusion.after_ref.refs_0_, bf16[4,112,128]{2,1,0:T(8,128)(2,1)S(1)} %collective-permute-done.3.refs_1_, bf16[4,112,128]{2,1,0:T(8,128)(2,1)S(1)} %pad_maximum_fusion.1.refs_0_.refs_2_, ...), custom_call_target="tpu_custom_call" | custom-call | tf_op jit(solution)/shard_map/score/pallas_call | solution.py:318
  23.7 11.1 %all_to_all.5.parts_ref = f32[16,8,128]{2,1,0:T(8,128)S(1)} all-to-all(f32[16,8,128]{2,1,0:T(8,128)S(1)} %bitcast.11), channel_id=1, replica_groups=mesh['groups'=2,'dp'=16] {'dp'}, dimensions={0} | all-to-all | bytes 131072 | tf_op jit(solution)/shard_map/all_to_all | solution.py:369
  34.8 0.6 %finish.1 = f32[4,96]{1,0:T(4,128)} custom-call(f32[16,8,128]{2,1,0:T(8,128)S(1)} %all_to_all.5.parts_ref), custom_call_target="tpu_custom_call" | custom-call | tf_op jit(solution)/shard_map/finish/pallas_call | solution.py:370
  (5 shorter events, 0.1 us)
Async XLA Ops:
  5.8 7.4 %collective-permute-start = (bf16[128,128]{1,0:T(8,128)(2,1)S(1)}, bf16[128,128]{1,0:T(8,128)(2,1)S(1)}, u32[]{:S(2)}, u32[]{:S(2)}) collective-permute-start(bf16[128,128]{1,0:T(8,128)(2,1)S(1)} %get-tuple-element.15), channel_id=1, source_target_pairs={{0,12},{1,13},{2,14},{3,15},{4,8},{5,9},{6,10},{7,11},{8,4},{9,5},... | collective-permute-start | bytes 98312 | tf_op jit(solution)/shard_map/ppermute | solution.py:337
  10.9 4.8 %collective-permute-start.1 = (bf16[128,128]{1,0:T(8,128)(2,1)S(1)}, bf16[128,128]{1,0:T(8,128)(2,1)S(1)}, u32[]{:S(2)}, u32[]{:S(2)}) collective-permute-start(bf16[128,128]{1,0:T(8,128)(2,1)S(1)} %get-tuple-element.16), channel_id=1, source_target_pairs={{0,8},{1,9},{2,10},{3,11},{4,12},{5,13},{6,14},{7,15},{8,0},{9,1},... | collective-permute-start | bytes 98312 | tf_op jit(solution)/shard_map/ppermute | solution.py:337
  10.9 4.8 %collective-permute-start.2 = (bf16[128,128]{1,0:T(8,128)(2,1)S(1)}, bf16[128,128]{1,0:T(8,128)(2,1)S(1)}, u32[]{:S(2)}, u32[]{:S(2)}) collective-permute-start(bf16[128,128]{1,0:T(8,128)(2,1)S(1)} %get-tuple-element.17), channel_id=1, source_target_pairs={{0,4},{1,5},{2,6},{3,7},{4,0},{5,1},{6,2},{7,3},{8,12},{9,13},{10,... | collective-permute-start | bytes 98312 | tf_op jit(solution)/shard_map/ppermute | solution.py:337
  11.5 8.3 %collective-permute-start.4 = (bf16[112,128]{1,0:T(8,128)(2,1)S(1)}, bf16[112,128]{1,0:T(8,128)(2,1)S(1)}, u32[]{:S(2)}, u32[]{:S(2)}) collective-permute-start(bf16[112,128]{1,0:T(8,128)(2,1)S(1)} %slice.10), channel_id=1, source_target_pairs={{0,2},{1,3},{2,0},{3,1},{4,6},{5,7},{6,4},{7,5},{8,10},{9,11},{10,... | collective-permute-start | bytes 86024 | tf_op jit(solution)/shard_map/ppermute | solution.py:337
  15.7 4.6 %collective-permute-start.5 = (bf16[3,112,128]{2,1,0:T(8,128)(2,1)S(1)}, bf16[3,112,128]{2,1,0:T(8,128)(2,1)S(1)}, u32[]{:S(2)}, u32[]{:S(2)}) collective-permute-start(bf16[3,112,128]{2,1,0:T(8,128)(2,1)S(1)} %pad_maximum_fusion.2), channel_id=1, source_target_pairs={{0,2},{1,3},{2,0},{3,1},{4,6},{5,7},{6,4},{7,5},{8,10},{9,11},{10,... | collective-permute-start | bytes 258056 | tf_op jit(solution)/shard_map/ppermute | solution.py:337
  17.4 3.5 %collective-permute-start.3 = (bf16[4,112,128]{2,1,0:T(8,128)(2,1)S(1)}, bf16[4,112,128]{2,1,0:T(8,128)(2,1)S(1)}, u32[]{:S(2)}, u32[]{:S(2)}) collective-permute-start(bf16[4,112,128]{2,1,0:T(8,128)(2,1)S(1)} %slice.12), channel_id=1, source_target_pairs={{0,1},{1,0},{2,3},{3,2},{4,5},{5,4},{6,7},{7,6},{8,9},{9,8},{10,11... | collective-permute-start | bytes 344072 | tf_op jit(solution)/shard_map/ppermute | solution.py:337
  20.3 1.4 %collective-permute-start.6 = (bf16[4,112,128]{2,1,0:T(8,128)(2,1)S(1)}, bf16[4,112,128]{2,1,0:T(8,128)(2,1)S(1)}, u32[]{:S(2)}, u32[]{:S(2)}) collective-permute-start(bf16[4,112,128]{2,1,0:T(8,128)(2,1)S(1)} %pad_maximum_fusion.1.refs_0_.refs_2_), channel_id=1, source_target_pairs={{0,1},{1,0},{2,3},{3,2},{4,5},{5,4},{6,7},{7,6},{8,9},{9,8},{10,11... | collective-permute-start | bytes 344072 | tf_op jit(solution)/shard_map/ppermute | solution.py:337

commit v6 on v5

--- a/solution.py
+++ b/solution.py
@@ -99,8 +99,10 @@
     q_in = jnp.zeros((queries, rank), F32)
     for c, cols in enumerate(parts):
         arrived()
-        t_in += dot_nt(th[:, cols], pi[:, cols])
-        q_in += dot_nt(qh[:, cols], pi[:, cols])
+        middle = (cols.start + cols.stop) // 2
+        for some in (slice(cols.start, middle), slice(middle, cols.stop)):
+            t_in += dot_nt(th[:, some], pi[:, some])
+            q_in += dot_nt(qh[:, some], pi[:, some])
         if c == 0:
             arrived()
             q_out = dot_nt(qc[...], po[...])
@@ -128,7 +130,7 @@
     for k in range(planes):
         shares = [
             grads[pl.ds(pl.multiple_of(((plane ^ k) * INNER + (inner ^ j)) * tile, tile), tile), :]
-            for j in (0, 1, 3, 2)
+            for j in ((0, 1, 3, 2) if k == 0 else (1, 0, 2, 3))
         ]
         outs[k][:edge, :] = jnp.concatenate(shares[:2], axis=0).astype(BF16)
         outs[k][edge : edge + queries, :] = message
@@ -347,22 +349,27 @@
         me, planes, train_hidden, train_cot, query_hidden, query_cot, proj_in, proj_out
     )
     coords = hess_inv.shape[1]
-    others = [INNER * k for k in range(planes - 1, 0, -1)]
+    others = [(INNER * k) ^ 1 for k in range(planes - 1, 0, -1)]
     far = [swap(messages[slot // INNER], slot, n) for slot in others]
     edge = (messages[0].shape[0] - tokens) // 2
-    own_two = swap(messages[0][edge:], 2, n)
-    by_plane = jnp.stack([messages[0]] + far)
+    by_plane = [messages[0]] + far
+    halves = by_plane[: planes // 2], by_plane[planes // 2 :]
+    by_two = jnp.concatenate([swap(jnp.stack(half)[:, edge:], 3, n) for half in halves], axis=0)
+    by_plane = jnp.stack(by_plane)
     by_plane_one = swap(by_plane[:, :-edge], 1, n)
-    by_two = jnp.concatenate([own_two[None], swap(jnp.stack(far)[:, edge:], 2, n)], axis=0)
     high, low = split(hess_inv, by_plane)
-    made = [prepare(tokens, qlen, coords, [edge, edge], by_plane, by_plane_one)]
-    by_two, high, low = lax.optimization_barrier((by_two, high, low))
+    made = prepare(tokens, qlen, coords, [edge], by_plane)
+    by_two, high, low, made = lax.optimization_barrier((by_two, high, low, made))
     by_two_one = swap(by_two, 1, n)
-    made += [prepare(tokens, qlen, coords, [0], piece) for piece in (by_two, by_two_one)]
-    slots = [[first ^ slot for slot in [0] + others] for first in (0, 1, 2, 3)]
-    rows_of = [slots[0] + slots[1], slots[2], slots[3]]
+    made = [
+        made,
+        prepare(tokens, qlen, coords, [edge, 0], by_plane_one, by_two),
+        prepare(tokens, qlen, coords, [0], by_two_one),
+    ]
+    slots = [[first ^ slot for slot in [0] + others] for first in (0, 1, 3, 2)]
+    rows_of = [slots[0], slots[1] + slots[2], slots[3]]
     pieces = [by_plane, by_plane_one, by_two, by_two_one]
-    shares = [(0, False), (0, True), (tokens, True), (tokens, False)]
+    shares = [(0, False), (0, True), (tokens, False), (tokens, True)]
     each = tokens // qlen
     parts = score(me, number, each, pieces, slots, shares, made, rows_of, high, low)
     parts = parts.reshape(n, -1, parts.shape[1])

time: 35.6 us -> 34.7 us (0.975)
  waiting for transfers between devices: 3.18 us -> 2.31 us
    ppermute x7, waiting for transfers between devices: 3.18 us -> 2.31 us  [swap(): return lax.ppermute(x, 'dp', [(i, i ^ k) for i in range(n)])]
where the time goes in v6:
time: 34.7 us; the launch traced here: 34.6 us
  Pallas kernels  11.7 us (34%)
  blocking collectives  11.1 us (32%)
  starting transfers between devices  9.31 us (27%)
  waiting for transfers between devices  2.31 us (7%)
    all_to_all x1, blocking collectives, fast(): parts = lax.all_to_all(parts, 'dp', 0, 0, tiled=True)  11.1 us
    ppermute x7, starting transfers between devices, swap(): return lax.ppermute(x, 'dp', [(i, i ^ k) for i in range(n)])  9.31 us
    pallas_call x1, Pallas kernels, project(): pl.pallas_call(functools.partial(project_kernel, planes, number, length,...  5.58 us
    pallas_call x1, Pallas kernels, split(): pl.pallas_call(functools.partial(split_kernel, chunks), out_shape=[pltpu....  2.35 us
    ppermute x7, waiting for transfers between devices, swap(): return lax.ppermute(x, 'dp', [(i, i ^ k) for i in range(n)])  2.31 us
    pallas_call x1, Pallas kernels, score(): pl.pallas_call(functools.partial(score_kernel, number, each, slots, share...  1.6 us
    pallas_call x3, Pallas kernels, prepare(): pl.pallas_call(functools.partial(prepare_kernel, tokens, qlen, starts), o...  1.51 us
  transfers between devices with their start and end apart: 7, of which 3 were waited for; matrix products, arithmetic and copies ran while one was open for 0% of the time, Pallas kernels for 10%

profile of v6, /device:TPU:0, one launch (start us, length us, event | category | flops | bytes accessed | tf_op | source)
XLA Modules:
  0.0 34.6 jit_solution(8133276189530422633)
XLA Ops:
  0.0 5.6 %project.1 = (bf16[128,128]{1,0:T(8,128)(2,1)S(1)}, bf16[128,128]{1,0:T(8,128)(2,1)S(1)}, bf16[128,128]{1,0:T(8,128)(2,1)S(1)}, bf16[128,128]{1,0:T(8,128)(2,1)S(1)}) custom-call(s32[1]{0:T(128)} %bitcast.me_ref, bf16[160,14336]{1,0:T(8,128)(2,1)} %bitcast.13, bf16[160,4096]{1,0:T(8,128)(2,1)} %bitcast.15, bf16[96,14336]{1,0:T(8,128)(2,1)} %bitcast.14, ...), custom_call_target="tpu_custom_call" | custom-call | tf_op jit(solution)/shard_map/project/pallas_call | solution.py:147
  5.6 4.6 %collective-permute-start = (bf16[128,128]{1,0:T(8,128)(2,1)S(1)}, bf16[128,128]{1,0:T(8,128)(2,1)S(1)}, u32[]{:S(2)}, u32[]{:S(2)}) collective-permute-start(bf16[128,128]{1,0:T(8,128)(2,1)S(1)} %get-tuple-element.16), channel_id=1, source_target_pairs={{0,13},{1,12},{2,15},{3,14},{4,9},{5,8},{6,11},{7,10},{8,5},{9,4},... | collective-permute-start | bytes 98312 | tf_op jit(solution)/shard_map/ppermute | solution.py:339
  10.2 0.0 collective-permute-start.1
  10.2 0.9 %collective-permute-start.2 = (bf16[128,128]{1,0:T(8,128)(2,1)S(1)}, bf16[128,128]{1,0:T(8,128)(2,1)S(1)}, u32[]{:S(2)}, u32[]{:S(2)}) collective-permute-start(bf16[128,128]{1,0:T(8,128)(2,1)S(1)} %get-tuple-element.18), channel_id=1, source_target_pairs={{0,5},{1,4},{2,7},{3,6},{4,1},{5,0},{6,3},{7,2},{8,13},{9,12},{10,... | collective-permute-start | bytes 98312 | tf_op jit(solution)/shard_map/ppermute | solution.py:339
  11.1 0.9 %collective-permute-done = bf16[128,128]{1,0:T(8,128)(2,1)S(1)} collective-permute-done((bf16[128,128]{1,0:T(8,128)(2,1)S(1)}, bf16[128,128]{1,0:T(8,128)(2,1)S(1)}, u32[]{:S(2)}, u32[]{:S(2)}) %collective-permute-start) | collective-permute-done | bytes 32800 | tf_op jit(solution)/shard_map/ppermute | solution.py:339
  11.9 1.6 %collective-permute-start.4 = (bf16[2,112,128]{2,1,0:T(8,128)(2,1)S(1)}, bf16[2,112,128]{2,1,0:T(8,128)(2,1)S(1)}, u32[]{:S(2)}, u32[]{:S(2)}) collective-permute-start(bf16[2,112,128]{2,1,0:T(8,128)(2,1)S(1)} %pad_maximum_fusion.3), channel_id=1, source_target_pairs={{0,3},{1,2},{2,1},{3,0},{4,7},{5,6},{6,5},{7,4},{8,11},{9,10},{10,... | collective-permute-start | bytes 172040 | tf_op jit(solution)/shard_map/ppermute | solution.py:339
  13.6 1.1 %collective-permute-done.1 = bf16[128,128]{1,0:T(8,128)(2,1)S(1)} collective-permute-done((bf16[128,128]{1,0:T(8,128)(2,1)S(1)}, bf16[128,128]{1,0:T(8,128)(2,1)S(1)}, u32[]{:S(2)}, u32[]{:S(2)}) %collective-permute-start.1) | collective-permute-done | bytes 32800 | tf_op jit(solution)/shard_map/ppermute | solution.py:339
  14.7 0.0 collective-permute-done.2
  14.7 1.6 %collective-permute-start.5 = (bf16[2,112,128]{2,1,0:T(8,128)(2,1)S(1)}, bf16[2,112,128]{2,1,0:T(8,128)(2,1)S(1)}, u32[]{:S(2)}, u32[]{:S(2)}) collective-permute-start(bf16[2,112,128]{2,1,0:T(8,128)(2,1)S(1)} %pad_maximum_fusion.2), channel_id=1, source_target_pairs={{0,3},{1,2},{2,1},{3,0},{4,7},{5,6},{6,5},{7,4},{8,11},{9,10},{10,... | collective-permute-start | bytes 172040 | tf_op jit(solution)/shard_map/ppermute | solution.py:339
  16.3 0.4 %prepare.3.refs_4_ = bf16[32,4096]{1,0:T(8,128)(2,1)S(1)} custom-call(bf16[4,128,128]{2,1,0:T(8,128)(2,1)S(1)} %pad_maximum_fusion.after_ref.refs_0_), custom_call_target="tpu_custom_call" | custom-call | tf_op jit(solution)/shard_map/prepare/pallas_call | solution.py:257
  16.8 0.2 collective-permute-start.3
  17.0 2.4 %split.1 = (bf16[256,4096]{1,0:T(8,128)(2,1)S(1)}, bf16[256,4096]{1,0:T(8,128)(2,1)S(1)}) custom-call(f32[256,4096]{1,0:T(8,128)} %hess_ref.1, bf16[4,128,128]{2,1,0:T(8,128)(2,1)S(1)} %pad_maximum_fusion.after_ref.refs_0_), custom_call_target="tpu_custom_call" | custom-call | tf_op jit(solution)/shard_map/split/pallas_call | solution.py:230
  19.3 0.0 collective-permute-done.4
  19.3 0.0 collective-permute-done.5
  19.4 0.4 %collective-permute-start.6 = (bf16[4,112,128]{2,1,0:T(8,128)(2,1)S(1)}, bf16[4,112,128]{2,1,0:T(8,128)(2,1)S(1)}, u32[]{:S(2)}, u32[]{:S(2)}) collective-permute-start(bf16[4,112,128]{2,1,0:T(8,128)(2,1)S(1)} %pad_maximum_fusion.1.refs_1_.refs_2_), channel_id=1, source_target_pairs={{0,1},{1,0},{2,3},{3,2},{4,5},{5,4},{6,7},{7,6},{8,9},{9,8},{10,11... | collective-permute-start | bytes 344072 | tf_op jit(solution)/shard_map/ppermute | solution.py:339
  19.8 0.0 collective-permute-done.3.refs_0_.refs_1_
  19.8 0.6 %prepare.4.refs_5_ = bf16[48,4096]{1,0:T(8,128)(2,1)S(1)} custom-call(bf16[4,112,128]{2,1,0:T(8,128)(2,1)S(1)} %collective-permute-done.3.refs_0_.refs_1_, bf16[4,112,128]{2,1,0:T(8,128)(2,1)S(1)} %pad_maximum_fusion.1.refs_1_.refs_2_), custom_call_target="tpu_custom_call" | custom-call | tf_op jit(solution)/shard_map/prepare/pallas_call | solution.py:257
  20.4 0.3 collective-permute-done.6.refs_0_.refs_3_
  20.8 0.4 %prepare.5.refs_6_ = bf16[32,4096]{1,0:T(8,128)(2,1)S(1)} custom-call(bf16[4,112,128]{2,1,0:T(8,128)(2,1)S(1)} %collective-permute-done.6.refs_0_.refs_3_), custom_call_target="tpu_custom_call" | custom-call | tf_op jit(solution)/shard_map/prepare/pallas_call | solution.py:257
  21.2 1.6 %score.1 = f32[128,128]{1,0:T(8,128)S(1)} custom-call(s32[1]{0:T(128)} %bitcast.me_ref, bf16[4,128,128]{2,1,0:T(8,128)(2,1)S(1)} %pad_maximum_fusion.after_ref.refs_0_, bf16[4,112,128]{2,1,0:T(8,128)(2,1)S(1)} %collective-permute-done.3.refs_0_.refs_1_, bf16[4,112,128]{2,1,0:T(8,128)(2,1)S(1)} %pad_maximum_fusion.1.refs_1_.refs_2_, ...), custom_call_target="tpu_custom_call" | custom-call | tf_op jit(solution)/shard_map/score/pallas_call | solution.py:320
  22.8 11.1 %all_to_all.5.parts_ref = f32[16,8,128]{2,1,0:T(8,128)S(1)} all-to-all(f32[16,8,128]{2,1,0:T(8,128)S(1)} %bitcast.10), channel_id=1, replica_groups=mesh['groups'=2,'dp'=16] {'dp'}, dimensions={0} | all-to-all | bytes 131072 | tf_op jit(solution)/shard_map/all_to_all | solution.py:376
  34.0 0.6 %finish.1 = f32[4,96]{1,0:T(4,128)} custom-call(f32[16,8,128]{2,1,0:T(8,128)S(1)} %all_to_all.5.parts_ref), custom_call_target="tpu_custom_call" | custom-call | tf_op jit(solution)/shard_map/finish/pallas_call | solution.py:377
  (5 shorter events, 0.1 us)
Async XLA Ops:
  5.6 6.3 %collective-permute-start = (bf16[128,128]{1,0:T(8,128)(2,1)S(1)}, bf16[128,128]{1,0:T(8,128)(2,1)S(1)}, u32[]{:S(2)}, u32[]{:S(2)}) collective-permute-start(bf16[128,128]{1,0:T(8,128)(2,1)S(1)} %get-tuple-element.16), channel_id=1, source_target_pairs={{0,13},{1,12},{2,15},{3,14},{4,9},{5,8},{6,11},{7,10},{8,5},{9,4},... | collective-permute-start | bytes 98312 | tf_op jit(solution)/shard_map/ppermute | solution.py:339
  10.2 4.5 %collective-permute-start.1 = (bf16[128,128]{1,0:T(8,128)(2,1)S(1)}, bf16[128,128]{1,0:T(8,128)(2,1)S(1)}, u32[]{:S(2)}, u32[]{:S(2)}) collective-permute-start(bf16[128,128]{1,0:T(8,128)(2,1)S(1)} %get-tuple-element.17), channel_id=1, source_target_pairs={{0,9},{1,8},{2,11},{3,10},{4,13},{5,12},{6,15},{7,14},{8,1},{9,0},... | collective-permute-start | bytes 98312 | tf_op jit(solution)/shard_map/ppermute | solution.py:339
  10.2 4.5 %collective-permute-start.2 = (bf16[128,128]{1,0:T(8,128)(2,1)S(1)}, bf16[128,128]{1,0:T(8,128)(2,1)S(1)}, u32[]{:S(2)}, u32[]{:S(2)}) collective-permute-start(bf16[128,128]{1,0:T(8,128)(2,1)S(1)} %get-tuple-element.18), channel_id=1, source_target_pairs={{0,5},{1,4},{2,7},{3,6},{4,1},{5,0},{6,3},{7,2},{8,13},{9,12},{10,... | collective-permute-start | bytes 98312 | tf_op jit(solution)/shard_map/ppermute | solution.py:339
  11.9 7.4 %collective-permute-start.4 = (bf16[2,112,128]{2,1,0:T(8,128)(2,1)S(1)}, bf16[2,112,128]{2,1,0:T(8,128)(2,1)S(1)}, u32[]{:S(2)}, u32[]{:S(2)}) collective-permute-start(bf16[2,112,128]{2,1,0:T(8,128)(2,1)S(1)} %pad_maximum_fusion.3), channel_id=1, source_target_pairs={{0,3},{1,2},{2,1},{3,0},{4,7},{5,6},{6,5},{7,4},{8,11},{9,10},{10,... | collective-permute-start | bytes 172040 | tf_op jit(solution)/shard_map/ppermute | solution.py:339
  14.7 4.6 %collective-permute-start.5 = (bf16[2,112,128]{2,1,0:T(8,128)(2,1)S(1)}, bf16[2,112,128]{2,1,0:T(8,128)(2,1)S(1)}, u32[]{:S(2)}, u32[]{:S(2)}) collective-permute-start(bf16[2,112,128]{2,1,0:T(8,128)(2,1)S(1)} %pad_maximum_fusion.2), channel_id=1, source_target_pairs={{0,3},{1,2},{2,1},{3,0},{4,7},{5,6},{6,5},{7,4},{8,11},{9,10},{10,... | collective-permute-start | bytes 172040 | tf_op jit(solution)/shard_map/ppermute | solution.py:339
  16.8 3.0 %collective-permute-start.3 = (bf16[4,112,128]{2,1,0:T(8,128)(2,1)S(1)}, bf16[4,112,128]{2,1,0:T(8,128)(2,1)S(1)}, u32[]{:S(2)}, u32[]{:S(2)}) collective-permute-start(bf16[4,112,128]{2,1,0:T(8,128)(2,1)S(1)} %slice.12), channel_id=1, source_target_pairs={{0,1},{1,0},{2,3},{3,2},{4,5},{5,4},{6,7},{7,6},{8,9},{9,8},{10,11... | collective-permute-start | bytes 344072 | tf_op jit(solution)/shard_map/ppermute | solution.py:339
  19.4 1.4 %collective-permute-start.6 = (bf16[4,112,128]{2,1,0:T(8,128)(2,1)S(1)}, bf16[4,112,128]{2,1,0:T(8,128)(2,1)S(1)}, u32[]{:S(2)}, u32[]{:S(2)}) collective-permute-start(bf16[4,112,128]{2,1,0:T(8,128)(2,1)S(1)} %pad_maximum_fusion.1.refs_1_.refs_2_), channel_id=1, source_target_pairs={{0,1},{1,0},{2,3},{3,2},{4,5},{5,4},{6,7},{7,6},{8,9},{9,8},{10,11... | collective-permute-start | bytes 344072 | tf_op jit(solution)/shard_map/ppermute | solution.py:339

commit v7 on v6

--- a/solution.py
+++ b/solution.py
@@ -353,8 +353,9 @@
     far = [swap(messages[slot // INNER], slot, n) for slot in others]
     edge = (messages[0].shape[0] - tokens) // 2
     by_plane = [messages[0]] + far
-    halves = by_plane[: planes // 2], by_plane[planes // 2 :]
-    by_two = jnp.concatenate([swap(jnp.stack(half)[:, edge:], 3, n) for half in halves], axis=0)
+    near = swap(messages[1][edge:], others[-1] ^ 3, n)
+    by_two = swap(jnp.stack(by_plane[:-1])[:, edge:], 3, n)
+    by_two = jnp.concatenate([by_two, near[None]], axis=0)
     by_plane = jnp.stack(by_plane)
     by_plane_one = swap(by_plane[:, :-edge], 1, n)
     high, low = split(hess_inv, by_plane)

time: 34.7 us -> 34.2 us (0.986)
  waiting for transfers between devices: 2.31 us -> 1.59 us
  starting transfers between devices: 9.31 us -> 10 us
  blocking collectives: 11.1 us -> 10.6 us
    ppermute x7, starting transfers between devices: 9.31 us -> 10 us  [swap(): return lax.ppermute(x, 'dp', [(i, i ^ k) for i in range(n)])]
    ppermute x7, waiting for transfers between devices: 2.31 us -> 1.59 us  [swap(): return lax.ppermute(x, 'dp', [(i, i ^ k) for i in range(n)])]
    all_to_all x1, blocking collectives: 11.1 us -> 10.6 us  [fast(): parts = lax.all_to_all(parts, 'dp', 0, 0, tiled=True)]
  transfers between devices with their start and end apart: 7 -> 7, of which waited for: 3 -> 2; matrix products, arithmetic and copies ran while one was open for 0% -> 0% of each run, Pallas kernels for 10% -> 10%
where the time goes in v7:
time: 34.2 us; the launch traced here: 34 us
  Pallas kernels  11.7 us (34%)
  blocking collectives  10.6 us (31%)
  starting transfers between devices  10 us (29%)
  waiting for transfers between devices  1.59 us (5%)
    all_to_all x1, blocking collectives, fast(): parts = lax.all_to_all(parts, 'dp', 0, 0, tiled=True)  10.6 us
    ppermute x7, starting transfers between devices, swap(): return lax.ppermute(x, 'dp', [(i, i ^ k) for i in range(n)])  10 us
    pallas_call x1, Pallas kernels, project(): pl.pallas_call(functools.partial(project_kernel, planes, number, length,...  5.58 us
    pallas_call x1, Pallas kernels, split(): pl.pallas_call(functools.partial(split_kernel, chunks), out_shape=[pltpu....  2.35 us
    pallas_call x1, Pallas kernels, score(): pl.pallas_call(functools.partial(score_kernel, number, each, slots, share...  1.6 us
    ppermute x7, waiting for transfers between devices, swap(): return lax.ppermute(x, 'dp', [(i, i ^ k) for i in range(n)])  1.59 us
    pallas_call x3, Pallas kernels, prepare(): pl.pallas_call(functools.partial(prepare_kernel, tokens, qlen, starts), o...  1.52 us
  transfers between devices with their start and end apart: 7, of which 2 were waited for; matrix products, arithmetic and copies ran while one was open for 0% of the time, Pallas kernels for 10%

profile of v7, /device:TPU:0, one launch (start us, length us, event | category | flops | bytes accessed | tf_op | source)
XLA Modules:
  0.0 34.0 jit_solution(1468193554752490332)
XLA Ops:
  0.0 5.6 %project.1 = (bf16[128,128]{1,0:T(8,128)(2,1)S(1)}, bf16[128,128]{1,0:T(8,128)(2,1)S(1)}, bf16[128,128]{1,0:T(8,128)(2,1)S(1)}, bf16[128,128]{1,0:T(8,128)(2,1)S(1)}) custom-call(s32[1]{0:T(128)} %bitcast.me_ref, bf16[160,14336]{1,0:T(8,128)(2,1)} %bitcast.14, bf16[160,4096]{1,0:T(8,128)(2,1)} %bitcast.16, bf16[96,14336]{1,0:T(8,128)(2,1)} %bitcast.15, ...), custom_call_target="tpu_custom_call" | custom-call | tf_op jit(solution)/shard_map/project/pallas_call | solution.py:147
  5.6 4.6 %collective-permute-start = (bf16[128,128]{1,0:T(8,128)(2,1)S(1)}, bf16[128,128]{1,0:T(8,128)(2,1)S(1)}, u32[]{:S(2)}, u32[]{:S(2)}) collective-permute-start(bf16[128,128]{1,0:T(8,128)(2,1)S(1)} %get-tuple-element.16), channel_id=1, source_target_pairs={{0,13},{1,12},{2,15},{3,14},{4,9},{5,8},{6,11},{7,10},{8,5},{9,4},... | collective-permute-start | bytes 98312 | tf_op jit(solution)/shard_map/ppermute | solution.py:339
  10.2 0.0 collective-permute-start.1
  10.2 0.9 %collective-permute-start.2 = (bf16[128,128]{1,0:T(8,128)(2,1)S(1)}, bf16[128,128]{1,0:T(8,128)(2,1)S(1)}, u32[]{:S(2)}, u32[]{:S(2)}) collective-permute-start(bf16[128,128]{1,0:T(8,128)(2,1)S(1)} %get-tuple-element.18), channel_id=1, source_target_pairs={{0,5},{1,4},{2,7},{3,6},{4,1},{5,0},{6,3},{7,2},{8,13},{9,12},{10,... | collective-permute-start | bytes 98312 | tf_op jit(solution)/shard_map/ppermute | solution.py:339
  11.1 2.3 %collective-permute-start.5 = (bf16[112,128]{1,0:T(8,128)(2,1)S(1)}, bf16[112,128]{1,0:T(8,128)(2,1)S(1)}, u32[]{:S(2)}, u32[]{:S(2)}) collective-permute-start(bf16[112,128]{1,0:T(8,128)(2,1)S(1)} %slice.11), channel_id=1, source_target_pairs={{0,6},{1,7},{2,4},{3,5},{4,2},{5,3},{6,0},{7,1},{8,14},{9,15},{10,... | collective-permute-start | bytes 86024 | tf_op jit(solution)/shard_map/ppermute | solution.py:339
  13.4 0.0 collective-permute-done
  13.4 1.3 %collective-permute-done.1 = bf16[128,128]{1,0:T(8,128)(2,1)S(1)} collective-permute-done((bf16[128,128]{1,0:T(8,128)(2,1)S(1)}, bf16[128,128]{1,0:T(8,128)(2,1)S(1)}, u32[]{:S(2)}, u32[]{:S(2)}) %collective-permute-start.1) | collective-permute-done | bytes 32800 | tf_op jit(solution)/shard_map/ppermute | solution.py:339
  14.7 1.6 %collective-permute-start.4 = (bf16[3,112,128]{2,1,0:T(8,128)(2,1)S(1)}, bf16[3,112,128]{2,1,0:T(8,128)(2,1)S(1)}, u32[]{:S(2)}, u32[]{:S(2)}) collective-permute-start(bf16[3,112,128]{2,1,0:T(8,128)(2,1)S(1)} %pad_maximum_fusion.2), channel_id=1, source_target_pairs={{0,3},{1,2},{2,1},{3,0},{4,7},{5,6},{6,5},{7,4},{8,11},{9,10},{10,... | collective-permute-start | bytes 258056 | tf_op jit(solution)/shard_map/ppermute | solution.py:339
  16.3 0.0 collective-permute-done.2
  16.3 0.4 %prepare.3.refs_4_ = bf16[32,4096]{1,0:T(8,128)(2,1)S(1)} custom-call(bf16[4,128,128]{2,1,0:T(8,128)(2,1)S(1)} %pad_maximum_fusion.after_ref.refs_0_), custom_call_target="tpu_custom_call" | custom-call | tf_op jit(solution)/shard_map/prepare/pallas_call | solution.py:257
  16.8 0.2 collective-permute-start.3
  17.0 2.4 %split.1 = (bf16[256,4096]{1,0:T(8,128)(2,1)S(1)}, bf16[256,4096]{1,0:T(8,128)(2,1)S(1)}) custom-call(f32[256,4096]{1,0:T(8,128)} %hess_ref.1, bf16[4,128,128]{2,1,0:T(8,128)(2,1)S(1)} %pad_maximum_fusion.after_ref.refs_0_), custom_call_target="tpu_custom_call" | custom-call | tf_op jit(solution)/shard_map/split/pallas_call | solution.py:230
  19.3 0.0 collective-permute-done.5
  19.3 0.0 collective-permute-done.4
  19.4 0.4 %collective-permute-start.6 = (bf16[4,112,128]{2,1,0:T(8,128)(2,1)S(1)}, bf16[4,112,128]{2,1,0:T(8,128)(2,1)S(1)}, u32[]{:S(2)}, u32[]{:S(2)}) collective-permute-start(bf16[4,112,128]{2,1,0:T(8,128)(2,1)S(1)} %pad_maximum_fusion.1.refs_1_.refs_2_), channel_id=1, source_target_pairs={{0,1},{1,0},{2,3},{3,2},{4,5},{5,4},{6,7},{7,6},{8,9},{9,8},{10,11... | collective-permute-start | bytes 344072 | tf_op jit(solution)/shard_map/ppermute | solution.py:339
  19.8 0.0 collective-permute-done.3.refs_0_.refs_1_
  19.8 0.6 %prepare.4.refs_5_ = bf16[48,4096]{1,0:T(8,128)(2,1)S(1)} custom-call(bf16[4,112,128]{2,1,0:T(8,128)(2,1)S(1)} %collective-permute-done.3.refs_0_.refs_1_, bf16[4,112,128]{2,1,0:T(8,128)(2,1)S(1)} %pad_maximum_fusion.1.refs_1_.refs_2_), custom_call_target="tpu_custom_call" | custom-call | tf_op jit(solution)/shard_map/prepare/pallas_call | solution.py:257
  20.4 0.3 collective-permute-done.6.refs_0_.refs_3_
  20.8 0.4 %prepare.5.refs_6_ = bf16[32,4096]{1,0:T(8,128)(2,1)S(1)} custom-call(bf16[4,112,128]{2,1,0:T(8,128)(2,1)S(1)} %collective-permute-done.6.refs_0_.refs_3_), custom_call_target="tpu_custom_call" | custom-call | tf_op jit(solution)/shard_map/prepare/pallas_call | solution.py:257
  21.2 1.6 %score.1 = f32[128,128]{1,0:T(8,128)S(1)} custom-call(s32[1]{0:T(128)} %bitcast.me_ref, bf16[4,128,128]{2,1,0:T(8,128)(2,1)S(1)} %pad_maximum_fusion.after_ref.refs_0_, bf16[4,112,128]{2,1,0:T(8,128)(2,1)S(1)} %collective-permute-done.3.refs_0_.refs_1_, bf16[4,112,128]{2,1,0:T(8,128)(2,1)S(1)} %pad_maximum_fusion.1.refs_1_.refs_2_, ...), custom_call_target="tpu_custom_call" | custom-call | tf_op jit(solution)/shard_map/score/pallas_call | solution.py:320
  22.8 10.6 %all_to_all.5.parts_ref = f32[16,8,128]{2,1,0:T(8,128)S(1)} all-to-all(f32[16,8,128]{2,1,0:T(8,128)S(1)} %bitcast.11), channel_id=1, replica_groups=mesh['groups'=2,'dp'=16] {'dp'}, dimensions={0} | all-to-all | bytes 131072 | tf_op jit(solution)/shard_map/all_to_all | solution.py:377
  33.4 0.6 %finish.1 = f32[4,96]{1,0:T(4,128)} custom-call(f32[16,8,128]{2,1,0:T(8,128)S(1)} %all_to_all.5.parts_ref), custom_call_target="tpu_custom_call" | custom-call | tf_op jit(solution)/shard_map/finish/pallas_call | solution.py:378
  (5 shorter events, 0.1 us)
Async XLA Ops:
  5.6 7.8 %collective-permute-start = (bf16[128,128]{1,0:T(8,128)(2,1)S(1)}, bf16[128,128]{1,0:T(8,128)(2,1)S(1)}, u32[]{:S(2)}, u32[]{:S(2)}) collective-permute-start(bf16[128,128]{1,0:T(8,128)(2,1)S(1)} %get-tuple-element.16), channel_id=1, source_target_pairs={{0,13},{1,12},{2,15},{3,14},{4,9},{5,8},{6,11},{7,10},{8,5},{9,4},... | collective-permute-start | bytes 98312 | tf_op jit(solution)/shard_map/ppermute | solution.py:339
  10.2 4.5 %collective-permute-start.1 = (bf16[128,128]{1,0:T(8,128)(2,1)S(1)}, bf16[128,128]{1,0:T(8,128)(2,1)S(1)}, u32[]{:S(2)}, u32[]{:S(2)}) collective-permute-start(bf16[128,128]{1,0:T(8,128)(2,1)S(1)} %get-tuple-element.17), channel_id=1, source_target_pairs={{0,9},{1,8},{2,11},{3,10},{4,13},{5,12},{6,15},{7,14},{8,1},{9,0},... | collective-permute-start | bytes 98312 | tf_op jit(solution)/shard_map/ppermute | solution.py:339
  10.2 6.1 %collective-permute-start.2 = (bf16[128,128]{1,0:T(8,128)(2,1)S(1)}, bf16[128,128]{1,0:T(8,128)(2,1)S(1)}, u32[]{:S(2)}, u32[]{:S(2)}) collective-permute-start(bf16[128,128]{1,0:T(8,128)(2,1)S(1)} %get-tuple-element.18), channel_id=1, source_target_pairs={{0,5},{1,4},{2,7},{3,6},{4,1},{5,0},{6,3},{7,2},{8,13},{9,12},{10,... | collective-permute-start | bytes 98312 | tf_op jit(solution)/shard_map/ppermute | solution.py:339
  11.1 8.2 %collective-permute-start.5 = (bf16[112,128]{1,0:T(8,128)(2,1)S(1)}, bf16[112,128]{1,0:T(8,128)(2,1)S(1)}, u32[]{:S(2)}, u32[]{:S(2)}) collective-permute-start(bf16[112,128]{1,0:T(8,128)(2,1)S(1)} %slice.11), channel_id=1, source_target_pairs={{0,6},{1,7},{2,4},{3,5},{4,2},{5,3},{6,0},{7,1},{8,14},{9,15},{10,... | collective-permute-start | bytes 86024 | tf_op jit(solution)/shard_map/ppermute | solution.py:339
  14.7 4.6 %collective-permute-start.4 = (bf16[3,112,128]{2,1,0:T(8,128)(2,1)S(1)}, bf16[3,112,128]{2,1,0:T(8,128)(2,1)S(1)}, u32[]{:S(2)}, u32[]{:S(2)}) collective-permute-start(bf16[3,112,128]{2,1,0:T(8,128)(2,1)S(1)} %pad_maximum_fusion.2), channel_id=1, source_target_pairs={{0,3},{1,2},{2,1},{3,0},{4,7},{5,6},{6,5},{7,4},{8,11},{9,10},{10,... | collective-permute-start | bytes 258056 | tf_op jit(solution)/shard_map/ppermute | solution.py:339
  16.8 3.0 %collective-permute-start.3 = (bf16[4,112,128]{2,1,0:T(8,128)(2,1)S(1)}, bf16[4,112,128]{2,1,0:T(8,128)(2,1)S(1)}, u32[]{:S(2)}, u32[]{:S(2)}) collective-permute-start(bf16[4,112,128]{2,1,0:T(8,128)(2,1)S(1)} %slice.12), channel_id=1, source_target_pairs={{0,1},{1,0},{2,3},{3,2},{4,5},{5,4},{6,7},{7,6},{8,9},{9,8},{10,11... | collective-permute-start | bytes 344072 | tf_op jit(solution)/shard_map/ppermute | solution.py:339
  19.4 1.4 %collective-permute-start.6 = (bf16[4,112,128]{2,1,0:T(8,128)(2,1)S(1)}, bf16[4,112,128]{2,1,0:T(8,128)(2,1)S(1)}, u32[]{:S(2)}, u32[]{:S(2)}) collective-permute-start(bf16[4,112,128]{2,1,0:T(8,128)(2,1)S(1)} %pad_maximum_fusion.1.refs_1_.refs_2_), channel_id=1, source_target_pairs={{0,1},{1,0},{2,3},{3,2},{4,5},{5,4},{6,7},{7,6},{8,9},{9,8},{10,11... | collective-permute-start | bytes 344072 | tf_op jit(solution)/shard_map/ppermute | solution.py:339

commit v8 on v6

--- a/solution.py
+++ b/solution.py
@@ -349,12 +349,15 @@
         me, planes, train_hidden, train_cot, query_hidden, query_cot, proj_in, proj_out
     )
     coords = hess_inv.shape[1]
-    others = [(INNER * k) ^ 1 for k in range(planes - 1, 0, -1)]
+    others = [(INNER * k) ^ 1 for k in range(1, planes)]
     far = [swap(messages[slot // INNER], slot, n) for slot in others]
     edge = (messages[0].shape[0] - tokens) // 2
     by_plane = [messages[0]] + far
-    halves = by_plane[: planes // 2], by_plane[planes // 2 :]
-    by_two = jnp.concatenate([swap(jnp.stack(half)[:, edge:], 3, n) for half in halves], axis=0)
+    own = swap(messages[0][edge:], 3, n)
+    near = swap(messages[1][edge:], others[0] ^ 3, n)
+    by_two = jnp.stack([own, near])
+    if planes > 2:
+        by_two = jnp.concatenate([by_two, swap(jnp.stack(far[1:])[:, edge:], 3, n)], axis=0)
     by_plane = jnp.stack(by_plane)
     by_plane_one = swap(by_plane[:, :-edge], 1, n)
     high, low = split(hess_inv, by_plane)

time: 34.7 us -> 33.7 us (0.971)
  starting transfers between devices: 9.31 us -> 10.7 us
  waiting for transfers between devices: 2.31 us -> 1.01 us
  blocking collectives: 11.1 us -> 10.1 us
    ppermute x7 -> x8, starting transfers between devices: 9.31 us -> 10.7 us  [swap(): return lax.ppermute(x, 'dp', [(i, i ^ k) for i in range(n)])]
    ppermute x7 -> x8, waiting for transfers between devices: 2.31 us -> 1.01 us  [swap(): return lax.ppermute(x, 'dp', [(i, i ^ k) for i in range(n)])]
    all_to_all x1, blocking collectives: 11.1 us -> 10.1 us  [fast(): parts = lax.all_to_all(parts, 'dp', 0, 0, tiled=True)]
  transfers between devices with their start and end apart: 7 -> 8, of which waited for: 3 -> 2; matrix products, arithmetic and copies ran while one was open for 0% -> 0% of each run, Pallas kernels for 10% -> 10%
where the time goes in v8:
time: 33.7 us; the launch traced here: 33.6 us
  Pallas kernels  11.7 us (35%)
  starting transfers between devices  10.7 us (32%)
  blocking collectives  10.1 us (30%)
  waiting for transfers between devices  1.01 us (3%)
    ppermute x8, starting transfers between devices, swap(): return lax.ppermute(x, 'dp', [(i, i ^ k) for i in range(n)])  10.7 us
    all_to_all x1, blocking collectives, fast(): parts = lax.all_to_all(parts, 'dp', 0, 0, tiled=True)  10.1 us
    pallas_call x1, Pallas kernels, project(): pl.pallas_call(functools.partial(project_kernel, planes, number, length,...  5.58 us
    pallas_call x1, Pallas kernels, split(): pl.pallas_call(functools.partial(split_kernel, chunks), out_shape=[pltpu....  2.36 us
    pallas_call x1, Pallas kernels, score(): pl.pallas_call(functools.partial(score_kernel, number, each, slots, share...  1.6 us
    pallas_call x3, Pallas kernels, prepare(): pl.pallas_call(functools.partial(prepare_kernel, tokens, qlen, starts), o...  1.52 us
    ppermute x8, waiting for transfers between devices, swap(): return lax.ppermute(x, 'dp', [(i, i ^ k) for i in range(n)])  1.01 us
  transfers between devices with their start and end apart: 8, of which 2 were waited for; matrix products, arithmetic and copies ran while one was open for 0% of the time, Pallas kernels for 10%

profile of v8, /device:TPU:0, one launch (start us, length us, event | category | flops | bytes accessed | tf_op | source)
XLA Modules:
  0.0 33.6 jit_solution(2761482571765626503)
XLA Ops:
  0.0 5.6 %project.1 = (bf16[128,128]{1,0:T(8,128)(2,1)S(1)}, bf16[128,128]{1,0:T(8,128)(2,1)S(1)}, bf16[128,128]{1,0:T(8,128)(2,1)S(1)}, bf16[128,128]{1,0:T(8,128)(2,1)S(1)}) custom-call(s32[1]{0:T(128)} %bitcast.me_ref, bf16[160,14336]{1,0:T(8,128)(2,1)} %bitcast.14, bf16[160,4096]{1,0:T(8,128)(2,1)} %bitcast.16, bf16[96,14336]{1,0:T(8,128)(2,1)} %bitcast.15, ...), custom_call_target="tpu_custom_call" | custom-call | tf_op jit(solution)/shard_map/project/pallas_call | solution.py:147
  5.6 3.6 %collective-permute-start.1 = (bf16[128,128]{1,0:T(8,128)(2,1)S(1)}, bf16[128,128]{1,0:T(8,128)(2,1)S(1)}, u32[]{:S(2)}, u32[]{:S(2)}) collective-permute-start(bf16[128,128]{1,0:T(8,128)(2,1)S(1)} %get-tuple-element.17), channel_id=1, source_target_pairs={{0,9},{1,8},{2,11},{3,10},{4,13},{5,12},{6,15},{7,14},{8,1},{9,0},... | collective-permute-start | bytes 98312 | tf_op jit(solution)/shard_map/ppermute | solution.py:339
  9.1 1.6 %collective-permute-start.2 = (bf16[128,128]{1,0:T(8,128)(2,1)S(1)}, bf16[128,128]{1,0:T(8,128)(2,1)S(1)}, u32[]{:S(2)}, u32[]{:S(2)}) collective-permute-start(bf16[128,128]{1,0:T(8,128)(2,1)S(1)} %get-tuple-element.18), channel_id=1, source_target_pairs={{0,13},{1,12},{2,15},{3,14},{4,9},{5,8},{6,11},{7,10},{8,5},{9,4},... | collective-permute-start | bytes 98312 | tf_op jit(solution)/shard_map/ppermute | solution.py:339
  10.8 0.2 collective-permute-start
  11.0 2.5 %collective-permute-start.5 = (bf16[112,128]{1,0:T(8,128)(2,1)S(1)}, bf16[112,128]{1,0:T(8,128)(2,1)S(1)}, u32[]{:S(2)}, u32[]{:S(2)}) collective-permute-start(bf16[112,128]{1,0:T(8,128)(2,1)S(1)} %slice.14), channel_id=1, source_target_pairs={{0,6},{1,7},{2,4},{3,5},{4,2},{5,3},{6,0},{7,1},{8,14},{9,15},{10,... | collective-permute-start | bytes 86024 | tf_op jit(solution)/shard_map/ppermute | solution.py:339
  13.5 0.2 collective-permute-start.4
  13.7 0.0 collective-permute-done.1
  13.7 0.7 %collective-permute-done.2 = bf16[128,128]{1,0:T(8,128)(2,1)S(1)} collective-permute-done((bf16[128,128]{1,0:T(8,128)(2,1)S(1)}, bf16[128,128]{1,0:T(8,128)(2,1)S(1)}, u32[]{:S(2)}, u32[]{:S(2)}) %collective-permute-start.2) | collective-permute-done | bytes 32800 | tf_op jit(solution)/shard_map/ppermute | solution.py:339
  14.4 1.9 %collective-permute-start.6 = (bf16[2,112,128]{2,1,0:T(8,128)(2,1)S(1)}, bf16[2,112,128]{2,1,0:T(8,128)(2,1)S(1)}, u32[]{:S(2)}, u32[]{:S(2)}) collective-permute-start(bf16[2,112,128]{2,1,0:T(8,128)(2,1)S(1)} %pad_maximum_fusion.2), channel_id=1, source_target_pairs={{0,3},{1,2},{2,1},{3,0},{4,7},{5,6},{6,5},{7,4},{8,11},{9,10},{10,... | collective-permute-start | bytes 172040 | tf_op jit(solution)/shard_map/ppermute | solution.py:339
  16.3 0.0 collective-permute-done
  16.4 0.4 %prepare.3.refs_4_ = bf16[32,4096]{1,0:T(8,128)(2,1)S(1)} custom-call(bf16[4,128,128]{2,1,0:T(8,128)(2,1)S(1)} %pad_maximum_fusion.after_ref.refs_0_), custom_call_target="tpu_custom_call" | custom-call | tf_op jit(solution)/shard_map/prepare/pallas_call | solution.py:257
  16.8 0.1 collective-permute-start.3
  16.9 2.4 %split.1 = (bf16[256,4096]{1,0:T(8,128)(2,1)S(1)}, bf16[256,4096]{1,0:T(8,128)(2,1)S(1)}) custom-call(f32[256,4096]{1,0:T(8,128)} %hess_ref.1, bf16[4,128,128]{2,1,0:T(8,128)(2,1)S(1)} %pad_maximum_fusion.after_ref.refs_0_), custom_call_target="tpu_custom_call" | custom-call | tf_op jit(solution)/shard_map/split/pallas_call | solution.py:230
  19.3 0.0 collective-permute-done.5
  19.3 0.0 collective-permute-done.4
  19.3 0.0 collective-permute-done.6
  19.3 0.6 %collective-permute-start.7 = (bf16[4,112,128]{2,1,0:T(8,128)(2,1)S(1)}, bf16[4,112,128]{2,1,0:T(8,128)(2,1)S(1)}, u32[]{:S(2)}, u32[]{:S(2)}) collective-permute-start(bf16[4,112,128]{2,1,0:T(8,128)(2,1)S(1)} %pad_maximum_fusion.1.refs_1_.refs_2_), channel_id=1, source_target_pairs={{0,1},{1,0},{2,3},{3,2},{4,5},{5,4},{6,7},{7,6},{8,9},{9,8},{10,11... | collective-permute-start | bytes 344072 | tf_op jit(solution)/shard_map/ppermute | solution.py:339
  19.9 0.0 collective-permute-done.3.refs_0_.refs_1_
  19.9 0.6 %prepare.4.refs_5_ = bf16[48,4096]{1,0:T(8,128)(2,1)S(1)} custom-call(bf16[4,112,128]{2,1,0:T(8,128)(2,1)S(1)} %collective-permute-done.3.refs_0_.refs_1_, bf16[4,112,128]{2,1,0:T(8,128)(2,1)S(1)} %pad_maximum_fusion.1.refs_1_.refs_2_), custom_call_target="tpu_custom_call" | custom-call | tf_op jit(solution)/shard_map/prepare/pallas_call | solution.py:257
  20.5 0.3 collective-permute-done.7.refs_0_.refs_3_
  20.8 0.4 %prepare.5.refs_6_ = bf16[32,4096]{1,0:T(8,128)(2,1)S(1)} custom-call(bf16[4,112,128]{2,1,0:T(8,128)(2,1)S(1)} %collective-permute-done.7.refs_0_.refs_3_), custom_call_target="tpu_custom_call" | custom-call | tf_op jit(solution)/shard_map/prepare/pallas_call | solution.py:257
  21.3 1.6 %score.1 = f32[128,128]{1,0:T(8,128)S(1)} custom-call(s32[1]{0:T(128)} %bitcast.me_ref, bf16[4,128,128]{2,1,0:T(8,128)(2,1)S(1)} %pad_maximum_fusion.after_ref.refs_0_, bf16[4,112,128]{2,1,0:T(8,128)(2,1)S(1)} %collective-permute-done.3.refs_0_.refs_1_, bf16[4,112,128]{2,1,0:T(8,128)(2,1)S(1)} %pad_maximum_fusion.1.refs_1_.refs_2_, ...), custom_call_target="tpu_custom_call" | custom-call | tf_op jit(solution)/shard_map/score/pallas_call | solution.py:320
  22.9 10.1 %all_to_all.5.parts_ref = f32[16,8,128]{2,1,0:T(8,128)S(1)} all-to-all(f32[16,8,128]{2,1,0:T(8,128)S(1)} %bitcast.12), channel_id=1, replica_groups=mesh['groups'=2,'dp'=16] {'dp'}, dimensions={0} | all-to-all | bytes 131072 | tf_op jit(solution)/shard_map/all_to_all | solution.py:379
  32.9 0.6 %finish.1 = f32[4,96]{1,0:T(4,128)} custom-call(f32[16,8,128]{2,1,0:T(8,128)S(1)} %all_to_all.5.parts_ref), custom_call_target="tpu_custom_call" | custom-call | tf_op jit(solution)/shard_map/finish/pallas_call | solution.py:380
  (6 shorter events, 0.1 us)
Async XLA Ops:
  5.6 8.1 %collective-permute-start.1 = (bf16[128,128]{1,0:T(8,128)(2,1)S(1)}, bf16[128,128]{1,0:T(8,128)(2,1)S(1)}, u32[]{:S(2)}, u32[]{:S(2)}) collective-permute-start(bf16[128,128]{1,0:T(8,128)(2,1)S(1)} %get-tuple-element.17), channel_id=1, source_target_pairs={{0,9},{1,8},{2,11},{3,10},{4,13},{5,12},{6,15},{7,14},{8,1},{9,0},... | collective-permute-start | bytes 98312 | tf_op jit(solution)/shard_map/ppermute | solution.py:339
  9.1 5.2 %collective-permute-start.2 = (bf16[128,128]{1,0:T(8,128)(2,1)S(1)}, bf16[128,128]{1,0:T(8,128)(2,1)S(1)}, u32[]{:S(2)}, u32[]{:S(2)}) collective-permute-start(bf16[128,128]{1,0:T(8,128)(2,1)S(1)} %get-tuple-element.18), channel_id=1, source_target_pairs={{0,13},{1,12},{2,15},{3,14},{4,9},{5,8},{6,11},{7,10},{8,5},{9,4},... | collective-permute-start | bytes 98312 | tf_op jit(solution)/shard_map/ppermute | solution.py:339
  10.8 5.6 %collective-permute-start = (bf16[128,128]{1,0:T(8,128)(2,1)S(1)}, bf16[128,128]{1,0:T(8,128)(2,1)S(1)}, u32[]{:S(2)}, u32[]{:S(2)}) collective-permute-start(bf16[128,128]{1,0:T(8,128)(2,1)S(1)} %get-tuple-element.16), channel_id=1, source_target_pairs={{0,5},{1,4},{2,7},{3,6},{4,1},{5,0},{6,3},{7,2},{8,13},{9,12},{10,... | collective-permute-start | bytes 98312 | tf_op jit(solution)/shard_map/ppermute | solution.py:339
  11.0 8.3 %collective-permute-start.5 = (bf16[112,128]{1,0:T(8,128)(2,1)S(1)}, bf16[112,128]{1,0:T(8,128)(2,1)S(1)}, u32[]{:S(2)}, u32[]{:S(2)}) collective-permute-start(bf16[112,128]{1,0:T(8,128)(2,1)S(1)} %slice.14), channel_id=1, source_target_pairs={{0,6},{1,7},{2,4},{3,5},{4,2},{5,3},{6,0},{7,1},{8,14},{9,15},{10,... | collective-permute-start | bytes 86024 | tf_op jit(solution)/shard_map/ppermute | solution.py:339
  13.5 5.8 %collective-permute-start.4 = (bf16[112,128]{1,0:T(8,128)(2,1)S(1)}, bf16[112,128]{1,0:T(8,128)(2,1)S(1)}, u32[]{:S(2)}, u32[]{:S(2)}) collective-permute-start(bf16[112,128]{1,0:T(8,128)(2,1)S(1)} %slice.13), channel_id=1, source_target_pairs={{0,3},{1,2},{2,1},{3,0},{4,7},{5,6},{6,5},{7,4},{8,11},{9,10},{10,... | collective-permute-start | bytes 86024 | tf_op jit(solution)/shard_map/ppermute | solution.py:339
  14.4 4.9 %collective-permute-start.6 = (bf16[2,112,128]{2,1,0:T(8,128)(2,1)S(1)}, bf16[2,112,128]{2,1,0:T(8,128)(2,1)S(1)}, u32[]{:S(2)}, u32[]{:S(2)}) collective-permute-start(bf16[2,112,128]{2,1,0:T(8,128)(2,1)S(1)} %pad_maximum_fusion.2), channel_id=1, source_target_pairs={{0,3},{1,2},{2,1},{3,0},{4,7},{5,6},{6,5},{7,4},{8,11},{9,10},{10,... | collective-permute-start | bytes 172040 | tf_op jit(solution)/shard_map/ppermute | solution.py:339
  16.8 3.1 %collective-permute-start.3 = (bf16[4,112,128]{2,1,0:T(8,128)(2,1)S(1)}, bf16[4,112,128]{2,1,0:T(8,128)(2,1)S(1)}, u32[]{:S(2)}, u32[]{:S(2)}) collective-permute-start(bf16[4,112,128]{2,1,0:T(8,128)(2,1)S(1)} %slice.16), channel_id=1, source_target_pairs={{0,1},{1,0},{2,3},{3,2},{4,5},{5,4},{6,7},{7,6},{8,9},{9,8},{10,11... | collective-permute-start | bytes 344072 | tf_op jit(solution)/shard_map/ppermute | solution.py:339
  19.3 1.5 %collective-permute-start.7 = (bf16[4,112,128]{2,1,0:T(8,128)(2,1)S(1)}, bf16[4,112,128]{2,1,0:T(8,128)(2,1)S(1)}, u32[]{:S(2)}, u32[]{:S(2)}) collective-permute-start(bf16[4,112,128]{2,1,0:T(8,128)(2,1)S(1)} %pad_maximum_fusion.1.refs_1_.refs_2_), channel_id=1, source_target_pairs={{0,1},{1,0},{2,3},{3,2},{4,5},{5,4},{6,7},{7,6},{8,9},{9,8},{10,11... | collective-permute-start | bytes 344072 | tf_op jit(solution)/shard_map/ppermute | solution.py:339

commit v9 on v8

--- a/solution.py
+++ b/solution.py
@@ -99,8 +99,8 @@
     q_in = jnp.zeros((queries, rank), F32)
     for c, cols in enumerate(parts):
         arrived()
-        middle = (cols.start + cols.stop) // 2
-        for some in (slice(cols.start, middle), slice(middle, cols.stop)):
+        step = (cols.stop - cols.start) // 4
+        for some in [slice(cols.start + i * step, cols.start + (i + 1) * step) for i in range(4)]:
             t_in += dot_nt(th[:, some], pi[:, some])
             q_in += dot_nt(qh[:, some], pi[:, some])
         if c == 0:
@@ -349,7 +349,7 @@
         me, planes, train_hidden, train_cot, query_hidden, query_cot, proj_in, proj_out
     )
     coords = hess_inv.shape[1]
-    others = [(INNER * k) ^ 1 for k in range(1, planes)]
+    others = [(INNER * k) ^ 1 for k in [1] + list(range(planes - 1, 1, -1))]
     far = [swap(messages[slot // INNER], slot, n) for slot in others]
     edge = (messages[0].shape[0] - tokens) // 2
     by_plane = [messages[0]] + far

time: 33.7 us -> 33.5 us (level)
  starting transfers between devices: 10.7 us -> 9.98 us
  waiting for transfers between devices: 1.01 us -> 1.58 us
    ppermute x8, starting transfers between devices: 10.7 us -> 9.98 us  [swap(): return lax.ppermute(x, 'dp', [(i, i ^ k) for i in range(n)])]
    ppermute x8, waiting for transfers between devices: 1.01 us -> 1.58 us  [swap(): return lax.ppermute(x, 'dp', [(i, i ^ k) for i in range(n)])]
where the time goes in v9:
time: 33.5 us; the launch traced here: 33.4 us
  Pallas kernels  11.7 us (35%)
  starting transfers between devices  9.98 us (30%)
  blocking collectives  9.98 us (30%)
  waiting for transfers between devices  1.58 us (5%)
    all_to_all x1, blocking collectives, fast(): parts = lax.all_to_all(parts, 'dp', 0, 0, tiled=True)  9.98 us
    ppermute x8, starting transfers between devices, swap(): return lax.ppermute(x, 'dp', [(i, i ^ k) for i in range(n)])  9.98 us
    pallas_call x1, Pallas kernels, project(): pl.pallas_call(functools.partial(project_kernel, planes, number, length,...  5.58 us
    pallas_call x1, Pallas kernels, split(): pl.pallas_call(functools.partial(split_kernel, chunks), out_shape=[pltpu....  2.35 us
    pallas_call x1, Pallas kernels, score(): pl.pallas_call(functools.partial(score_kernel, number, each, slots, share...  1.6 us
    ppermute x8, waiting for transfers between devices, swap(): return lax.ppermute(x, 'dp', [(i, i ^ k) for i in range(n)])  1.58 us
    pallas_call x3, Pallas kernels, prepare(): pl.pallas_call(functools.partial(prepare_kernel, tokens, qlen, starts), o...  1.52 us
  transfers between devices with their start and end apart: 8, of which 2 were waited for; matrix products, arithmetic and copies ran while one was open for 0% of the time, Pallas kernels for 10%

profile of v9, /device:TPU:0, one launch (start us, length us, event | category | flops | bytes accessed | tf_op | source)
XLA Modules:
  0.0 33.4 jit_solution(709900510200857131)
XLA Ops:
  0.0 5.6 %project.1 = (bf16[128,128]{1,0:T(8,128)(2,1)S(1)}, bf16[128,128]{1,0:T(8,128)(2,1)S(1)}, bf16[128,128]{1,0:T(8,128)(2,1)S(1)}, bf16[128,128]{1,0:T(8,128)(2,1)S(1)}) custom-call(s32[1]{0:T(128)} %bitcast.me_ref, bf16[160,14336]{1,0:T(8,128)(2,1)} %bitcast.14, bf16[160,4096]{1,0:T(8,128)(2,1)} %bitcast.16, bf16[96,14336]{1,0:T(8,128)(2,1)} %bitcast.15, ...), custom_call_target="tpu_custom_call" | custom-call | tf_op jit(solution)/shard_map/project/pallas_call | solution.py:147
  5.6 4.6 %collective-permute-start.1 = (bf16[128,128]{1,0:T(8,128)(2,1)S(1)}, bf16[128,128]{1,0:T(8,128)(2,1)S(1)}, u32[]{:S(2)}, u32[]{:S(2)}) collective-permute-start(bf16[128,128]{1,0:T(8,128)(2,1)S(1)} %get-tuple-element.17), channel_id=1, source_target_pairs={{0,13},{1,12},{2,15},{3,14},{4,9},{5,8},{6,11},{7,10},{8,5},{9,4},... | collective-permute-start | bytes 98312 | tf_op jit(solution)/shard_map/ppermute | solution.py:339
  10.2 0.0 collective-permute-start.2
  10.2 0.9 %collective-permute-start = (bf16[128,128]{1,0:T(8,128)(2,1)S(1)}, bf16[128,128]{1,0:T(8,128)(2,1)S(1)}, u32[]{:S(2)}, u32[]{:S(2)}) collective-permute-start(bf16[128,128]{1,0:T(8,128)(2,1)S(1)} %get-tuple-element.16), channel_id=1, source_target_pairs={{0,5},{1,4},{2,7},{3,6},{4,1},{5,0},{6,3},{7,2},{8,13},{9,12},{10,... | collective-permute-start | bytes 98312 | tf_op jit(solution)/shard_map/ppermute | solution.py:339
  11.1 2.3 %collective-permute-start.5 = (bf16[112,128]{1,0:T(8,128)(2,1)S(1)}, bf16[112,128]{1,0:T(8,128)(2,1)S(1)}, u32[]{:S(2)}, u32[]{:S(2)}) collective-permute-start(bf16[112,128]{1,0:T(8,128)(2,1)S(1)} %slice.14), channel_id=1, source_target_pairs={{0,6},{1,7},{2,4},{3,5},{4,2},{5,3},{6,0},{7,1},{8,14},{9,15},{10,... | collective-permute-start | bytes 86024 | tf_op jit(solution)/shard_map/ppermute | solution.py:339
  13.4 0.0 collective-permute-start.4
  13.4 0.0 collective-permute-done.1
  13.4 1.3 %collective-permute-done.2 = bf16[128,128]{1,0:T(8,128)(2,1)S(1)} collective-permute-done((bf16[128,128]{1,0:T(8,128)(2,1)S(1)}, bf16[128,128]{1,0:T(8,128)(2,1)S(1)}, u32[]{:S(2)}, u32[]{:S(2)}) %collective-permute-start.2) | collective-permute-done | bytes 32800 | tf_op jit(solution)/shard_map/ppermute | solution.py:339
  14.7 1.5 %collective-permute-start.6 = (bf16[2,112,128]{2,1,0:T(8,128)(2,1)S(1)}, bf16[2,112,128]{2,1,0:T(8,128)(2,1)S(1)}, u32[]{:S(2)}, u32[]{:S(2)}) collective-permute-start(bf16[2,112,128]{2,1,0:T(8,128)(2,1)S(1)} %pad_maximum_fusion.2), channel_id=1, source_target_pairs={{0,3},{1,2},{2,1},{3,0},{4,7},{5,6},{6,5},{7,4},{8,11},{9,10},{10,... | collective-permute-start | bytes 172040 | tf_op jit(solution)/shard_map/ppermute | solution.py:339
  16.2 0.0 collective-permute-done
  16.2 0.4 %prepare.3.refs_4_ = bf16[32,4096]{1,0:T(8,128)(2,1)S(1)} custom-call(bf16[4,128,128]{2,1,0:T(8,128)(2,1)S(1)} %pad_maximum_fusion.after_ref.refs_0_), custom_call_target="tpu_custom_call" | custom-call | tf_op jit(solution)/shard_map/prepare/pallas_call | solution.py:257
  16.7 0.2 collective-permute-start.3
  16.9 2.4 %split.1 = (bf16[256,4096]{1,0:T(8,128)(2,1)S(1)}, bf16[256,4096]{1,0:T(8,128)(2,1)S(1)}) custom-call(f32[256,4096]{1,0:T(8,128)} %hess_ref.1, bf16[4,128,128]{2,1,0:T(8,128)(2,1)S(1)} %pad_maximum_fusion.after_ref.refs_0_), custom_call_target="tpu_custom_call" | custom-call | tf_op jit(solution)/shard_map/split/pallas_call | solution.py:230
  19.3 0.0 collective-permute-done.5
  19.3 0.0 collective-permute-done.4
  19.3 0.0 collective-permute-done.6
  19.3 0.4 %collective-permute-start.7 = (bf16[4,112,128]{2,1,0:T(8,128)(2,1)S(1)}, bf16[4,112,128]{2,1,0:T(8,128)(2,1)S(1)}, u32[]{:S(2)}, u32[]{:S(2)}) collective-permute-start(bf16[4,112,128]{2,1,0:T(8,128)(2,1)S(1)} %pad_maximum_fusion.1.refs_1_.refs_2_), channel_id=1, source_target_pairs={{0,1},{1,0},{2,3},{3,2},{4,5},{5,4},{6,7},{7,6},{8,9},{9,8},{10,11... | collective-permute-start | bytes 344072 | tf_op jit(solution)/shard_map/ppermute | solution.py:339
  19.7 0.0 collective-permute-done.3.refs_0_.refs_1_
  19.7 0.6 %prepare.4.refs_5_ = bf16[48,4096]{1,0:T(8,128)(2,1)S(1)} custom-call(bf16[4,112,128]{2,1,0:T(8,128)(2,1)S(1)} %collective-permute-done.3.refs_0_.refs_1_, bf16[4,112,128]{2,1,0:T(8,128)(2,1)S(1)} %pad_maximum_fusion.1.refs_1_.refs_2_), custom_call_target="tpu_custom_call" | custom-call | tf_op jit(solution)/shard_map/prepare/pallas_call | solution.py:257
  20.4 0.3 collective-permute-done.7.refs_0_.refs_3_
  20.7 0.4 %prepare.5.refs_6_ = bf16[32,4096]{1,0:T(8,128)(2,1)S(1)} custom-call(bf16[4,112,128]{2,1,0:T(8,128)(2,1)S(1)} %collective-permute-done.7.refs_0_.refs_3_), custom_call_target="tpu_custom_call" | custom-call | tf_op jit(solution)/shard_map/prepare/pallas_call | solution.py:257
  21.2 1.6 %score.1 = f32[128,128]{1,0:T(8,128)S(1)} custom-call(s32[1]{0:T(128)} %bitcast.me_ref, bf16[4,128,128]{2,1,0:T(8,128)(2,1)S(1)} %pad_maximum_fusion.after_ref.refs_0_, bf16[4,112,128]{2,1,0:T(8,128)(2,1)S(1)} %collective-permute-done.3.refs_0_.refs_1_, bf16[4,112,128]{2,1,0:T(8,128)(2,1)S(1)} %pad_maximum_fusion.1.refs_1_.refs_2_, ...), custom_call_target="tpu_custom_call" | custom-call | tf_op jit(solution)/shard_map/score/pallas_call | solution.py:320
  22.8 10.0 %all_to_all.5.parts_ref = f32[16,8,128]{2,1,0:T(8,128)S(1)} all-to-all(f32[16,8,128]{2,1,0:T(8,128)S(1)} %bitcast.12), channel_id=1, replica_groups=mesh['groups'=2,'dp'=16] {'dp'}, dimensions={0} | all-to-all | bytes 131072 | tf_op jit(solution)/shard_map/all_to_all | solution.py:379
  32.7 0.6 %finish.1 = f32[4,96]{1,0:T(4,128)} custom-call(f32[16,8,128]{2,1,0:T(8,128)S(1)} %all_to_all.5.parts_ref), custom_call_target="tpu_custom_call" | custom-call | tf_op jit(solution)/shard_map/finish/pallas_call | solution.py:380
  (6 shorter events, 0.1 us)
Async XLA Ops:
  5.6 7.8 %collective-permute-start.1 = (bf16[128,128]{1,0:T(8,128)(2,1)S(1)}, bf16[128,128]{1,0:T(8,128)(2,1)S(1)}, u32[]{:S(2)}, u32[]{:S(2)}) collective-permute-start(bf16[128,128]{1,0:T(8,128)(2,1)S(1)} %get-tuple-element.17), channel_id=1, source_target_pairs={{0,13},{1,12},{2,15},{3,14},{4,9},{5,8},{6,11},{7,10},{8,5},{9,4},... | collective-permute-start | bytes 98312 | tf_op jit(solution)/shard_map/ppermute | solution.py:339
  10.2 4.5 %collective-permute-start.2 = (bf16[128,128]{1,0:T(8,128)(2,1)S(1)}, bf16[128,128]{1,0:T(8,128)(2,1)S(1)}, u32[]{:S(2)}, u32[]{:S(2)}) collective-permute-start(bf16[128,128]{1,0:T(8,128)(2,1)S(1)} %get-tuple-element.18), channel_id=1, source_target_pairs={{0,9},{1,8},{2,11},{3,10},{4,13},{5,12},{6,15},{7,14},{8,1},{9,0},... | collective-permute-start | bytes 98312 | tf_op jit(solution)/shard_map/ppermute | solution.py:339
  10.2 6.0 %collective-permute-start = (bf16[128,128]{1,0:T(8,128)(2,1)S(1)}, bf16[128,128]{1,0:T(8,128)(2,1)S(1)}, u32[]{:S(2)}, u32[]{:S(2)}) collective-permute-start(bf16[128,128]{1,0:T(8,128)(2,1)S(1)} %get-tuple-element.16), channel_id=1, source_target_pairs={{0,5},{1,4},{2,7},{3,6},{4,1},{5,0},{6,3},{7,2},{8,13},{9,12},{10,... | collective-permute-start | bytes 98312 | tf_op jit(solution)/shard_map/ppermute | solution.py:339
  11.1 8.2 %collective-permute-start.5 = (bf16[112,128]{1,0:T(8,128)(2,1)S(1)}, bf16[112,128]{1,0:T(8,128)(2,1)S(1)}, u32[]{:S(2)}, u32[]{:S(2)}) collective-permute-start(bf16[112,128]{1,0:T(8,128)(2,1)S(1)} %slice.14), channel_id=1, source_target_pairs={{0,6},{1,7},{2,4},{3,5},{4,2},{5,3},{6,0},{7,1},{8,14},{9,15},{10,... | collective-permute-start | bytes 86024 | tf_op jit(solution)/shard_map/ppermute | solution.py:339
  13.4 5.8 %collective-permute-start.4 = (bf16[112,128]{1,0:T(8,128)(2,1)S(1)}, bf16[112,128]{1,0:T(8,128)(2,1)S(1)}, u32[]{:S(2)}, u32[]{:S(2)}) collective-permute-start(bf16[112,128]{1,0:T(8,128)(2,1)S(1)} %slice.13), channel_id=1, source_target_pairs={{0,3},{1,2},{2,1},{3,0},{4,7},{5,6},{6,5},{7,4},{8,11},{9,10},{10,... | collective-permute-start | bytes 86024 | tf_op jit(solution)/shard_map/ppermute | solution.py:339
  14.7 4.6 %collective-permute-start.6 = (bf16[2,112,128]{2,1,0:T(8,128)(2,1)S(1)}, bf16[2,112,128]{2,1,0:T(8,128)(2,1)S(1)}, u32[]{:S(2)}, u32[]{:S(2)}) collective-permute-start(bf16[2,112,128]{2,1,0:T(8,128)(2,1)S(1)} %pad_maximum_fusion.2), channel_id=1, source_target_pairs={{0,3},{1,2},{2,1},{3,0},{4,7},{5,6},{6,5},{7,4},{8,11},{9,10},{10,... | collective-permute-start | bytes 172040 | tf_op jit(solution)/shard_map/ppermute | solution.py:339
  16.7 3.1 %collective-permute-start.3 = (bf16[4,112,128]{2,1,0:T(8,128)(2,1)S(1)}, bf16[4,112,128]{2,1,0:T(8,128)(2,1)S(1)}, u32[]{:S(2)}, u32[]{:S(2)}) collective-permute-start(bf16[4,112,128]{2,1,0:T(8,128)(2,1)S(1)} %slice.16), channel_id=1, source_target_pairs={{0,1},{1,0},{2,3},{3,2},{4,5},{5,4},{6,7},{7,6},{8,9},{9,8},{10,11... | collective-permute-start | bytes 344072 | tf_op jit(solution)/shard_map/ppermute | solution.py:339
  19.3 1.4 %collective-permute-start.7 = (bf16[4,112,128]{2,1,0:T(8,128)(2,1)S(1)}, bf16[4,112,128]{2,1,0:T(8,128)(2,1)S(1)}, u32[]{:S(2)}, u32[]{:S(2)}) collective-permute-start(bf16[4,112,128]{2,1,0:T(8,128)(2,1)S(1)} %pad_maximum_fusion.1.refs_1_.refs_2_), channel_id=1, source_target_pairs={{0,1},{1,0},{2,3},{3,2},{4,5},{5,4},{6,7},{7,6},{8,9},{9,8},{10,11... | collective-permute-start | bytes 344072 | tf_op jit(solution)/shard_map/ppermute | solution.py:339
